TPU v7x, 128 devices: a whole 4x4x4 slice. The times are simulated.
128 devices in a mesh: wide: 16 (over x, y), grp: 8 (over z, core).
Axes of the slice: x: 4, y: 4, z: 4, core: 2. Of those that a mesh axis runs over, the one named last changes fastest.
Arguments:
- velocity: float32 [3, 768, 128, 512], P(None, 'wide', 'grp'), may hold values from -5 to 5
- scalar: float32 [768, 128, 512], P('wide', 'grp'), may hold values from -5 to 5
- marker_owner: int32 [131072], P(('wide', 'grp')), may hold values from 0 to 127, as said below
- marker_tile: int32 [131072], P(('wide', 'grp')), may hold values from 0 to 3071
- marker_offset: int32 [131072], P(('wide', 'grp')), may hold values from 0 to 127
- marker_target: float32 [4, 131072], P(None, ('wide', 'grp')), may hold values from -4 to 4
- marker_eta: float32 [131072], P(('wide', 'grp')), may hold values from 0.1 to 1
Outputs:
- velocity_out: float32 [3, 768, 128, 512], P(None, 'wide', 'grp')
- scalar_out: float32 [768, 128, 512], P('wide', 'grp')
- marker_force: float32 [4, 131072], P(None, ('wide', 'grp'))
Inputs may be any that keep to these rules, and one draw needn't show every extreme that they name: `marker_owner`: in each device's aligned block of 1024 markers no owner is named more than 32 times; one owner, the same for all blocks, is named exactly 32 times in every block, and in every block 8 further owners, which may differ from block to block, are named exactly 32 times each.
All inputs are finite; a program needn't handle non-finite values.
Results may differ from a plain program's by a relative error of at most 0.0003.
Values sent between devices are 32-bit elements; how exact they have to be, the bound alone decides.
No kernel may reach another device: no remote copies, remote signals or barrier semaphores. Data moves between devices by JAX's collectives and lax.ppermute only.
A program may use at most 192 MiB of HBM per device.

v0:
```python
import math

import jax
import jax.numpy as jnp
from jax import lax
from jax.sharding import PartitionSpec as P

time_step = 0.1
viscosity = 0.4
diffusivity = 0.25
highest = lax.Precision.HIGHEST


def with_halo(cells, sides, width):
    for axis, dim in sides:
        count = lax.axis_size(axis)
        head = lax.slice_in_dim(cells, 0, width, axis=dim)
        tail = lax.slice_in_dim(cells, cells.shape[dim] - width, cells.shape[dim], axis=dim)
        cells = jnp.concatenate(
            [
                lax.ppermute(tail, axis, [(i, (i + 1) % count) for i in range(count)]),
                cells,
                lax.ppermute(head, axis, [((i + 1) % count, i) for i in range(count)]),
            ],
            axis=dim,
        )
    return cells


def passed_along(value, axis, steps):
    count = lax.axis_size(axis)
    pairs = [(source, (source + steps) % count) for source in range(count)]
    return lax.ppermute(value, axis, pairs)


def update(center, east, west, north, south, upper, lower):
    coeffs = jnp.array([viscosity, viscosity, viscosity, diffusivity], dtype=jnp.float32)[
        :, None, None, None
    ]
    transport = (
        center[0] * ((east - west) * 0.5)
        + center[1] * ((north - south) * 0.5)
        + center[2] * ((upper - lower) * 0.5)
    )
    laplace = east + west + north + south + upper + lower - 6.0 * center
    return center + time_step * (coeffs * laplace - transport)


def wave_terms(index, length):
    theta = 2.0 * math.pi / length * index.astype(jnp.float32)
    half_sin = jnp.sin(0.5 * theta)
    return (-2.0 * half_sin * half_sin, jnp.sin(theta), 4.0 * half_sin * half_sin)


def cos_sin(first, second, length):
    product = first * second % length
    theta = 2.0 * math.pi / length * product.astype(jnp.float32)
    return (jnp.cos(theta), jnp.sin(theta))


def complex_product(form, real_part, imag_part, cosine, sine, sign):
    real_cos = jnp.einsum(form, real_part, cosine, precision=highest)
    real_sin = jnp.einsum(form, real_part, sine, precision=highest)
    imag_cos = jnp.einsum(form, imag_part, cosine, precision=highest)
    imag_sin = jnp.einsum(form, imag_part, sine, precision=highest)
    return (real_cos - sign * imag_sin, imag_cos + sign * real_sin)


def make_tables(length_x, full_y, depth_z, n_grp):
    modes = length_x // 2
    along_x = jnp.arange(length_x, dtype=jnp.int32)
    mode_x = jnp.arange(modes, dtype=jnp.int32)
    x_cos, x_sin = cos_sin(along_x[:, None], mode_x[None, :], length_x)
    alternate = (1 - 2 * (along_x % 2)).astype(jnp.float32)
    first_mode = (mode_x == 0)[None, :]
    x_sin = jnp.where(first_mode, -alternate[:, None], x_sin)
    weight = jnp.where(mode_x == 0, 1.0, 2.0).astype(jnp.float32)[None, :]
    back_cos = (x_cos * weight).T
    back_sin = (x_sin * weight).T
    along_y = jnp.arange(full_y, dtype=jnp.int32)
    y_cos, y_sin = cos_sin(along_y[:, None], along_y[None, :], full_y)
    full_z = depth_z * n_grp
    z_place = (
        jnp.arange(n_grp, dtype=jnp.int32)[:, None] * depth_z
        + jnp.arange(depth_z, dtype=jnp.int32)[None, :]
    )[:, :, None]
    z_cos, z_sin = cos_sin(z_place, jnp.arange(full_z, dtype=jnp.int32)[None, None, :], full_z)
    return (x_cos, x_sin, back_cos, back_sin, y_cos, y_sin, z_cos, z_sin)


def to_spectrum(real_fields, tables):
    x_cos, x_sin, back_cos, back_sin, y_cos, y_sin, z_cos, z_sin = tables
    count, rows_y, depth_z, length_x = real_fields.shape
    modes = x_cos.shape[1]
    n_wide = lax.axis_size("wide")
    n_grp = lax.axis_size("grp")
    real_part = jnp.einsum("cyzx,xk->cykz", real_fields, x_cos, precision=highest).reshape(
        count, rows_y, modes * depth_z
    )
    imag_part = -jnp.einsum("cyzx,xk->cykz", real_fields, x_sin, precision=highest).reshape(
        count, rows_y, modes * depth_z
    )
    moved = (
        lax.all_to_all(
            lax.all_to_all(real_part, "wide", split_axis=2, concat_axis=1, tiled=True),
            "grp",
            split_axis=2,
            concat_axis=2,
            tiled=True,
        ),
        lax.all_to_all(
            lax.all_to_all(imag_part, "wide", split_axis=2, concat_axis=1, tiled=True),
            "grp",
            split_axis=2,
            concat_axis=2,
            tiled=True,
        ),
    )
    local_kx = modes // (n_wide * n_grp)
    slab_shape = (count, rows_y * n_wide, n_grp, local_kx, depth_z)
    real_part, imag_part = complex_product(
        "cyguz,yv->cvguz",
        moved[0].reshape(slab_shape),
        moved[1].reshape(slab_shape),
        y_cos,
        y_sin,
        -1.0,
    )
    return complex_product("cvguz,gzw->cvuw", real_part, imag_part, z_cos, z_sin, -1.0)


def from_spectrum(real_part, imag_part, tables, length_x, depth_z):
    x_cos, x_sin, back_cos, back_sin, y_cos, y_sin, z_cos, z_sin = tables
    count, full_y, local_kx, full_z = real_part.shape
    modes = back_cos.shape[0]
    n_wide = lax.axis_size("wide")
    n_grp = lax.axis_size("grp")
    full_z = depth_z * n_grp
    real_part, imag_part = complex_product(
        "cvuw,gzw->cvguz", real_part, imag_part, z_cos, z_sin, 1.0
    )
    real_part, imag_part = complex_product(
        "cvguz,yv->cyguz", real_part, imag_part, y_cos, y_sin, 1.0
    )
    flat_shape = (count, full_y, 1, n_grp * local_kx * depth_z)
    moved = (
        lax.all_to_all(
            lax.all_to_all(
                real_part.reshape(flat_shape), "wide", split_axis=1, concat_axis=2, tiled=True
            ),
            "grp",
            split_axis=3,
            concat_axis=3,
            tiled=True,
        ),
        lax.all_to_all(
            lax.all_to_all(
                imag_part.reshape(flat_shape), "wide", split_axis=1, concat_axis=2, tiled=True
            ),
            "grp",
            split_axis=3,
            concat_axis=3,
            tiled=True,
        ),
    )
    rows_y = full_y // n_wide
    pencil_shape = (count, rows_y, modes, depth_z)
    real_x = jnp.einsum(
        "cykz,kx->cyzx", moved[0].reshape(pencil_shape), back_cos, precision=highest
    )
    imag_x = jnp.einsum(
        "cykz,kx->cyzx", moved[1].reshape(pencil_shape), back_sin, precision=highest
    )
    return (real_x - imag_x) * (1.0 / (length_x * full_y * full_z))


def spectral_terms(kx_index, full_y, full_z, length_x):
    x_real, x_imag, x_square = wave_terms(kx_index, length_x)
    y_real, y_imag, y_square = wave_terms(jnp.arange(full_y, dtype=jnp.int32), full_y)
    z_real, z_imag, z_square = wave_terms(jnp.arange(full_z, dtype=jnp.int32), full_z)
    factor_terms = (
        (x_real[None, :, None], x_imag[None, :, None]),
        (y_real[:, None, None], y_imag[:, None, None]),
        (z_real[None, None, :], z_imag[None, None, :]),
    )
    total_square = x_square[None, :, None] + y_square[:, None, None] + z_square[None, None, :]
    inverse_square = jnp.where(
        total_square > 0, 1.0 / jnp.where(total_square > 0, total_square, 1.0), 0.0
    )
    return (factor_terms, inverse_square)


def project_pressure(spec_real, spec_imag, factor_terms, inverse_square):
    return (-spec_real * inverse_square, -spec_imag * inverse_square)


def mirror(values):
    values = jnp.roll(jnp.flip(values, 1), 1, 1)
    return jnp.roll(jnp.flip(values, 3), 1, 3)


def project_band(spec_real, spec_imag, project, local_kx, full_y, full_z, length_x):
    n_grp = lax.axis_size("grp")
    first_kx = lax.axis_index("wide") * (n_grp * local_kx) + lax.axis_index("grp") * local_kx
    kx_index = first_kx + jnp.arange(local_kx, dtype=jnp.int32)
    factor_terms, inverse_square = spectral_terms(kx_index, full_y, full_z, length_x)
    new_real, new_imag = project(spec_real, spec_imag, factor_terms, inverse_square)
    col_real = spec_real[:, :, 0:1]
    col_imag = spec_imag[:, :, 0:1]
    flip_real = mirror(col_real)
    flip_imag = mirror(col_imag)
    mean_real = (col_real + flip_real) * 0.5
    mean_imag = (col_imag - flip_imag) * 0.5
    top_real = (col_imag + flip_imag) * 0.5
    top_imag = (flip_real - col_real) * 0.5
    zero_terms, zero_inverse = spectral_terms(jnp.zeros((1,), jnp.int32), full_y, full_z, length_x)
    top_terms, top_inverse = spectral_terms(
        jnp.full((1,), length_x // 2, jnp.int32), full_y, full_z, length_x
    )
    mean_real, mean_imag = project(mean_real, mean_imag, zero_terms, zero_inverse)
    top_real, top_imag = project(top_real, top_imag, top_terms, top_inverse)
    packed_real = mean_real - top_imag
    packed_imag = mean_imag + top_real
    is_first = first_kx == 0
    head_real = jnp.where(is_first, packed_real, new_real[:, :, 0:1])
    head_imag = jnp.where(is_first, packed_imag, new_imag[:, :, 0:1])
    return (
        jnp.concatenate([head_real, new_real[:, :, 1:]], axis=2),
        jnp.concatenate([head_imag, new_imag[:, :, 1:]], axis=2),
    )


def per_device(
    velocity, scalar, marker_owner, marker_tile, marker_offset, marker_target, marker_eta
):
    rows_y = velocity.shape[1]
    depth_z = velocity.shape[2]
    length_x = velocity.shape[3]
    n_wide = lax.axis_size("wide")
    n_grp = lax.axis_size("grp")
    owners = n_wide * n_grp
    full_y = rows_y * n_wide
    full_z = depth_z * n_grp
    local_kx = length_x // 2 // owners
    fields = jnp.concatenate([velocity, scalar[None]], axis=0)
    padded = with_halo(fields, (("wide", 1), ("grp", 2)), 1)
    star = update(
        fields,
        jnp.roll(fields, -1, 3),
        jnp.roll(fields, 1, 3),
        padded[:, 2:, 1:-1],
        padded[:, :-2, 1:-1],
        padded[:, 1:-1, 2:],
        padded[:, 1:-1, :-2],
    )
    held = marker_owner.shape[0]
    capacity = held // 32
    buffer_len = owners * capacity
    onehot = (marker_owner[:, None] == jnp.arange(owners, dtype=jnp.int32)[None, :]).astype(
        jnp.int32
    )
    running = jnp.cumsum(onehot, axis=0)
    placing = jnp.sum(running * onehot, axis=1) - 1
    slot_index = marker_owner * capacity + placing
    local_cell = marker_tile * 128 + marker_offset
    payload = jnp.concatenate([marker_target, marker_eta[None, :]], axis=0)
    send_values = jnp.zeros((5, buffer_len), jnp.float32).at[:, slot_index].set(payload)
    send_cells = jnp.zeros((1, buffer_len), jnp.int32).at[:, slot_index].set(local_cell[None, :])
    recv_values, recv_cells = (
        lax.all_to_all(send_values, ("wide", "grp"), split_axis=1, concat_axis=1, tiled=True),
        lax.all_to_all(send_cells, ("wide", "grp"), split_axis=1, concat_axis=1, tiled=True),
    )
    star_flat = star.reshape(4, rows_y * depth_z * length_x)
    target_cells = recv_cells[0]
    sampled = jnp.take(star_flat, target_cells, axis=1)
    force_terms = recv_values[4:5] * (recv_values[:4] - sampled)
    forced = star_flat.at[:, target_cells].add(force_terms).reshape(star.shape)
    returned = lax.all_to_all(force_terms, ("wide", "grp"), split_axis=1, concat_axis=1, tiled=True)
    marker_force = jnp.take(returned, slot_index, axis=1)
    tables = make_tables(length_x, full_y, depth_z, n_grp)
    flow = forced[:3]
    next_row = passed_along(flow[1, :1], "wide", -1)
    after_y = jnp.concatenate([flow[1, 1:], next_row], axis=0)
    next_plane = passed_along(flow[2, :, :1], "grp", -1)
    after_z = jnp.concatenate([flow[2, :, 1:], next_plane], axis=1)
    divergence = jnp.roll(flow[0], -1, 2) - flow[0] + (after_y - flow[1]) + (after_z - flow[2])
    div_real, div_imag = to_spectrum(divergence[None], tables)
    press_real, press_imag = project_band(
        div_real, div_imag, project_pressure, local_kx, full_y, full_z, length_x
    )
    pressure = from_spectrum(press_real, press_imag, tables, length_x, depth_z)[0]
    prev_row = passed_along(pressure[-1:], "wide", 1)
    prev_plane = passed_along(pressure[:, -1:], "grp", 1)
    grad_x = pressure - jnp.roll(pressure, 1, 2)
    grad_y = pressure - jnp.concatenate([prev_row, pressure[:-1]], axis=0)
    grad_z = pressure - jnp.concatenate([prev_plane, pressure[:, :-1]], axis=1)
    velocity_out = flow - jnp.stack([grad_x, grad_y, grad_z])
    return (velocity_out, forced[3], marker_force)


def solution(mesh):
    return jax.shard_map(
        per_device,
        mesh=mesh,
        in_specs=(
            P(None, "wide", "grp", None),
            P("wide", "grp", None),
            P(("wide", "grp")),
            P(("wide", "grp")),
            P(("wide", "grp")),
            P(None, ("wide", "grp")),
            P(("wide", "grp")),
        ),
        out_specs=(P(None, "wide", "grp", None), P("wide", "grp", None), P(None, ("wide", "grp"))),
        check_vma=False,
    )
```

profile of v0, /device:TPU:1, one launch (start us, length us, event | category | flops | bytes accessed | tf_op | source)
XLA Modules:
  0.0 1168.7 jit_solution(9835051673824826002)
XLA Ops:
  1.7 5.8 collective-permute-start
  8.9 4.3 scatter_custom_fusion
  14.0 10.6 all-to-all-start
  24.6 8.6 fusion
  33.3 2.2 fusion.25
  35.5 2.3 multiply_bitcast_fusion.2
  39.2 4.5 scatter_custom_fusion.1
  43.7 2.4 copy.97
  47.0 10.1 all-to-all-start.1
  60.0 2.7 pad_maximum_fusion.18
  73.2 19.3 %multiply_add_fusion = f32[4,48,16,512]{3,2,1,0:T(8,128)S(1)} fusion(f32[1,48,16,512]{3,2,1,0:T(8,128)S(1)} %bitcast.231, f32[3,48,16,512]{3,2,1,0:T(8,128)} %param.8, f32[4,1,16,512]{3,2,1,0:T(8,128)S(1)} %collective-permute-done, f32[4,1,16,512]{3,2,1,0:T(8,128)S(1)} %collective-permute-done.1, f32[4,50,1,512]{3,2,1,0:T(1,128)S(1)} %copy.92, ...), kind=kLoop, calls=%fused_computation.34 | loop fusion | flops 53477376 | bytes 30965776 | tf_op jit(solution)/shard_map/add | solution.py:46
  92.6 6.7 copy.137
  99.3 138.9 %gather_fusion = f32[4096,4]{0,1:T(4,128)S(1)} fusion(f32[4,393216]{1,0:T(4,128)} %bitcast.218, s32[4096]{0:T(1024)S(1)} %copy-done.14), kind=kCustom, calls=%fused_computation | custom fusion | bytes 147456 | tf_op jit(solution)/shard_map/jit(_take)/gather | solution.py:275
  239.3 516.9 %scatter_fusion = f32[4,393216]{1,0:T(4,128)} fusion(f32[4,393216]{1,0:T(4,128)} %bitcast.219, s32[4096]{0:T(1024)S(1)} %bitcast.284, f32[4096,4]{0,1:T(4,128)S(1)} %multiply_bitcast_fusion.5), kind=kCustom, calls=%fused_computation.4 | custom fusion | flops 16384 | bytes 212992 | tf_op jit(solution)/shard_map/scatter-add | solution.py:277
  756.3 25.6 %slice_reduce_fusion = (f32[393216]{0:T(1024)}, f32[393216]{0:T(1024)S(1)}, f32[393216]{0:T(1024)}, f32[393216]{0:T(1024)}) fusion(f32[4,393216]{1,0:T(4,128)} %scatter_fusion), kind=kLoop, calls=%fused_computation.55 | loop fusion | bytes 12582912 | tf_op jit(solution)/shard_map/slice | solution.py:298
  786.7 9.9 collective-permute-start.5
  796.6 7.9 collective-permute-start.4
  809.2 2.6 squeeze.33
  813.9 4.6 fusion.28
  819.6 4.0 fusion.46
  825.0 19.3 %reduce.26 = f32[4096,48]{1,0:T(8,128)} reduce(f32[4096,1,48]{2,1,0:T(1,128)S(1)} %bitcast.241, f32[]{:T(128)} %broadcast.558), dimensions={1}, to_apply=%bitcast.199.reduce_sub_computation | reduce | bytes 1572868
  844.3 4.5 reshape.652
  848.8 4.1 all-to-all-start.4
  852.9 4.7 fusion.40
  857.6 2.4 copy.102
  860.1 19.3 %reduce.28 = f32[4096,48]{1,0:T(8,128)} reduce(f32[4096,1,48]{2,1,0:T(1,128)S(1)} %bitcast.242, f32[]{:T(128)} %broadcast.558), dimensions={1}, to_apply=%bitcast.197.reduce_sub_computation | reduce | bytes 1572868
  879.4 4.1 reshape.650
  884.3 6.8 all-to-all-start.2
  891.2 4.5 reduce.27
  895.7 5.7 reshape.653
  906.4 9.7 all-to-all-start.5
  916.8 3.5 reduce.29
  920.3 5.7 reshape.651
  929.1 4.8 all-to-all-start.3
  935.6 13.0 %fusion.22 = f32[768,256]{0,1:S(1)} fusion(f32[1,768,256]{1,0,2:T(1,128)} %all-to-all-done.5), kind=kOutput, calls=%fused_computation.51 | convolution fusion | flops 1817247744 | bytes 1572864
  948.7 10.8 all-to-all-start.10
  959.5 11.9 %fusion.14 = f32[768,256]{0,1:S(1)} fusion(f32[1,768,256]{1,0,2:T(1,128)S(1)} %all-to-all-done.3), kind=kOutput, calls=%fused_computation.47 | convolution fusion | flops 1817247744 | bytes 1572864
  973.0 13.0 %fusion.12 = f32[768,256]{0,1:S(1)} fusion(f32[1,768,256]{1,0,2:T(1,128)} %all-to-all-done.5), kind=kOutput, calls=%fused_computation.46 | convolution fusion | flops 1817247744 | bytes 1572864
  986.0 12.1 %fusion.20 = f32[768,256]{0,1:S(1)} fusion(f32[1,768,256]{1,0,2:T(1,128)S(1)} %all-to-all-done.3), kind=kOutput, calls=%fused_computation.50 | convolution fusion | flops 1817247744 | bytes 1572864
  1007.0 3.1 slice.251
  1014.9 11.8 %fusion.8 = f32[768,256]{0,1:S(1)} fusion(f32[768,256]{0,1:T(8,128)S(1)} %bitcast.273), kind=kOutput, calls=%fused_computation.44 | convolution fusion | flops 1817247744 | bytes 1572864
  1027.8 11.9 %fusion.16 = f32[768,256]{0,1:S(1)} fusion(f32[768,256]{0,1:T(8,128)S(1)} %bitcast.275), kind=kOutput, calls=%fused_computation.48 | convolution fusion | flops 1817247744 | bytes 1572864
  1041.6 7.2 all-to-all-start.8
  1048.7 11.9 %fusion.18 = f32[768,256]{0,1:S(1)} fusion(f32[768,256]{0,1:T(8,128)S(1)} %bitcast.274), kind=kOutput, calls=%fused_computation.49 | convolution fusion | flops 1817247744 | bytes 1572864
  1060.6 11.8 %fusion.10 = f32[768,256]{0,1:S(1)} fusion(f32[768,256]{0,1:T(8,128)S(1)} %bitcast.276), kind=kOutput, calls=%fused_computation.45 | convolution fusion | flops 1817247744 | bytes 1572864
  1074.3 6.8 all-to-all-start.6
  1082.0 2.4 copy.118
  1084.5 2.9 reshape.656
  1087.4 6.4 all-to-all-done.6
  1094.8 7.5 all-to-all-start.9
  1102.3 2.1 copy.131
  1104.3 2.4 copy.114
  1106.8 2.9 reshape.654
  1109.7 4.8 all-to-all-done.9
  1114.5 5.0 all-to-all-start.7
  1123.4 2.8 gather_fusion.1
  1127.3 3.6 reduce.31
  1134.9 3.6 copy.120
  1138.5 3.6 reduce.30
  1145.0 2.9 copy.116
  1147.8 3.6 fusion.92
  1151.4 3.5 subtract_multiply_fusion
  1157.4 5.5 collective-permute-done.6
  1165.1 3.3 maximum_subtract_fusion
  (208 shorter events, 83.4 us)
Async XLA Ops:
  0.6 6.9 copy-start.16
  1.6 7.3 copy-start.25
  1.6 7.3 copy-start.26
  1.6 23.0 %copy-start.1 = (f32[48,16,512]{2,1,0:T(8,128)S(1)}, f32[48,16,512]{2,1,0:T(8,128)}, u32[]{:S(2)}) copy-start(f32[48,16,512]{2,1,0:T(8,128)} %param.9) | copy-start | bytes 4718596
  1.7 58.3 %collective-permute-start = (f32[4,1,16,512]{3,2,1,0:T(8,128)S(1)}, f32[4,1,16,512]{3,2,1,0:T(8,128)S(1)}, u32[]{:S(2)}, u32[]{:S(2)}) collective-permute-start(f32[4,1,16,512]{3,2,1,0:T(8,128)S(1)} %get-tuple-element.28), channel_id=1, source_target_pairs={{8,0},{16,8},{24,16},{32,24},{40,32},{48,40},{56,48},{64,56},{72,6... | collective-permute-start | bytes 393224 | tf_op jit(solution)/shard_map/ppermute | solution.py:23
  7.5 52.5 %collective-permute-start.1 = (f32[4,1,16,512]{3,2,1,0:T(8,128)S(1)}, f32[4,1,16,512]{3,2,1,0:T(8,128)S(1)}, u32[]{:S(2)}, u32[]{:S(2)}) collective-permute-start(f32[4,1,16,512]{3,2,1,0:T(8,128)S(1)} %get-tuple-element.27), channel_id=1, source_target_pairs={{0,8},{8,16},{16,24},{24,32},{32,40},{40,48},{48,56},{56,64},{64,7... | collective-permute-start | bytes 393224 | tf_op jit(solution)/shard_map/ppermute | solution.py:21
  8.0 25.2 %slice-start = ((s8[4718592]{0:T(1024)(128)(4,1)}), s8[524288]{0:T(1024)(128)(4,1)S(1)}, s32[]{:S(2)}) async-start(s8[4718592]{0:T(1024)(128)(4,1)} %bitcast.221), calls=%async_computation.11 | async-start | bytes 1048576
  8.9 30.3 %copy-start.20 = (s32[1024]{0:T(1024)}, s32[1024]{0:T(1024)S(1)}, u32[]{:S(2)}) copy-start(s32[1024]{0:T(1024)S(1)} %get-tuple-element.20) | copy-start | bytes 12292
  14.0 33.1 %all-to-all-start = ((s32[1,128,32]{2,0,1:T(1,128)}), s32[1,128,32]{2,0,1:T(1,128)S(1)}, u32[]{:S(2)}, u32[]{:S(2)}) async-start(s32[1,128,32]{2,0,1:T(1,128)} %bitcast.8), calls=%async_computation | async-start | bytes 131072 | tf_op jit(solution)/shard_map/all_to_all | solution.py:271
  24.6 8.6 slice-start.1
  35.5 2.9 copy-start.19
  35.5 2.9 copy-start.27
  47.0 19.9 %all-to-all-start.1 = ((f32[128,1,160]{2,1,0:T(1,128)}), f32[128,1,160]{2,1,0:T(1,128)S(1)}, u32[]{:S(2)}, u32[]{:S(2)}) async-start(f32[128,1,160]{2,1,0:T(1,128)} %reshape.648), calls=%async_computation.1 | async-start | bytes 262144 | tf_op jit(solution)/shard_map/all_to_all | solution.py:270
  62.7 8.6 collective-permute-start.2
  64.5 7.3 collective-permute-start.3
  92.6 6.7 copy-start.14
  99.3 139.1 %copy-start.12 = (f32[1,128,32]{2,0,1:T(1,128)S(1)}, f32[1,128,32]{2,0,1:T(1,128)}, u32[]{:S(2)}) copy-start(f32[1,128,32]{2,0,1:T(1,128)} %get-tuple-element.39) | copy-start | bytes 49156
  99.3 139.1 %copy-start.13 = (pred[128,32]{1,0:T(8,128)(4,1)S(1)}, pred[128,32]{1,0:T(8,128)(4,1)}, u32[]{:S(2)}) copy-start(pred[128,32]{1,0:T(8,128)(4,1)} %compare_and_fusion) | copy-start | bytes 12292
  99.3 140.0 %copy-start.15 = (f32[4096]{0:T(1024)S(1)}, f32[4096]{0:T(1024)}, u32[]{:S(2)}) copy-start(f32[4096]{0:T(1024)} %mul.564) | copy-start | bytes 49156
  99.3 140.0 %copy-start.18 = (pred[4096]{0:T(1024)(128)(4,1)S(1)}, pred[4096]{0:T(1024)(128)(4,1)}, u32[]{:S(2)}) copy-start(pred[4096]{0:T(1024)(128)(4,1)} %compare_and_fusion.1) | copy-start | bytes 12292
  756.3 25.6 %copy-start = (f32[4,393216]{1,0:T(4,128)S(1)}, f32[4,393216]{1,0:T(4,128)}, u32[]{:S(2)}) copy-start(f32[4,393216]{1,0:T(4,128)} %scatter_fusion) | copy-start | bytes 18874372
  783.4 22.4 %copy-start.2 = (f32[1,3,768,512]{3,2,1,0:T(8,128)}, f32[1,3,768,512]{3,2,1,0:T(8,128)S(1)}, u32[]{:S(2)}) copy-start(f32[1,3,768,512]{3,2,1,0:T(8,128)S(1)} %copy.138) | copy-start | bytes 14155780
  786.7 26.6 %collective-permute-start.5 = (f32[48,1,512]{2,1,0:T(1,128)}, f32[48,1,512]{2,1,0:T(1,128)}, u32[]{:S(2)}, u32[]{:S(2)}) collective-permute-start(f32[48,1,512]{2,1,0:T(1,128)} %slice_bitcast_fusion.3), channel_id=1, source_target_pairs={{0,7},{1,0},{2,1},{3,2},{4,3},{5,4},{6,5},{7,6},{8,15},{9,8},{10,9... | collective-permute-start | bytes 294920 | tf_op jit(solution)/shard_map/ppermute | solution.py:33
  796.6 16.7 %collective-permute-start.4 = (f32[1,16,512]{2,1,0:T(8,128)}, f32[1,16,512]{2,1,0:T(8,128)}, u32[]{:S(2)}, u32[]{:S(2)}) collective-permute-start(f32[1,16,512]{2,1,0:T(8,128)} %slice_bitcast_fusion.5), channel_id=1, source_target_pairs={{0,120},{8,0},{16,8},{24,16},{32,24},{40,32},{48,40},{56,48},{64,5... | collective-permute-start | bytes 98312 | tf_op jit(solution)/shard_map/ppermute | solution.py:33
  807.5 4.3 copy-start.3
  811.8 1.9 copy-start.4
  811.8 2.0 slice-start.4
  813.3 6.3 copy-start.22
  813.3 6.3 copy-start.31
  818.5 1.1 copy-start.9
  844.3 8.7 copy-start.10
  848.8 34.6 %all-to-all-start.4 = ((f32[16,1,12288]{2,1,0:T(1,128)}), f32[16,1,12288]{2,1,0:T(1,128)S(1)}, u32[]{:S(2)}, u32[]{:S(2)}) async-start(f32[16,1,12288]{2,1,0:T(1,128)} %reshape.652), calls=%async_computation.4 | async-start | bytes 1572864 | tf_op jit(solution)/shard_map/all_to_all | solution.py:112
  883.4 0.9 copy-start.6
  884.3 22.1 %all-to-all-start.2 = ((f32[16,1,12288]{2,1,0:T(1,128)}), f32[16,1,12288]{2,1,0:T(1,128)S(1)}, u32[]{:S(2)}, u32[]{:S(2)}) async-start(f32[16,1,12288]{2,1,0:T(1,128)} %reshape.650), calls=%async_computation.2 | async-start | bytes 1572864 | tf_op jit(solution)/shard_map/all_to_all | solution.py:105
  906.4 22.7 %all-to-all-start.5 = ((f32[1,768,256]{1,0,2:T(1,128)}), f32[1,768,256]{1,0,2:T(1,128)}, u32[]{:S(2)}, u32[]{:S(2)}) async-start(f32[1,768,256]{1,0,2:T(1,128)} %copy.112), calls=%async_computation.5 | async-start | bytes 1572864 | tf_op jit(solution)/shard_map/all_to_all | solution.py:111
  926.8 7.9 copy-start.11
  929.1 19.6 %all-to-all-start.3 = ((f32[1,768,256]{1,0,2:T(1,128)}), f32[1,768,256]{1,0,2:T(1,128)S(1)}, u32[]{:S(2)}, u32[]{:S(2)}) async-start(f32[1,768,256]{1,0,2:T(1,128)} %copy.106), calls=%async_computation.3 | async-start | bytes 1572864 | tf_op jit(solution)/shard_map/all_to_all | solution.py:104
  948.7 22.7 %copy-start.33 = (f32[768,256]{0,1}, f32[768,256]{0,1:S(1)}, u32[]{:S(2)}) copy-start(f32[768,256]{0,1:S(1)} %fusion.22) | copy-start | bytes 2359300
  948.7 92.9 %all-to-all-start.10 = ((f32[128,1,128]{2,1,0:T(1,128)}), f32[128,1,128]{2,1,0:T(1,128)}, u32[]{:S(2)}, u32[]{:S(2)}) async-start(f32[128,1,128]{2,1,0:T(1,128)} %reshape.658), calls=%async_computation.10 | async-start | bytes 131072 | tf_op jit(solution)/shard_map/all_to_all | solution.py:278
  999.8 1.7 copy-start.34
  999.8 4.8 copy-start.29
  1004.6 0.9 copy-start.30
  1007.0 4.0 copy-start.17
  1007.0 4.0 copy-start.28
  1041.6 32.7 %all-to-all-start.8 = ((f32[1,768,1,256]{3,2,0,1:T(1,128)}), f32[1,768,1,256]{3,2,0,1:T(1,128)S(1)}, u32[]{:S(2)}, u32[]{:S(2)}) async-start(f32[1,768,1,256]{3,2,0,1:T(1,128)} %copy.117), calls=%async_computation.8 | async-start | bytes 1572864 | tf_op jit(solution)/shard_map/all_to_all | solution.py:157
  1074.3 19.5 %all-to-all-start.6 = ((f32[1,768,1,256]{3,2,0,1:T(1,128)}), f32[1,768,1,256]{3,2,0,1:T(1,128)S(1)}, u32[]{:S(2)}, u32[]{:S(2)}) async-start(f32[1,768,1,256]{3,2,0,1:T(1,128)} %copy.113), calls=%async_computation.6 | async-start | bytes 1572864 | tf_op jit(solution)/shard_map/all_to_all | solution.py:148
  1093.8 0.9 copy-start.7
  1094.8 19.7 %all-to-all-start.9 = ((f32[8,1,24576]{2,1,0:T(1,128)}), f32[8,1,24576]{2,1,0:T(1,128)S(1)}, u32[]{:S(2)}, u32[]{:S(2)}) async-start(f32[8,1,24576]{2,1,0:T(1,128)} %reshape.656), calls=%async_computation.9 | async-start | bytes 1572864 | tf_op jit(solution)/shard_map/all_to_all | solution.py:156
  1106.8 12.7 %copy-start.21 = (s32[1024]{0:T(1024)S(1)}, s32[1024]{0:T(1024)}, u32[]{:S(2)}) copy-start(s32[1024]{0:T(1024)} %copy-done.20) | copy-start | bytes 12292
  1109.7 9.8 copy-start.5
  1114.5 24.0 %all-to-all-start.7 = ((f32[8,1,24576]{2,1,0:T(1,128)}), f32[8,1,24576]{2,1,0:T(1,128)}, u32[]{:S(2)}, u32[]{:S(2)}) async-start(f32[8,1,24576]{2,1,0:T(1,128)} %reshape.654), calls=%async_computation.7 | async-start | bytes 1572864 | tf_op jit(solution)/shard_map/all_to_all | solution.py:147
  1119.5 6.8 copy-start.24
  1145.0 6.5 copy-start.8
  1145.0 6.5 copy-start.23
  1145.0 6.5 copy-start.32
  1155.1 7.7 collective-permute-start.7
  1156.7 6.1 collective-permute-start.6
  1162.8 2.2 slice-start.2
  1162.8 2.3 slice-start.3
where the time goes:
time: 1190 us; the launch traced here: 1170 us
  other arithmetic  629 us (53%)
  local copies, waits for them, and re-layouts  285 us (24%)
  matrix products  124 us (10%)
  starting transfers between devices  111 us (9%)
  waiting for transfers between devices  17.7 us (1%)
    scatter-add x1, other arithmetic, per_device(): forced = star_flat.at[:, target_cells].add(force_terms).reshape(star.shape)  517 us
    gather x2, local copies, waits for them, and re-layouts, per_device(): sampled = jnp.take(star_flat, target_cells, axis=1)  139 us
    unnamed x8, matrix products  97.3 us
    unnamed x95, local copies, waits for them, and re-layouts  47.5 us
    unnamed x4, other arithmetic  38.6 us
    slice x1, local copies, waits for them, and re-layouts, per_device(): return (velocity_out, forced[3], marker_force)  25.6 us
  transfers between devices with their start and end apart: 19, of which 4 were waited for; matrix products, arithmetic and copies ran while one was open for 22% of the time, Pallas kernels for 0%

commit v1 on v0

v1 whole, which is shorter than its diff:
```python
import functools
import math

import jax
import jax.numpy as jnp
import ml_dtypes
import numpy as np
from jax import lax
from jax.experimental import pallas as pl
from jax.experimental.pallas import tpu as pltpu
from jax.sharding import PartitionSpec as P

time_step = 0.1
viscosity = 0.4
diffusivity = 0.25
f32 = jnp.float32
bf16 = jnp.bfloat16
lanes = 128
slots = 32
vmem = pl.BlockSpec(memory_space=pltpu.VMEM)


def iota(shape, dim):
    return lax.broadcasted_iota(jnp.int32, shape, dim)


def call(body, out, args, scratch=(), name=None, micros=0):
    shapes = [jax.ShapeDtypeStruct(s, d) for s, d in out]
    moved = sum(a.size * a.dtype.itemsize for a in args)
    moved += sum(s.size * s.dtype.itemsize for s in shapes)
    held = moved + sum(math.prod(s.shape) * 4 for s in scratch if hasattr(s, "dtype"))
    moved = max(moved, micros * 3000000)
    return pl.pallas_call(
        body,
        out_shape=shapes,
        in_specs=[vmem] * len(args),
        out_specs=[vmem] * len(out),
        scratch_shapes=list(scratch),
        compiler_params=pltpu.CompilerParams(vmem_limit_bytes=held + 6 * 2**20),
        cost_estimate=pl.CostEstimate(flops=0, bytes_accessed=moved, transcendentals=0),
        name=name,
    )(*args)


def passed_along(value, axis, steps):
    count = lax.axis_size(axis)
    return lax.ppermute(value, axis, [(i, (i + steps) % count) for i in range(count)])


def real_basis(length):
    place = np.arange(length)
    columns, squares = [], []
    for k in range(length // 2 + 1):
        angle = 2.0 * np.pi * ((k * place) % length) / length
        scale = math.sqrt((1.0 if k in (0, length // 2) else 2.0) / length)
        square = 4.0 * math.sin(math.pi * k / length) ** 2
        columns.append(scale * np.cos(angle))
        squares.append(square)
        if k not in (0, length // 2):
            columns.append(scale * np.sin(angle))
            squares.append(square)
    return np.stack(columns, axis=1), np.array(squares)


def two_parts(table):
    high = table.astype(np.float32).astype(ml_dtypes.bfloat16)
    low = (table - high.astype(np.float64)).astype(np.float32).astype(ml_dtypes.bfloat16)
    return high, low


def decay_tables(squares_x, squares_z, n_grp, n_wide, rows_y):
    full_y = n_wide * rows_y
    local = squares_x.shape[0] // n_grp
    square = squares_z[None, :, None] + squares_x.reshape(n_grp, 1, local)
    mean_mode = square == 0.0
    safe = np.where(mean_mode, 1.0, square)
    root = 1.0 / (1.0 + safe / 2.0 + np.sqrt(safe + safe * safe / 4.0))
    root = np.where(mean_mode, 0.0, root)
    gain = np.where(mean_mode, 0.0, -root / (1.0 - root * root))
    half = rows_y // 2
    full = np.stack([root, root**half, gain], axis=1)
    full = np.concatenate([full, full], axis=3)
    device = root**rows_y
    small = np.stack([device, 1.0 / (1.0 - root**full_y)], axis=1)
    upper = small.shape[2] // 2
    small = np.concatenate([small[:, :, :upper], small[:, :, upper:]], axis=3)
    share = upper // n_wide
    small = small.reshape(n_grp, 2, n_wide, share, 2 * local).transpose(0, 2, 1, 3, 4)
    small = np.concatenate([small, small], axis=3)
    return full.astype(np.float32), small.astype(np.float32)


def split_two(value):
    high = value.astype(bf16)
    return high, (value - high.astype(f32)).astype(bf16)


def split_three(value):
    high = value.astype(bf16)
    rest = value - high.astype(f32)
    middle = rest.astype(bf16)
    return high, middle, (rest - middle.astype(f32)).astype(bf16)


def dot(left, right, dims=((1,), (0,))):
    return lax.dot_general(left, right, (dims, ((), ())), preferred_element_type=f32)


def pack_body(owner_ref, tile_ref, offset_ref, target_ref, eta_ref, send_ref, rank_ref):
    owners = send_ref.shape[0]
    held = owner_ref.shape[1]
    onehot = owner_ref[...] == iota((owners, held), 0)
    onehot = jnp.where(onehot, 1.0, 0.0)
    upto = jnp.where(iota((lanes, lanes), 0) <= iota((lanes, lanes), 1), 1.0, 0.0).astype(bf16)
    carry = jnp.zeros((owners, 1), f32)
    ranks = []
    for start in range(0, held, lanes):
        piece = onehot[:, start : start + lanes]
        running = dot(piece.astype(bf16), upto) + carry
        ranks.append(jnp.sum(running * piece, axis=0, keepdims=True) - 1.0)
        carry = carry + jnp.sum(piece, axis=1, keepdims=True)
    rank = jnp.concatenate(ranks, axis=1).astype(jnp.int32)
    rank_ref[...] = rank
    chosen = rank == iota((slots, held), 0)
    cell = (tile_ref[...] * lanes + offset_ref[...]).astype(f32)
    values = [target_ref[k : k + 1, :] for k in range(4)] + [eta_ref[...], cell]
    onehot = onehot.astype(bf16)
    total = jnp.zeros((owners, 6 * slots), f32)
    for part in range(3):
        rows = [
            jnp.where(chosen, split_three(v)[part].astype(f32), 0.0).astype(bf16) for v in values
        ]
        total = total + dot(onehot, jnp.concatenate(rows, axis=0), ((1,), (1,)))
    column = iota((owners, 2 * lanes), 1)
    slot = column - 5 * slots
    spare = (slot >= 0) & (slot < slots) & (slot.astype(f32) >= carry)
    total = jnp.concatenate([total, jnp.zeros((owners, 2 * lanes - 6 * slots), f32)], axis=1)
    send_ref[...] = total + jnp.where(spare, (slot * lanes).astype(f32), 0.0)


def unpack_body(
    n_grp, all_rows, row_cells, owner_ref, rank_ref, back_ref, place_ref, force_ref, mean_ref
):
    size = back_ref.shape[1] // 3
    owners = back_ref.shape[0] * n_grp
    held = owner_ref.shape[1]
    onehot = jnp.where(owner_ref[...] == iota((owners, held), 0), 1.0, 0.0).astype(bf16)
    sums = back_ref[:, 2 * size, :]
    sums = jnp.concatenate([sums, jnp.zeros((lanes - sums.shape[0], lanes), f32)], axis=0).T
    mine = jnp.where(place_ref[...] == 0, sums, 0.0)
    mean = jnp.sum(jnp.sum(sums, axis=1, keepdims=True), axis=0, keepdims=True)
    mine = jnp.sum(mine, axis=1, keepdims=True) * (1.0 / row_cells)
    mean_ref[...] = jnp.broadcast_to(mine - mean * (1.0 / (all_rows * row_cells)), mean_ref.shape)
    back = back_ref[:, size : 2 * size, :].reshape(owners, lanes).T
    spread = sum(dot(part, onehot) for part in split_three(back))
    chosen = rank_ref[...] == iota((slots, held), 0)
    for k in range(4):
        piece = jnp.where(chosen, spread[k * slots : (k + 1) * slots], 0.0)
        force_ref[k : k + 1, :] = jnp.sum(piece, axis=0, keepdims=True)


def swap_groups(value):
    row = iota(value.shape, 0) & 3
    group = lax.shift_right_logical(iota(value.shape, 1), 5)
    count = value.shape[0]
    out = value
    for k in (1, 2, 3):
        moved = pltpu.roll(value, 32 * k, 1)
        moved = jnp.where(
            row + k < 4, pltpu.roll(moved, count - k, 0), pltpu.roll(moved, 4 - k, 0)
        )
        out = jnp.where(((group - row) & 3) == k, moved, out)
    return out


def marker_part(recv_ref, out_ref, force_ref, samp, table, index, sem, tiles_x, depth_z):
    sources = recv_ref.shape[0]
    wide_lane = iota((sources, lanes), 1)
    second = recv_ref[:, lanes : 2 * lanes]
    cell = pltpu.roll(second.astype(jnp.int32), lanes - 32, 1)
    tile = lax.shift_right_logical(cell, 7)
    shift_x = tiles_x.bit_length() - 1
    shift_z = shift_x + depth_z.bit_length() - 1
    row = lax.shift_right_logical(tile, shift_z) * tiles_x + (tile & (tiles_x - 1))
    row = row * depth_z + (lax.shift_right_logical(tile, shift_x) & (depth_z - 1))
    spot = (iota((sources, lanes), 0) & 3) * 32 + (wide_lane & 31)
    there = (spot - cell) & (lanes - 1)
    back = (cell - spot) & (lanes - 1)
    table[...] = jnp.where(
        wide_lane < 32,
        4 * row,
        jnp.where(wide_lane < 64, pltpu.roll(there, 32, 1), pltpu.roll(back, 64, 1)),
    )
    copy = pltpu.make_async_copy(table, index, sem)
    copy.start()
    copy.wait()
    lane = iota((4, lanes), 1)

    def at(place):
        return pl.ds(pl.multiple_of(place, 4), 4)

    def gather(batch, carry):
        found = jnp.zeros((4, lanes), f32)
        for q in range(4):
            for r in range(slots):
                source = 4 * batch + q
                value = out_ref[at(index[source, r]), :]
                value = pltpu.roll(value, index[source, 32 + r], 1)
                found = jnp.where(lane == 32 * q + r, value, found)
        samp[pl.ds(pl.multiple_of(4 * batch, 4), 4), :] = found
        return carry

    lax.fori_loop(0, sources // 4, gather, 0)
    eta = jnp.where(wide_lane < 32, second, 0.0)
    eta = eta + pltpu.roll(eta, 32, 1)
    eta = eta + pltpu.roll(eta, 64, 1)
    force = swap_groups(eta) * (swap_groups(recv_ref[:, 0:lanes]) - samp[...])
    samp[...] = force
    force_ref[...] = swap_groups(force)

    def scatter(batch, carry):
        mine = samp[pl.ds(pl.multiple_of(4 * batch, 4), 4), :]
        for sub in range(4):
            source = 4 * batch + sub
            terms = []
            for r in range(slots):
                only = jnp.where(lane == 32 * sub + r, mine, 0.0)
                terms.append(pltpu.roll(only, index[source, 64 + r], 1))
            for q in range(0, slots, 4):
                places = [index[source, q + j] for j in range(4)]
                values = [out_ref[at(place), :] for place in places]
                for j in range(4):
                    for i in range(j):
                        values[j] = jnp.where(places[i] == places[j], values[i], values[j])
                    values[j] = values[j] + terms[q + j]
                for j in range(4):
                    out_ref[at(places[j]), :] = values[j]
        return carry

    lax.fori_loop(0, sources // 4, scatter, 0)


def at_row(y, x, f, tiles_x, depth_z):
    return pl.ds((y * tiles_x + x) * (4 * depth_z) + f, depth_z, stride=4)


def stencil_part(vel_ref, scal_ref, ylo_ref, yhi_ref, zlo_ref, zhi_ref, out_ref):
    _, rows_y, depth_z, length_x = vel_ref.shape
    tiles_x = length_x // lanes
    level = iota((depth_z, length_x), 0)

    def one_row(y, carry):
        at_low = y == 0
        at_high = y == rows_y - 1
        below = jnp.maximum(y - 1, 0)
        above = jnp.minimum(y + 1, rows_y - 1)
        flow = [vel_ref[f, y] for f in range(3)]
        for f in range(4):
            if f < 3:
                center = flow[f]
                low, high = vel_ref[f, below], vel_ref[f, above]
            else:
                center = scal_ref[y]
                low, high = scal_ref[below], scal_ref[above]
            south = jnp.where(at_low, ylo_ref[f], low)
            north = jnp.where(at_high, yhi_ref[f], high)
            east = pltpu.roll(center, length_x - 1, 1)
            west = pltpu.roll(center, 1, 1)
            top = jnp.broadcast_to(zhi_ref[f, pl.ds(y, 1), :], center.shape)
            bottom = jnp.broadcast_to(zlo_ref[f, pl.ds(y, 1), :], center.shape)
            upper = jnp.where(level == depth_z - 1, top, pltpu.roll(center, depth_z - 1, 0))
            lower = jnp.where(level == 0, bottom, pltpu.roll(center, 1, 0))
            transport = (
                flow[0] * (east - west) + flow[1] * (north - south) + flow[2] * (upper - lower)
            )
            around = east + west + north + south + upper + lower
            coeff = viscosity if f < 3 else diffusivity
            star = (
                center * (1.0 - 6.0 * time_step * coeff)
                + (time_step * coeff) * around
                - (0.5 * time_step) * transport
            )
            for x in range(tiles_x):
                out_ref[at_row(y, x, f, tiles_x, depth_z), :] = star[:, x * lanes : (x + 1) * lanes]
        return carry

    lax.fori_loop(0, rows_y, one_row, 0)


def wide_row(ref, f, y, tiles_x, depth_z):
    return jnp.concatenate(
        [ref[at_row(y, x, f, tiles_x, depth_z), :] for x in range(tiles_x)], axis=1
    )


def packed_rows(rows_y, depth_z, n_wide):
    cells = rows_y // 2 * depth_z
    row = cells + depth_z // 2
    plane = row + rows_y // 2
    return cells, row, plane, plane + n_wide, plane + n_wide + 8


def halves(one, two, first_half):
    even = jnp.where(first_half, one, pltpu.roll(two, lanes // 2, 1))
    odd = jnp.where(first_half, pltpu.roll(one, lanes // 2, 1), two)
    return even, odd


def times_x(value, high_ref, low_ref):
    high, low = split_two(value)
    return dot(high, high_ref[...]) + dot(low, high_ref[...]) + dot(high, low_ref[...])


def divergence_part(forced_ref, div, sums, shape):
    rows_y, depth_z, length_x = shape
    tiles_x = length_x // lanes
    rows = rows_y * depth_z
    level = iota((depth_z, length_x), 0)
    sums[...] = jnp.zeros_like(sums)

    def one_row(y, carry):
        after = jnp.minimum(y + 1, rows_y - 1)
        along = wide_row(forced_ref, 0, y, tiles_x, depth_z)
        second = wide_row(forced_ref, 1, y, tiles_x, depth_z)
        third = wide_row(forced_ref, 2, y, tiles_x, depth_z)
        north = wide_row(forced_ref, 1, after, tiles_x, depth_z)
        north = jnp.where(y == rows_y - 1, 0.0, north)
        upper = jnp.where(level == depth_z - 1, 0.0, pltpu.roll(third, depth_z - 1, 0))
        total = pltpu.roll(along, length_x - 1, 1) - along + (north - second) + (upper - third)
        div[pl.ds(pl.multiple_of(y * depth_z, depth_z), depth_z), :] = total
        div[pl.ds(rows + depth_z + y, 1), :] = third[0:1, :]
        folded = sum(second[:, x * lanes : (x + 1) * lanes] for x in range(tiles_x))
        sums[pl.ds(y, 1), :] = jnp.sum(folded, axis=0, keepdims=True)
        return carry

    lax.fori_loop(0, rows_y, one_row, 0)
    div[rows : rows + depth_z, :] = wide_row(forced_ref, 1, 0, tiles_x, depth_z)


def first_body(
    vel_ref,
    scal_ref,
    ylo_ref,
    yhi_ref,
    zlo_ref,
    zhi_ref,
    recv_ref,
    high_ref,
    low_ref,
    forced_ref,
    out_ref,
    force,
    samp,
    table,
    div,
    modes,
    index,
    sem,
):
    _, rows_y, depth_z, length_x = vel_ref.shape
    n_grp = out_ref.shape[0]
    n_wide = recv_ref.shape[0] // n_grp
    rows = rows_y * depth_z
    tiles_x = length_x // lanes
    stencil_part(vel_ref, scal_ref, ylo_ref, yhi_ref, zlo_ref, zhi_ref, forced_ref)
    marker_part(recv_ref, forced_ref, force, samp, table, index, sem, tiles_x, depth_z)
    divergence_part(forced_ref, div, samp, (rows_y, depth_z, length_x))
    chunk = div.shape[0] // 4
    for start in range(0, 4 * chunk, chunk):
        modes[start : start + chunk, :] = times_x(div[start : start + chunk, :], high_ref, low_ref)
    cells, row, plane, forces, end = packed_rows(rows_y, depth_z, n_wide)

    def send(front, back, size, place):
        first_half = iota((size, lanes), 1) < lanes // 2
        for j in range(n_grp // 2):
            one = modes[pl.ds(front, size), j * lanes : (j + 1) * lanes]
            two = modes[pl.ds(back, size), j * lanes : (j + 1) * lanes]
            even, odd = halves(one, two, first_half)
            out_ref[2 * j, pl.ds(place, size), :] = even
            out_ref[2 * j + 1, pl.ds(place, size), :] = odd

    def shuffle(y, carry):
        front = pl.multiple_of(y * depth_z, depth_z)
        back = pl.multiple_of((y + rows_y // 2) * depth_z, depth_z)
        send(front, back, depth_z, front)
        return carry

    lax.fori_loop(0, rows_y // 2, shuffle, 0)
    send(rows, rows + depth_z // 2, depth_z // 2, cells)
    send(rows + depth_z, rows + depth_z + rows_y // 2, rows_y // 2, row)
    total = jnp.broadcast_to(jnp.sum(samp[...].T, axis=0, keepdims=True), (end - forces, lanes))
    for g in range(n_grp):
        out_ref[g, plane:forces, :] = force[pl.ds(g, n_wide, stride=n_grp), :]
        out_ref[g, forces:end, :] = total


def times_z(value, high_ref, low_ref):
    high, low = split_two(value)
    return dot(high_ref[...], high) + dot(high_ref[...], low) + dot(low_ref[...], high)


def forward_z_body(
    rows_y, recv_ref, high_ref, low_ref, table_ref, coef_ref, ends_ref, small_ref
):
    n_grp = recv_ref.shape[0]
    n_wide = small_ref.shape[0]
    steps, full_z, _ = coef_ref.shape
    depth_z = full_z // n_grp
    cells, row, plane, forces, end = packed_rows(rows_y, depth_z, n_wide)
    root = table_ref[0]
    last = iota((n_grp, depth_z, lanes), 1) == depth_z - 1
    first_half = iota((full_z, lanes), 1) < lanes // 2

    def cells_of(step):
        value = recv_ref[:, pl.ds(pl.multiple_of(step * depth_z, depth_z), depth_z), :]
        edge = recv_ref[:, pl.ds(row + step, 1), :]
        edge = jnp.concatenate([edge[1:], edge[:1]], axis=0)
        value = value + jnp.where(last, jnp.broadcast_to(edge, value.shape), 0.0)
        return value.reshape(full_z, lanes)

    def one_pair(pair, total):
        value = jnp.concatenate([cells_of(2 * pair), cells_of(2 * pair + 1)], axis=1)
        found = times_z(value, high_ref, low_ref)
        coef_ref[2 * pair] = found[:, :lanes]
        coef_ref[2 * pair + 1] = found[:, lanes:]
        return found[:, lanes:] + root * (found[:, :lanes] + root * total)

    packed = recv_ref[:, cells:row, :]
    other = jnp.stack([pltpu.roll(packed[g], lanes // 2, 1) for g in range(n_grp)], axis=0)
    extra = jnp.concatenate([packed, other], axis=1).reshape(full_z, lanes)
    extra = jnp.where(first_half, times_z(extra, high_ref, low_ref), 0.0)
    ends_ref[2] = extra
    up = lax.fori_loop(0, steps // 2, one_pair, extra)
    down = lax.fori_loop(
        0,
        steps,
        lambda i, total: coef_ref[steps - 1 - i] + root * total,
        jnp.zeros((full_z, lanes), f32),
    )
    down = root * down
    ends_ref[0] = up
    ends_ref[1] = down
    over = table_ref[1]
    up_other = pltpu.roll(up, lanes // 2, 1)
    down_other = pltpu.roll(down, lanes // 2, 1)
    up = jnp.where(first_half, up_other + over * up, up + over * up_other)
    down = jnp.where(first_half, down + over * down_other, down_other + over * down)
    down = down + extra + pltpu.roll(extra, lanes // 2, 1)
    upper = full_z // 2
    share = upper // n_wide
    for k, value in enumerate((up, down)):
        value = jnp.where(first_half[:upper], value[:upper], value[upper:])
        for i in range(n_wide):
            small_ref[i, k * share : (k + 1) * share, :] = value[i * share : (i + 1) * share]
    sums = sum(recv_ref[g, forces:end, :] for g in range(n_grp))
    for i in range(n_wide):
        for g in range(n_grp):
            place = 2 * share + g
            small_ref[i, place : place + 1, :] = recv_ref[g, plane + i : plane + i + 1, :]
        small_ref[i, 2 * share + n_grp : 2 * share + n_grp + 8, :] = sums


def widen(small):
    first_half = iota(small.shape, 1) < lanes // 2
    other = pltpu.roll(small, lanes // 2, 1)
    return jnp.concatenate(
        [jnp.where(first_half, small, other), jnp.where(first_half, other, small)], axis=0
    )


def backward_z_body(
    rows_y, coef_ref, ends_ref, small_ref, table_ref, high_ref, low_ref, out_ref, ups, small
):
    n_grp = out_ref.shape[0]
    steps, full_z, _ = coef_ref.shape
    depth_z = full_z // n_grp
    cells, row, _, _, _ = packed_rows(rows_y, depth_z, small_ref.shape[0])
    root, over, gain = table_ref[0], table_ref[1], table_ref[2]
    first_half = iota((full_z, lanes), 1) < lanes // 2
    share = small_ref.shape[1] // 2
    for i in range(small_ref.shape[0]):
        for k in range(2):
            small[k, i * share : (i + 1) * share] = small_ref[i, k * share : (k + 1) * share]
    up_in = widen(small[0])
    down_in = widen(small[1])
    up_start = jnp.where(
        first_half,
        up_in + ends_ref[2],
        pltpu.roll(ends_ref[0], lanes // 2, 1) + over * up_in,
    )
    down = jnp.where(
        first_half, pltpu.roll(ends_ref[1], lanes // 2, 1) + over * down_in, down_in
    )

    def rising(step, total):
        total = coef_ref[step] + root * total
        ups[step] = total
        return total

    lax.fori_loop(0, steps, rising, up_start)

    def falling(i, total):
        pair = steps // 2 - 1 - i
        second = gain * (ups[2 * pair + 1] + total)
        total = root * (coef_ref[2 * pair + 1] + total)
        first = gain * (ups[2 * pair] + total)
        total = root * (coef_ref[2 * pair] + total)
        found = times_z(jnp.concatenate([first, second], axis=1), high_ref, low_ref)
        for j in range(2):
            step = 2 * pair + j
            value = found[:, j * lanes : (j + 1) * lanes]
            start = pl.multiple_of(step * depth_z, depth_z)
            out_ref[:, pl.ds(start, depth_z), :] = value.reshape(n_grp, depth_z, lanes)
            for g in range(n_grp):
                before = (g * depth_z - 1) % full_z
                out_ref[g, pl.ds(row + step, 1), :] = value[before : before + 1, :]
        return total

    down = lax.fori_loop(0, steps // 2, falling, down)
    extra = times_z(gain * (up_start + down), high_ref, low_ref)
    half = depth_z // 2
    for g in range(n_grp):
        start = g * depth_z
        out_ref[g, cells:row, :] = jnp.where(
            first_half[:half],
            extra[start : start + half],
            pltpu.roll(extra[start + half : start + depth_z], lanes // 2, 1),
        )


def last_body(recv_ref, forced_ref, mean_ref, high_ref, low_ref, vel_ref, scal_ref, modes, press_ref):
    n_grp = recv_ref.shape[0]
    _, rows_y, depth_z, length_x = vel_ref.shape
    rows = rows_y * depth_z
    tiles_x = length_x // lanes
    cells, row, _, _, _ = packed_rows(rows_y, depth_z, 0)

    def take(front, back, size, place):
        first_half = iota((size, lanes), 1) < lanes // 2
        for j in range(n_grp // 2):
            even = recv_ref[2 * j, pl.ds(place, size), :]
            odd = recv_ref[2 * j + 1, pl.ds(place, size), :]
            one, two = halves(even, odd, first_half)
            modes[pl.ds(front, size), j * lanes : (j + 1) * lanes] = one
            modes[pl.ds(back, size), j * lanes : (j + 1) * lanes] = two

    def shuffle(y, carry):
        front = pl.multiple_of(y * depth_z, depth_z)
        back = pl.multiple_of((y + rows_y // 2) * depth_z, depth_z)
        take(front, back, depth_z, front)
        return carry

    lax.fori_loop(0, rows_y // 2, shuffle, 0)
    take(rows, rows + depth_z // 2, depth_z // 2, cells)
    take(rows + depth_z, rows + depth_z + rows_y // 2, rows_y // 2, row)
    chunk = modes.shape[0] // 4
    for start in range(0, 4 * chunk, chunk):
        press_ref[start : start + chunk, :] = times_x(
            modes[start : start + chunk, :], high_ref, low_ref
        )
    level = iota((depth_z, length_x), 0)

    def one_row(y, carry):
        start = pl.multiple_of(y * depth_z, depth_z)
        before = pl.multiple_of(jnp.where(y == 0, rows, start - depth_z), depth_z)
        press = press_ref[pl.ds(start, depth_z), :]
        south = press_ref[pl.ds(before, depth_z), :]
        below = jnp.broadcast_to(press_ref[pl.ds(rows + depth_z + y, 1), :], press.shape)
        lower = jnp.where(level == 0, below, pltpu.roll(press, 1, 0))
        west = pltpu.roll(press, 1, 1)
        mean = mean_ref[pl.ds(y, 1), :]
        mean = jnp.concatenate([mean] * tiles_x, axis=1)
        vel_ref[0, y] = wide_row(forced_ref, 0, y, tiles_x, depth_z) - (press - west)
        vel_ref[1, y] = wide_row(forced_ref, 1, y, tiles_x, depth_z) - (press - south) - mean
        vel_ref[2, y] = wide_row(forced_ref, 2, y, tiles_x, depth_z) - (press - lower)
        scal_ref[y] = wide_row(forced_ref, 3, y, tiles_x, depth_z)
        return carry

    lax.fori_loop(0, rows_y, one_row, 0)


def ring_body(recv_ref, table_ref, out_ref):
    count, size, _ = out_ref.shape
    rising = iota((size, lanes), 0) < size // 2
    ends = [
        jnp.where(rising, recv_ref[i, 0:size, :], recv_ref[count - 1 - i, 0:size, :])
        for i in range(count)
    ]
    step, whole = table_ref[0], table_ref[1]
    total = ends[0]
    for i in range(1, count):
        total = ends[i] + step * total
    total = whole * total
    reached = []
    for i in range(count):
        reached.append(total)
        total = ends[i] + step * total
    for i in range(count):
        out_ref[i] = jnp.where(rising, reached[i], reached[count - 1 - i])


def per_device(
    tables, velocity, scalar, marker_owner, marker_tile, marker_offset, marker_target, marker_eta
):
    _, rows_y, depth_z, length_x = velocity.shape
    n_wide = lax.axis_size("wide")
    n_grp = lax.axis_size("grp")
    owners = n_wide * n_grp
    full_z = depth_z * n_grp
    rows = rows_y * depth_z
    tiles_x = length_x // lanes
    held = marker_owner.shape[0]
    x_high, x_low, xt_high, xt_low, z_high, z_low, zt_high, zt_low, full, small_table = tables
    my_grp = lax.axis_index("grp")
    my_wide = lax.axis_index("wide")
    full = lax.dynamic_index_in_dim(full, my_grp, 0, keepdims=False)
    small_table = lax.dynamic_slice(
        small_table, (my_grp, my_wide, 0, 0, 0), (1, 1) + small_table.shape[2:]
    )[0, 0]

    def edge(part, dim):
        index = 0 if part == 0 else velocity.shape[dim] - 1
        return jnp.concatenate(
            [
                lax.index_in_dim(velocity, index, dim, keepdims=False),
                lax.index_in_dim(scalar, index, dim - 1, keepdims=False)[None],
            ],
            axis=0,
        )

    y_low = passed_along(edge(1, 1), "wide", 1)
    y_high = passed_along(edge(0, 1), "wide", -1)
    z_low_cells = passed_along(edge(1, 2), "grp", 1)
    z_high_cells = passed_along(edge(0, 2), "grp", -1)

    owner = marker_owner[None, :]
    send, rank = call(
        pack_body,
        [((owners, 2 * lanes), f32), ((1, held), jnp.int32)],
        [owner, marker_tile[None, :], marker_offset[None, :], marker_target, marker_eta[None, :]],
        name="pack",
    )
    recv = lax.all_to_all(send, ("wide", "grp"), split_axis=0, concat_axis=0, tiled=True)
    flat = 4 * tiles_x * rows
    sent_rows = packed_rows(rows_y, depth_z, n_wide)[-1]
    back_rows = packed_rows(rows_y, depth_z, n_wide)[2]
    with_edges = rows + depth_z + rows_y
    forced, chunks = call(
        first_body,
        [((flat, lanes), f32), ((n_grp, sent_rows, lanes), f32)],
        [velocity, scalar, y_low, y_high, z_low_cells, z_high_cells, recv, x_high, x_low],
        [
            pltpu.VMEM((owners, lanes), f32),
            pltpu.VMEM((owners, lanes), f32),
            pltpu.VMEM((owners, lanes), jnp.int32),
            pltpu.VMEM((with_edges, length_x), f32),
            pltpu.VMEM((with_edges, length_x), f32),
            pltpu.SMEM((owners, lanes), jnp.int32),
            pltpu.SemaphoreType.DMA(()),
        ],
        name="first",
        micros=40,
    )
    chunks = lax.all_to_all(chunks, "grp", split_axis=0, concat_axis=0, tiled=True)
    ends_size = full_z // n_wide
    coef, ends, small = call(
        functools.partial(forward_z_body, rows_y),
        [
            ((rows_y // 2, full_z, lanes), f32),
            ((3, full_z, lanes), f32),
            ((n_wide, ends_size + n_grp + 8, lanes), f32),
        ],
        [chunks, z_high, z_low, full],
        name="forward_z",
    )
    small = lax.all_to_all(small, "wide", split_axis=0, concat_axis=0, tiled=True)
    (reach,) = call(
        ring_body, [((n_wide, ends_size, lanes), f32)], [small, small_table], name="ring"
    )
    reach = lax.all_to_all(reach, "wide", split_axis=0, concat_axis=0, tiled=True)
    place = (jnp.arange(lanes, dtype=jnp.int32) - my_wide)[None, :]
    marker_force, mine = call(
        functools.partial(unpack_body, n_grp, n_wide * rows_y, length_x * depth_z * n_grp),
        [((4, held), f32), ((lanes, lanes), f32)],
        [owner, rank, small, place],
        name="unpack",
    )
    (chunks,) = call(
        functools.partial(backward_z_body, rows_y),
        [((n_grp, back_rows, lanes), f32)],
        [coef, ends, reach, full, zt_high, zt_low],
        [
            pltpu.VMEM((rows_y // 2, full_z, lanes), f32),
            pltpu.VMEM((2, full_z // 2, lanes), f32),
        ],
        name="backward_z",
    )
    chunks = lax.all_to_all(chunks, "grp", split_axis=0, concat_axis=0, tiled=True)
    velocity_out, scalar_out = call(
        last_body,
        [(velocity.shape, f32), (scalar.shape, f32)],
        [chunks, forced, mine, xt_high, xt_low],
        [pltpu.VMEM((with_edges, length_x), f32), pltpu.VMEM((with_edges, length_x), f32)],
        name="last",
    )
    return velocity_out, scalar_out, marker_force


def solution(mesh):
    n_wide, n_grp = mesh.shape["wide"], mesh.shape["grp"]
    rows_y, full_z, length_x = 48, 128, 512
    basis_x, squares_x = real_basis(length_x)
    basis_z, squares_z = real_basis(full_z)
    parts = (
        two_parts(basis_x)
        + two_parts(basis_x.T)
        + two_parts(basis_z.T)
        + two_parts(basis_z)
        + decay_tables(squares_x, squares_z, n_grp, n_wide, rows_y)
    )

    def whole(*args):
        tables = tuple(jnp.asarray(part) for part in parts)
        return per_device(tables, *args)

    return jax.shard_map(
        whole,
        mesh=mesh,
        in_specs=(
            P(None, "wide", "grp", None),
            P("wide", "grp", None),
            P(("wide", "grp")),
            P(("wide", "grp")),
            P(("wide", "grp")),
            P(None, ("wide", "grp")),
            P(("wide", "grp")),
        ),
        out_specs=(P(None, "wide", "grp", None), P("wide", "grp", None), P(None, ("wide", "grp"))),
        check_vma=False,
    )
```

time: 1190 us -> 181 us (0.15); the launches traced: 1170 us -> 180 us
  other arithmetic: 629 us -> 0.08 us
  local copies, waits for them, and re-layouts: 285 us -> 18.9 us
  matrix products: 124 us -> 0 us
  starting transfers between devices: 111 us -> 23.1 us
  Pallas kernels: 0 us -> 61.1 us
  waiting for transfers between devices: 17.7 us -> 49.8 us
  blocking collectives: 0 us -> 26.7 us
    scatter-add x1 -> x0, other arithmetic: 517 us -> none  [per_device(): forced = star_flat.at[:, target_cells].add(force_terms).reshape(star.shape)]
    gather x3 -> x0, local copies, waits for them, and re-layouts: 142 us -> none  [the longest x2 139 us: per_device(): sampled = jnp.take(star_flat, target_cells, axis=1)]
    unnamed x8 -> x0, matrix products: 97.3 us -> none
    all_to_all x11 -> x3, starting transfers between devices: 83.5 us -> 14.9 us  [the longest x2 11.4 us: per_device(): lax.all_to_all(chunks, 'grp', split_axis=0, concat_axis=0, tiled=True)]
    pallas_call x0 -> x7, Pallas kernels: none -> 61.1 us  [call(): pl.pallas_call(body, out_shape=shapes, in_specs=[vmem] * len(args), out_s...]
    unnamed x4 -> x0, other arithmetic: 38.6 us -> none
    all_to_all x11 -> x3, waiting for transfers between devices: 12.2 us -> 49.8 us  [the longest x2 43.3 us: per_device(): lax.all_to_all(chunks, 'grp', split_axis=0, concat_axis=0, tiled=True)]
    unnamed x95 -> x45, local copies, waits for them, and re-layouts: 47.5 us -> 11.4 us
  transfers between devices with their start and end apart: 19 -> 7, of which waited for: 4 -> 3; matrix products, arithmetic and copies ran while one was open for 22% -> 2% of each run, Pallas kernels for 0% -> 1%
where the time goes in v1:
time: 181 us; the launch traced here: 180 us
  Pallas kernels  61.1 us (34%)
  waiting for transfers between devices  49.8 us (28%)
  blocking collectives  26.7 us (15%)
  starting transfers between devices  23.1 us (13%)
  local copies, waits for them, and re-layouts  18.9 us (10%)
    pallas_call x7, Pallas kernels, call(): pl.pallas_call(body, out_shape=shapes, in_specs=[vmem] * len(args), out_s...  61.1 us
    all_to_all x2, waiting for transfers between devices, per_device(): lax.all_to_all(chunks, 'grp', split_axis=0, concat_axis=0, tiled=True)  43.3 us
    all_to_all x1, blocking collectives, per_device(): lax.all_to_all(send, ('wide', 'grp'), split_axis=0, concat_axis=0, tiled=...  16.9 us
    all_to_all x2, starting transfers between devices, per_device(): lax.all_to_all(chunks, 'grp', split_axis=0, concat_axis=0, tiled=True)  11.4 us
    unnamed x45, local copies, waits for them, and re-layouts  11.4 us
    all_to_all x1, blocking collectives, per_device(): lax.all_to_all(reach, 'wide', split_axis=0, concat_axis=0, tiled=True)  9.79 us
    ppermute x4, starting transfers between devices, passed_along(): lax.ppermute(value, axis, [(i, (i + steps) % count) for i in range(count)])  8.14 us
    all_to_all x1, waiting for transfers between devices, per_device(): lax.all_to_all(small, 'wide', split_axis=0, concat_axis=0, tiled=True)  6.44 us
  transfers between devices with their start and end apart: 7, of which 3 were waited for; matrix products, arithmetic and copies ran while one was open for 2% of the time, Pallas kernels for 1%

profile of v1, /device:TPU:1, one launch (start us, length us, event | category | flops | bytes accessed | tf_op | source)
XLA Modules:
  0.0 180.5 jit_solution(2620929416830977936)
XLA Ops:
  0.6 0.0 copy-start
  0.6 1.7 fusion.1
  2.4 3.1 %fusion = (f32[3,48,1,512]{3,2,1,0:T(1,128)S(1)}, f32[3,48,1,512]{3,2,1,0:T(1,128)S(1)}) fusion(f32[3,48,16,512]{3,2,1,0:T(8,128)} %vel_ref.1), kind=kLoop, calls=%fused_computation.14 | loop fusion | bytes 1179648 | tf_op jit(solution)/shard_map/slice | solution.py:625
  5.5 0.0 copy-start.15
  5.5 0.0 copy-start.16
  5.5 0.0 copy-start.17
  5.6 0.0 copy-start.18
  5.6 0.0 copy-start.19
  5.6 3.0 %collective-permute-start.2 = (f32[4,48,512]{2,1,0:T(8,128)S(1)}, f32[4,48,512]{2,1,0:T(8,128)S(1)}, u32[]{:S(2)}, u32[]{:S(2)}) collective-permute-start(f32[4,48,512]{2,1,0:T(8,128)S(1)} %pad_maximum_fusion), channel_id=1, source_target_pairs={{0,1},{1,2},{2,3},{3,4},{4,5},{5,6},{6,7},{7,0},{8,9},{9,10},{10,1... | collective-permute-start | bytes 1179656 | tf_op jit(solution)/shard_map/ppermute | solution.py:47
  8.7 0.0 copy-start.3
  8.7 0.0 collective-permute-start.3
  8.8 0.0 copy-done
  8.8 0.9 fusion.2
  9.7 1.4 collective-permute-start
  11.1 3.7 %collective-permute-start.1 = (f32[4,16,512]{2,1,0:T(8,128)S(1)}, f32[4,16,512]{2,1,0:T(8,128)S(1)}, u32[]{:S(2)}, u32[]{:S(2)}) collective-permute-start(f32[4,16,512]{2,1,0:T(8,128)S(1)} %pad_maximum_fusion.3), channel_id=1, source_target_pairs={{0,120},{8,0},{16,8},{24,16},{32,24},{40,32},{48,40},{56,48},{64,5... | collective-permute-start | bytes 393224 | tf_op jit(solution)/shard_map/ppermute | solution.py:47
  14.8 0.0 copy-done.15
  14.8 0.0 copy-done.16
  14.8 0.0 copy-done.17
  14.8 0.0 copy-done.18
  14.8 0.0 copy-done.19
  14.8 0.7 pack.1
  15.5 0.1 copy.32
  15.7 16.9 %all_to_all.31 = f32[128,1,256]{2,1,0:T(1,128)S(1)} all-to-all(f32[128,1,256]{2,1,0:T(1,128)S(1)} %copy.32), channel_id=1, replica_groups=mesh['wide'=16,'grp'=8] {'wide','grp'}, dimensions={0} | all-to-all | bytes 262144 | tf_op jit(solution)/shard_map/all_to_all | solution.py:643
  32.6 0.0 collective-permute-done.ylo_ref
  32.6 0.0 collective-permute-done.1.yhi_ref
  32.7 0.0 collective-permute-done.2.zlo_ref
  32.7 0.0 collective-permute-done.3.zhi_ref
  32.7 0.0 copy-done.3
  32.7 0.0 copy-start.9
  32.7 1.0 copy-done.9
  33.7 0.0 copy-start.10
  33.7 1.0 copy-done.10
  34.8 40.7 %first.1 = (f32[12288,128]{1,0:T(8,128)S(1)}, f32[8,440,128]{2,1,0:T(8,128)S(1)}) custom-call(f32[3,48,16,512]{3,2,1,0:T(8,128)S(1)} %copy-done, f32[48,16,512]{2,1,0:T(8,128)S(1)} %copy-done.3, f32[4,16,512]{2,1,0:T(8,128)S(1)} %collective-permute-done.ylo_ref, f32[4,16,512]{2,1,0:T(8,128)S(1)} %collective-permute-done.1.yhi_ref, ...), custom_call_target="tpu_custom_call" | custom-call | bytes 120000000 | tf_op jit(solution)/shard_map/first/pallas_call | solution.py:33
  75.5 0.0 copy-start.1
  75.5 2.6 %copy-done.1 = f32[12288,128]{1,0:T(8,128)} copy-done((f32[12288,128]{1,0:T(8,128)}, f32[12288,128]{1,0:T(8,128)S(1)}, u32[]{:S(2)}) %copy-start.1) | copy-done | bytes 6291480
  78.1 0.0 copy-start.4
  78.1 1.2 copy-done.4
  79.3 0.0 copy-start.11
  79.3 0.0 copy-start.12
  79.3 4.6 %all-to-all-start.1 = ((f32[8,440,128]{2,1,0:T(8,128)}), f32[8,440,128]{2,1,0:T(8,128)S(1)}, u32[]{:S(2)}, u32[]{:S(2)}) async-start(f32[8,440,128]{2,1,0:T(8,128)} %copy-done.4), calls=%async_computation.1 | async-start | bytes 3604480 | tf_op jit(solution)/shard_map/all_to_all | solution.py:664
  83.9 0.0 copy-start.13
  83.9 0.0 copy-start.14
  83.9 0.9 dynamic-slice_bitcast_fusion.table_ref
  84.9 22.2 %all-to-all-done.1.recv_ref = f32[8,440,128]{2,1,0:T(8,128)S(1)} async-done(((f32[8,440,128]{2,1,0:T(8,128)}), f32[8,440,128]{2,1,0:T(8,128)S(1)}, u32[]{:S(2)}, u32[]{:S(2)}) %all-to-all-start.1) | async-done | bytes 1802272 | tf_op jit(solution)/shard_map/all_to_all | solution.py:664
  107.1 0.0 copy-done.11
  107.1 0.0 copy-done.12
  107.1 3.8 %forward_z.1 = (f32[24,128,128]{2,1,0:T(8,128)S(1)}, f32[3,128,128]{2,1,0:T(8,128)S(1)}, f32[16,24,128]{2,1,0:T(8,128)}) custom-call(f32[8,440,128]{2,1,0:T(8,128)S(1)} %all-to-all-done.1.recv_ref, bf16[128,128]{1,0:T(8,128)(2,1)S(1)} %copy-done.12, bf16[128,128]{1,0:T(8,128)(2,1)S(1)} %copy-done.11, f32[3,128,128]{2,1,0:T(8,128)S(1)} %dynamic-slice_bitcast_fusion.table_ref), custom_call_target="tpu_custom_call" | custom-call | bytes 4030464 | tf_op jit(solution)/shard_map/forward_z/pallas_call | solution.py:33
  110.9 1.1 copy-done.5
  112.0 3.5 %all-to-all-start.2 = ((f32[16,24,128]{2,1,0:T(8,128)}), f32[16,24,128]{2,1,0:T(8,128)S(1)}, u32[]{:S(2)}, u32[]{:S(2)}) async-start(f32[16,24,128]{2,1,0:T(8,128)} %get-tuple-element.18), calls=%async_computation.2 | async-start | bytes 393216 | tf_op jit(solution)/shard_map/all_to_all | solution.py:676
  115.6 0.7 dynamic-slice_bitcast_fusion.1.table_ref
  116.3 6.4 %all-to-all-done.2.recv_ref.back_ref = f32[16,24,128]{2,1,0:T(8,128)S(1)} async-done(((f32[16,24,128]{2,1,0:T(8,128)}), f32[16,24,128]{2,1,0:T(8,128)S(1)}, u32[]{:S(2)}, u32[]{:S(2)}) %all-to-all-start.2) | async-done | bytes 196640 | tf_op jit(solution)/shard_map/all_to_all | solution.py:676
  122.7 0.1 ring.1
  122.8 9.8 %all_to_all.32.small_ref = f32[16,8,128]{2,1,0:T(8,128)S(1)} all-to-all(f32[16,8,128]{2,1,0:T(8,128)S(1)} %ring.1), channel_id=1, replica_groups=mesh['wide'=16,'grp'=8] {'wide'}, dimensions={0} | all-to-all | bytes 131072 | tf_op jit(solution)/shard_map/all_to_all | solution.py:680
  132.6 0.0 copy-done.13
  132.6 0.0 copy-done.14
  132.6 1.4 copy-done.6
  134.0 4.6 %backward_z.1 = f32[8,416,128]{2,1,0:T(8,128)} custom-call(f32[24,128,128]{2,1,0:T(8,128)S(1)} %copy-done.6, f32[3,128,128]{2,1,0:T(8,128)S(1)} %get-tuple-element.17.ends_ref, f32[16,8,128]{2,1,0:T(8,128)S(1)} %all_to_all.32.small_ref, f32[3,128,128]{2,1,0:T(8,128)S(1)} %dynamic-slice_bitcast_fusion.table_ref, bf16[128,128]{1,0:T(8,128)(2,1)S(1)} %copy-done.14, ...), custom_call_target="tpu_custom_call" | custom-call | bytes 3801088 | tf_op jit(solution)/shard_map/backward_z/pallas_call | solution.py:33
  138.6 6.8 %all-to-all-start.4 = ((f32[8,416,128]{2,1,0:T(8,128)}), f32[8,416,128]{2,1,0:T(8,128)S(1)}, u32[]{:S(2)}, u32[]{:S(2)}) async-start(f32[8,416,128]{2,1,0:T(8,128)} %backward_z.1), calls=%async_computation.4 | async-start | bytes 3407872 | tf_op jit(solution)/shard_map/all_to_all | solution.py:698
  145.4 1.0 unpack.1
  146.4 21.1 %all-to-all-done.4.recv_ref = f32[8,416,128]{2,1,0:T(8,128)S(1)} async-done(((f32[8,416,128]{2,1,0:T(8,128)}), f32[8,416,128]{2,1,0:T(8,128)S(1)}, u32[]{:S(2)}, u32[]{:S(2)}) %all-to-all-start.4) | async-done | bytes 1703968 | tf_op jit(solution)/shard_map/all_to_all | solution.py:698
  167.6 0.0 copy-done.7
  167.6 0.0 copy-done.8
  167.6 2.8 %copy-done.2 = f32[12288,128]{1,0:T(8,128)S(1)} copy-done((f32[12288,128]{1,0:T(8,128)S(1)}, f32[12288,128]{1,0:T(8,128)}, u32[]{:S(2)}) %copy-start.2) | copy-done | bytes 6291480
  170.3 10.2 %last.1 = (f32[3,48,16,512]{3,2,1,0:T(8,128)}, f32[48,16,512]{2,1,0:T(8,128)}) custom-call(f32[8,416,128]{2,1,0:T(8,128)S(1)} %all-to-all-done.4.recv_ref, f32[12288,128]{1,0:T(8,128)S(1)} %copy-done.2, f32[128,128]{1,0:T(8,128)S(1)} %get-tuple-element.21.mean_ref, bf16[512,512]{1,0:T(8,128)(2,1)S(1)} %copy-done.8, bf16[512,512]{1,0:T(8,128)(2,1)S(1)} %copy-done.7), custom_call_target="tpu_custom_call" | custom-call | bytes 15400960 | tf_op jit(solution)/shard_map/last/pallas_call | solution.py:33
  (16 shorter events, 0.2 us)
Async XLA Ops:
  0.6 8.1 %copy-start = (f32[3,48,16,512]{3,2,1,0:T(8,128)S(1)}, f32[3,48,16,512]{3,2,1,0:T(8,128)}, u32[]{:S(2)}) copy-start(f32[3,48,16,512]{3,2,1,0:T(8,128)} %vel_ref.1) | copy-start | bytes 14155780
  5.5 9.3 %copy-start.15 = (f32[4,1024]{1,0:T(4,128)S(1)}, f32[4,1024]{1,0:T(4,128)}, u32[]{:S(2)}) copy-start(f32[4,1024]{1,0:T(4,128)} %target_ref.1) | copy-start | bytes 49156
  5.5 9.3 %copy-start.16 = (s32[1024]{0:T(1024)S(1)}, s32[1024]{0:T(1024)}, u32[]{:S(2)}) copy-start(s32[1024]{0:T(1024)} %param.19) | copy-start | bytes 12292
  5.5 9.2 %copy-start.17 = (s32[1024]{0:T(1024)S(1)}, s32[1024]{0:T(1024)}, u32[]{:S(2)}) copy-start(s32[1024]{0:T(1024)} %param.20) | copy-start | bytes 12292
  5.6 9.2 %copy-start.18 = (s32[1024]{0:T(1024)S(1)}, s32[1024]{0:T(1024)}, u32[]{:S(2)}) copy-start(s32[1024]{0:T(1024)} %param.21) | copy-start | bytes 12292
  5.6 9.2 %copy-start.19 = (f32[1024]{0:T(1024)S(1)}, f32[1024]{0:T(1024)}, u32[]{:S(2)}) copy-start(f32[1024]{0:T(1024)} %param.23) | copy-start | bytes 12292
  5.6 27.0 %collective-permute-start.2 = (f32[4,48,512]{2,1,0:T(8,128)S(1)}, f32[4,48,512]{2,1,0:T(8,128)S(1)}, u32[]{:S(2)}, u32[]{:S(2)}) collective-permute-start(f32[4,48,512]{2,1,0:T(8,128)S(1)} %pad_maximum_fusion), channel_id=1, source_target_pairs={{0,1},{1,2},{2,3},{3,4},{4,5},{5,6},{6,7},{7,0},{8,9},{9,10},{10,1... | collective-permute-start | bytes 1179656 | tf_op jit(solution)/shard_map/ppermute | solution.py:47
  8.7 24.0 %copy-start.3 = (f32[48,16,512]{2,1,0:T(8,128)S(1)}, f32[48,16,512]{2,1,0:T(8,128)}, u32[]{:S(2)}) copy-start(f32[48,16,512]{2,1,0:T(8,128)} %scal_ref.1) | copy-start | bytes 4718596
  8.7 23.9 %collective-permute-start.3 = (f32[4,48,512]{2,1,0:T(8,128)S(1)}, f32[4,48,512]{2,1,0:T(8,128)S(1)}, u32[]{:S(2)}, u32[]{:S(2)}) collective-permute-start(f32[4,48,512]{2,1,0:T(8,128)S(1)} %pad_maximum_fusion.1), channel_id=1, source_target_pairs={{0,7},{1,0},{2,1},{3,2},{4,3},{5,4},{6,5},{7,6},{8,15},{9,8},{10,9... | collective-permute-start | bytes 1179656 | tf_op jit(solution)/shard_map/ppermute | solution.py:47
  9.7 23.0 %collective-permute-start = (f32[4,16,512]{2,1,0:T(8,128)S(1)}, f32[4,16,512]{2,1,0:T(8,128)S(1)}, u32[]{:S(2)}, u32[]{:S(2)}) collective-permute-start(f32[4,16,512]{2,1,0:T(8,128)S(1)} %pad_maximum_fusion.2), channel_id=1, source_target_pairs={{0,8},{8,16},{16,24},{24,32},{32,40},{40,48},{48,56},{56,64},{64,7... | collective-permute-start | bytes 393224 | tf_op jit(solution)/shard_map/ppermute | solution.py:47
  11.1 21.6 %collective-permute-start.1 = (f32[4,16,512]{2,1,0:T(8,128)S(1)}, f32[4,16,512]{2,1,0:T(8,128)S(1)}, u32[]{:S(2)}, u32[]{:S(2)}) collective-permute-start(f32[4,16,512]{2,1,0:T(8,128)S(1)} %pad_maximum_fusion.3), channel_id=1, source_target_pairs={{0,120},{8,0},{16,8},{24,16},{32,24},{40,32},{48,40},{56,48},{64,5... | collective-permute-start | bytes 393224 | tf_op jit(solution)/shard_map/ppermute | solution.py:47
  32.7 1.0 copy-start.9
  33.7 1.0 copy-start.10
  75.5 2.6 %copy-start.1 = (f32[12288,128]{1,0:T(8,128)}, f32[12288,128]{1,0:T(8,128)S(1)}, u32[]{:S(2)}) copy-start(f32[12288,128]{1,0:T(8,128)S(1)} %get-tuple-element.19.forced_ref) | copy-start | bytes 18874372
  78.1 1.2 copy-start.4
  79.3 27.8 %copy-start.11 = (bf16[128,128]{1,0:T(8,128)(2,1)S(1)}, bf16[128,128]{1,0:T(8,128)(2,1)}, u32[]{:S(2)}) copy-start(bf16[128,128]{1,0:T(8,128)(2,1)} %constant.44.clone.low_ref) | copy-start | bytes 98308
  79.3 27.8 %copy-start.12 = (bf16[128,128]{1,0:T(8,128)(2,1)S(1)}, bf16[128,128]{1,0:T(8,128)(2,1)}, u32[]{:S(2)}) copy-start(bf16[128,128]{1,0:T(8,128)(2,1)} %constant.43.clone.high_ref) | copy-start | bytes 98308
  79.3 27.8 %all-to-all-start.1 = ((f32[8,440,128]{2,1,0:T(8,128)}), f32[8,440,128]{2,1,0:T(8,128)S(1)}, u32[]{:S(2)}, u32[]{:S(2)}) async-start(f32[8,440,128]{2,1,0:T(8,128)} %copy-done.4), calls=%async_computation.1 | async-start | bytes 3604480 | tf_op jit(solution)/shard_map/all_to_all | solution.py:664
  83.9 48.7 %copy-start.13 = (bf16[128,128]{1,0:T(8,128)(2,1)S(1)}, bf16[128,128]{1,0:T(8,128)(2,1)}, u32[]{:S(2)}) copy-start(bf16[128,128]{1,0:T(8,128)(2,1)} %constant.46.clone.low_ref) | copy-start | bytes 98308
  83.9 48.7 %copy-start.14 = (bf16[128,128]{1,0:T(8,128)(2,1)S(1)}, bf16[128,128]{1,0:T(8,128)(2,1)}, u32[]{:S(2)}) copy-start(bf16[128,128]{1,0:T(8,128)(2,1)} %constant.45.clone.high_ref) | copy-start | bytes 98308
  110.9 1.1 copy-start.5
  112.0 10.7 %all-to-all-start.2 = ((f32[16,24,128]{2,1,0:T(8,128)}), f32[16,24,128]{2,1,0:T(8,128)S(1)}, u32[]{:S(2)}, u32[]{:S(2)}) async-start(f32[16,24,128]{2,1,0:T(8,128)} %get-tuple-element.18), calls=%async_computation.2 | async-start | bytes 393216 | tf_op jit(solution)/shard_map/all_to_all | solution.py:676
  132.6 1.4 copy-start.6
  138.6 28.9 %copy-start.7 = (bf16[512,512]{1,0:T(8,128)(2,1)S(1)}, bf16[512,512]{1,0:T(8,128)(2,1)}, u32[]{:S(2)}) copy-start(bf16[512,512]{1,0:T(8,128)(2,1)} %constant.42.clone.low_ref) | copy-start | bytes 1572868
  138.6 28.9 %copy-start.8 = (bf16[512,512]{1,0:T(8,128)(2,1)S(1)}, bf16[512,512]{1,0:T(8,128)(2,1)}, u32[]{:S(2)}) copy-start(bf16[512,512]{1,0:T(8,128)(2,1)} %constant.41.clone.high_ref) | copy-start | bytes 1572868
  138.6 28.9 %all-to-all-start.4 = ((f32[8,416,128]{2,1,0:T(8,128)}), f32[8,416,128]{2,1,0:T(8,128)S(1)}, u32[]{:S(2)}, u32[]{:S(2)}) async-start(f32[8,416,128]{2,1,0:T(8,128)} %backward_z.1), calls=%async_computation.4 | async-start | bytes 3407872 | tf_op jit(solution)/shard_map/all_to_all | solution.py:698
  167.6 2.8 %copy-start.2 = (f32[12288,128]{1,0:T(8,128)S(1)}, f32[12288,128]{1,0:T(8,128)}, u32[]{:S(2)}) copy-start(f32[12288,128]{1,0:T(8,128)} %copy-done.1) | copy-start | bytes 18874372

commit v2 on v1

--- a/solution.py
+++ b/solution.py
@@ -18,25 +18,29 @@
 lanes = 128
 slots = 32
 vmem = pl.BlockSpec(memory_space=pltpu.VMEM)
+hbm = pl.BlockSpec(memory_space=pltpu.HBM)
 
 
 def iota(shape, dim):
     return lax.broadcasted_iota(jnp.int32, shape, dim)
 
 
-def call(body, out, args, scratch=(), name=None, micros=0):
+def call(body, out, args, scratch=(), name=None, micros=0, far_in=(), far_out=(), room=0):
     shapes = [jax.ShapeDtypeStruct(s, d) for s, d in out]
     moved = sum(a.size * a.dtype.itemsize for a in args)
     moved += sum(s.size * s.dtype.itemsize for s in shapes)
-    held = moved + sum(math.prod(s.shape) * 4 for s in scratch if hasattr(s, "dtype"))
+    near = [a for i, a in enumerate(args) if i not in far_in]
+    near += [s for i, s in enumerate(shapes) if i not in far_out]
+    held = sum(a.size * a.dtype.itemsize for a in near)
+    held += sum(math.prod(s.shape) * 4 for s in scratch if s.shape)
     moved = max(moved, micros * 3000000)
     return pl.pallas_call(
         body,
         out_shape=shapes,
-        in_specs=[vmem] * len(args),
-        out_specs=[vmem] * len(out),
+        in_specs=[hbm if i in far_in else vmem for i in range(len(args))],
+        out_specs=[hbm if i in far_out else vmem for i in range(len(out))],
         scratch_shapes=list(scratch),
-        compiler_params=pltpu.CompilerParams(vmem_limit_bytes=held + 6 * 2**20),
+        compiler_params=pltpu.CompilerParams(vmem_limit_bytes=max(held + 6 * 2**20, room * 2**20)),
         cost_estimate=pl.CostEstimate(flops=0, bytes_accessed=moved, transcendentals=0),
         name=name,
     )(*args)
@@ -106,7 +110,35 @@
     return lax.dot_general(left, right, (dims, ((), ())), preferred_element_type=f32)
 
 
-def pack_body(owner_ref, tile_ref, offset_ref, target_ref, eta_ref, send_ref, rank_ref):
+def pack_body(*refs):
+    far, near, sems = refs[:7], refs[13:20], refs[20]
+    send_ref, rank_ref, y_first, y_last, z_first, z_last = refs[7:13]
+    owner_ref, tile_ref, offset_ref, target_ref, eta_ref, vel_ref, scal_ref = near
+    copies = [pltpu.make_async_copy(a, b, sems.at[i]) for i, (a, b) in enumerate(zip(far, near))]
+    for copy in copies:
+        copy.start()
+    for copy in copies[:5]:
+        copy.wait()
+    pack_markers(owner_ref, tile_ref, offset_ref, target_ref, eta_ref, send_ref, rank_ref)
+    for copy in copies[5:]:
+        copy.wait()
+    rows_y, depth_z, _ = scal_ref.shape
+
+    def edges(y, carry):
+        for z, out in ((0, z_first), (depth_z - 1, z_last)):
+            for f in range(3):
+                out[f, pl.ds(y, 1), :] = vel_ref[f, y, z : z + 1, :]
+            out[3, pl.ds(y, 1), :] = scal_ref[y, z : z + 1, :]
+        return carry
+
+    lax.fori_loop(0, rows_y, edges, 0)
+    for y, out in ((0, y_first), (rows_y - 1, y_last)):
+        for f in range(3):
+            out[f] = vel_ref[f, y]
+        out[3] = scal_ref[y]
+
+
+def pack_markers(owner_ref, tile_ref, offset_ref, target_ref, eta_ref, send_ref, rank_ref):
     owners = send_ref.shape[0]
     held = owner_ref.shape[1]
     onehot = owner_ref[...] == iota((owners, held), 0)
@@ -244,7 +276,9 @@
     return pl.ds((y * tiles_x + x) * (4 * depth_z) + f, depth_z, stride=4)
 
 
-def stencil_part(vel_ref, scal_ref, ylo_ref, yhi_ref, zlo_ref, zhi_ref, out_ref):
+def stencil_part(
+    vel_far, scal_far, ylo_ref, yhi_ref, zlo_ref, zhi_ref, vel_ref, scal_ref, out_ref, sems
+):
     _, rows_y, depth_z, length_x = vel_ref.shape
     tiles_x = length_x // lanes
     level = iota((depth_z, length_x), 0)
@@ -284,7 +318,29 @@
                 out_ref[at_row(y, x, f, tiles_x, depth_z), :] = star[:, x * lanes : (x + 1) * lanes]
         return carry
 
-    lax.fori_loop(0, rows_y, one_row, 0)
+    pieces = sems.shape[0] // 2
+    size = rows_y // pieces
+    fetches = []
+    for piece in range(pieces):
+        part = pl.ds(piece * size, size)
+        fetches.append(
+            [
+                pltpu.make_async_copy(
+                    vel_far.at[:, part], vel_ref.at[:, part], sems.at[2 * piece]
+                ),
+                pltpu.make_async_copy(
+                    scal_far.at[part], scal_ref.at[part], sems.at[2 * piece + 1]
+                ),
+            ]
+        )
+        for copy in fetches[-1]:
+            copy.start()
+    for copy in fetches[0]:
+        copy.wait()
+    for piece in range(pieces):
+        for copy in fetches[piece + 1] if piece + 1 < pieces else ():
+            copy.wait()
+        lax.fori_loop(piece * size, (piece + 1) * size, one_row, 0)
 
 
 def wide_row(ref, f, y, tiles_x, depth_z):
@@ -298,6 +354,29 @@
     row = cells + depth_z // 2
     plane = row + rows_y // 2
     return cells, row, plane, plane + n_wide, plane + n_wide + 8
+
+
+partners = (4, 5, 2, 3, 6, 7, 1, 0)
+
+
+def by_partner(ref, parts):
+    mine = lax.axis_index("grp")
+    for d, part in zip(partners, parts):
+        part[...] = ref[jnp.bitwise_xor(mine, d)]
+
+
+def from_partner(parts, ref):
+    mine = lax.axis_index("grp")
+    for d, part in zip(partners, parts):
+        ref[jnp.bitwise_xor(mine, d)] = part[...]
+
+
+def exchanged(parts):
+    count = len(parts)
+    return [
+        part if d == 0 else lax.ppermute(part, "grp", [(i, i ^ d) for i in range(count)])
+        for d, part in zip(partners, parts)
+    ]
 
 
 def halves(one, two, first_half):
@@ -337,38 +416,25 @@
     div[rows : rows + depth_z, :] = wide_row(forced_ref, 1, 0, tiles_x, depth_z)
 
 
-def first_body(
-    vel_ref,
-    scal_ref,
-    ylo_ref,
-    yhi_ref,
-    zlo_ref,
-    zhi_ref,
-    recv_ref,
-    high_ref,
-    low_ref,
-    forced_ref,
-    out_ref,
-    force,
-    samp,
-    table,
-    div,
-    modes,
-    index,
-    sem,
-):
-    _, rows_y, depth_z, length_x = vel_ref.shape
+def first_body(shape, *refs):
+    vel_far, scal_far, ylo, yhi, zlo, zhi, recv_ref, high_ref, low_ref, far_ref, *rest = refs
+    out_refs, rest = rest[:-13], rest[-13:]
+    vel_ref, scal_ref, sems, forced_ref, out_ref, *rest = rest
+    force, samp, table, div, modes, index, sem, far_sem = rest
+    rows_y, depth_z, length_x = shape
     n_grp = out_ref.shape[0]
     n_wide = recv_ref.shape[0] // n_grp
     rows = rows_y * depth_z
     tiles_x = length_x // lanes
-    stencil_part(vel_ref, scal_ref, ylo_ref, yhi_ref, zlo_ref, zhi_ref, forced_ref)
+    stencil_part(vel_far, scal_far, ylo, yhi, zlo, zhi, vel_ref, scal_ref, forced_ref, sems)
     marker_part(recv_ref, forced_ref, force, samp, table, index, sem, tiles_x, depth_z)
+    keep = pltpu.make_async_copy(forced_ref, far_ref, far_sem)
+    keep.start()
     divergence_part(forced_ref, div, samp, (rows_y, depth_z, length_x))
     chunk = div.shape[0] // 4
     for start in range(0, 4 * chunk, chunk):
         modes[start : start + chunk, :] = times_x(div[start : start + chunk, :], high_ref, low_ref)
-    cells, row, plane, forces, end = packed_rows(rows_y, depth_z, n_wide)
+    row, plane, forces, sums_row, end = packed_rows(rows_y, depth_z, n_wide)
 
     def send(front, back, size, place):
         first_half = iota((size, lanes), 1) < lanes // 2
@@ -386,12 +452,14 @@
         return carry
 
     lax.fori_loop(0, rows_y // 2, shuffle, 0)
-    send(rows, rows + depth_z // 2, depth_z // 2, cells)
-    send(rows + depth_z, rows + depth_z + rows_y // 2, rows_y // 2, row)
-    total = jnp.broadcast_to(jnp.sum(samp[...].T, axis=0, keepdims=True), (end - forces, lanes))
+    send(rows, rows + depth_z // 2, depth_z // 2, row)
+    send(rows + depth_z, rows + depth_z + rows_y // 2, rows_y // 2, plane)
+    total = jnp.broadcast_to(jnp.sum(samp[...].T, axis=0, keepdims=True), (end - sums_row, lanes))
     for g in range(n_grp):
-        out_ref[g, plane:forces, :] = force[pl.ds(g, n_wide, stride=n_grp), :]
-        out_ref[g, forces:end, :] = total
+        out_ref[g, forces:sums_row, :] = force[pl.ds(g, n_wide, stride=n_grp), :]
+        out_ref[g, sums_row:end, :] = total
+    by_partner(out_ref, out_refs)
+    keep.wait()
 
 
 def times_z(value, high_ref, low_ref):
@@ -399,21 +467,22 @@
     return dot(high_ref[...], high) + dot(high_ref[...], low) + dot(low_ref[...], high)
 
 
-def forward_z_body(
-    rows_y, recv_ref, high_ref, low_ref, table_ref, coef_ref, ends_ref, small_ref
-):
+def forward_z_body(rows_y, *refs):
+    recv_refs, refs = refs[:-7], refs[-7:]
+    high_ref, low_ref, table_ref, coef_ref, ends_ref, small_ref, recv_ref = refs
     n_grp = recv_ref.shape[0]
+    from_partner(recv_refs, recv_ref)
     n_wide = small_ref.shape[0]
     steps, full_z, _ = coef_ref.shape
     depth_z = full_z // n_grp
-    cells, row, plane, forces, end = packed_rows(rows_y, depth_z, n_wide)
+    row, plane, forces, sums_row, end = packed_rows(rows_y, depth_z, n_wide)
     root = table_ref[0]
     last = iota((n_grp, depth_z, lanes), 1) == depth_z - 1
     first_half = iota((full_z, lanes), 1) < lanes // 2
 
     def cells_of(step):
         value = recv_ref[:, pl.ds(pl.multiple_of(step * depth_z, depth_z), depth_z), :]
-        edge = recv_ref[:, pl.ds(row + step, 1), :]
+        edge = recv_ref[:, pl.ds(plane + step, 1), :]
         edge = jnp.concatenate([edge[1:], edge[:1]], axis=0)
         value = value + jnp.where(last, jnp.broadcast_to(edge, value.shape), 0.0)
         return value.reshape(full_z, lanes)
@@ -425,7 +494,7 @@
         coef_ref[2 * pair + 1] = found[:, lanes:]
         return found[:, lanes:] + root * (found[:, :lanes] + root * total)
 
-    packed = recv_ref[:, cells:row, :]
+    packed = recv_ref[:, row:plane, :]
     other = jnp.stack([pltpu.roll(packed[g], lanes // 2, 1) for g in range(n_grp)], axis=0)
     extra = jnp.concatenate([packed, other], axis=1).reshape(full_z, lanes)
     extra = jnp.where(first_half, times_z(extra, high_ref, low_ref), 0.0)
@@ -452,11 +521,11 @@
         value = jnp.where(first_half[:upper], value[:upper], value[upper:])
         for i in range(n_wide):
             small_ref[i, k * share : (k + 1) * share, :] = value[i * share : (i + 1) * share]
-    sums = sum(recv_ref[g, forces:end, :] for g in range(n_grp))
+    sums = sum(recv_ref[g, sums_row:end, :] for g in range(n_grp))
     for i in range(n_wide):
         for g in range(n_grp):
             place = 2 * share + g
-            small_ref[i, place : place + 1, :] = recv_ref[g, plane + i : plane + i + 1, :]
+            small_ref[i, place : place + 1, :] = recv_ref[g, forces + i : forces + i + 1, :]
         small_ref[i, 2 * share + n_grp : 2 * share + n_grp + 8, :] = sums
 
 
@@ -469,12 +538,14 @@
 
 
 def backward_z_body(
-    rows_y, coef_ref, ends_ref, small_ref, table_ref, high_ref, low_ref, out_ref, ups, small
+    rows_y, coef_ref, ends_ref, small_ref, table_ref, high_ref, low_ref, *rest
 ):
+    out_refs, rest = rest[:-3], rest[-3:]
+    out_ref, ups, small = rest
     n_grp = out_ref.shape[0]
     steps, full_z, _ = coef_ref.shape
     depth_z = full_z // n_grp
-    cells, row, _, _, _ = packed_rows(rows_y, depth_z, small_ref.shape[0])
+    row, plane, _, _, _ = packed_rows(rows_y, depth_z, small_ref.shape[0])
     root, over, gain = table_ref[0], table_ref[1], table_ref[2]
     first_half = iota((full_z, lanes), 1) < lanes // 2
     share = small_ref.shape[1] // 2
@@ -513,7 +584,7 @@
             out_ref[:, pl.ds(start, depth_z), :] = value.reshape(n_grp, depth_z, lanes)
             for g in range(n_grp):
                 before = (g * depth_z - 1) % full_z
-                out_ref[g, pl.ds(row + step, 1), :] = value[before : before + 1, :]
+                out_ref[g, pl.ds(plane + step, 1), :] = value[before : before + 1, :]
         return total
 
     down = lax.fori_loop(0, steps // 2, falling, down)
@@ -521,19 +592,25 @@
     half = depth_z // 2
     for g in range(n_grp):
         start = g * depth_z
-        out_ref[g, cells:row, :] = jnp.where(
+        out_ref[g, row:plane, :] = jnp.where(
             first_half[:half],
             extra[start : start + half],
             pltpu.roll(extra[start + half : start + depth_z], lanes // 2, 1),
         )
-
-
-def last_body(recv_ref, forced_ref, mean_ref, high_ref, low_ref, vel_ref, scal_ref, modes, press_ref):
+    by_partner(out_ref, out_refs)
+
+
+def last_body(far_ref, mean_ref, high_ref, low_ref, *refs):
+    recv_refs, refs = refs[:-10], refs[-10:]
+    vel_far, scal_far, vel_ref, scal_ref, recv_ref, forced_ref, modes, press_ref, sem, sems = refs
+    fetch = pltpu.make_async_copy(far_ref, forced_ref, sem)
+    fetch.start()
+    from_partner(recv_refs, recv_ref)
     n_grp = recv_ref.shape[0]
     _, rows_y, depth_z, length_x = vel_ref.shape
     rows = rows_y * depth_z
     tiles_x = length_x // lanes
-    cells, row, _, _, _ = packed_rows(rows_y, depth_z, 0)
+    row, plane, _, _, _ = packed_rows(rows_y, depth_z, 0)
 
     def take(front, back, size, place):
         first_half = iota((size, lanes), 1) < lanes // 2
@@ -551,8 +628,8 @@
         return carry
 
     lax.fori_loop(0, rows_y // 2, shuffle, 0)
-    take(rows, rows + depth_z // 2, depth_z // 2, cells)
-    take(rows + depth_z, rows + depth_z + rows_y // 2, rows_y // 2, row)
+    take(rows, rows + depth_z // 2, depth_z // 2, row)
+    take(rows + depth_z, rows + depth_z + rows_y // 2, rows_y // 2, plane)
     chunk = modes.shape[0] // 4
     for start in range(0, 4 * chunk, chunk):
         press_ref[start : start + chunk, :] = times_x(
@@ -576,7 +653,25 @@
         scal_ref[y] = wide_row(forced_ref, 3, y, tiles_x, depth_z)
         return carry
 
-    lax.fori_loop(0, rows_y, one_row, 0)
+    fetch.wait()
+    pieces = sems.shape[0] // 2
+    size = rows_y // pieces
+    copies = []
+    for piece in range(pieces):
+        lax.fori_loop(piece * size, (piece + 1) * size, one_row, 0)
+        part = pl.ds(piece * size, size)
+        copies += [
+            pltpu.make_async_copy(
+                vel_ref.at[:, part], vel_far.at[:, part], sems.at[2 * piece]
+            ),
+            pltpu.make_async_copy(
+                scal_ref.at[part], scal_far.at[part], sems.at[2 * piece + 1]
+            ),
+        ]
+        copies[-2].start()
+        copies[-1].start()
+    for copy in copies:
+        copy.wait()
 
 
 def ring_body(recv_ref, table_ref, out_ref):
@@ -610,7 +705,7 @@
     rows = rows_y * depth_z
     tiles_x = length_x // lanes
     held = marker_owner.shape[0]
-    x_high, x_low, xt_high, xt_low, z_high, z_low, zt_high, zt_low, full, small_table = tables
+    x_high, x_low, xt_high, xt_low, fz_high, fz_low, bz_high, bz_low, full, small_table = tables
     my_grp = lax.axis_index("grp")
     my_wide = lax.axis_index("wide")
     full = lax.dynamic_index_in_dim(full, my_grp, 0, keepdims=False)
@@ -618,38 +713,54 @@
         small_table, (my_grp, my_wide, 0, 0, 0), (1, 1) + small_table.shape[2:]
     )[0, 0]
 
-    def edge(part, dim):
-        index = 0 if part == 0 else velocity.shape[dim] - 1
-        return jnp.concatenate(
-            [
-                lax.index_in_dim(velocity, index, dim, keepdims=False),
-                lax.index_in_dim(scalar, index, dim - 1, keepdims=False)[None],
-            ],
-            axis=0,
-        )
-
-    y_low = passed_along(edge(1, 1), "wide", 1)
-    y_high = passed_along(edge(0, 1), "wide", -1)
-    z_low_cells = passed_along(edge(1, 2), "grp", 1)
-    z_high_cells = passed_along(edge(0, 2), "grp", -1)
-
     owner = marker_owner[None, :]
-    send, rank = call(
+    send, rank, y_first, y_last, z_first, z_last = call(
         pack_body,
-        [((owners, 2 * lanes), f32), ((1, held), jnp.int32)],
-        [owner, marker_tile[None, :], marker_offset[None, :], marker_target, marker_eta[None, :]],
+        [((owners, 2 * lanes), f32), ((1, held), jnp.int32)]
+        + [((4, depth_z, length_x), f32)] * 2
+        + [((4, rows_y, length_x), f32)] * 2,
+        [
+            owner,
+            marker_tile[None, :],
+            marker_offset[None, :],
+            marker_target,
+            marker_eta[None, :],
+            velocity,
+            scalar,
+        ],
+        [
+            pltpu.VMEM((1, held), jnp.int32),
+            pltpu.VMEM((1, held), jnp.int32),
+            pltpu.VMEM((1, held), jnp.int32),
+            pltpu.VMEM((4, held), f32),
+            pltpu.VMEM((1, held), f32),
+            pltpu.VMEM(velocity.shape, f32),
+            pltpu.VMEM(scalar.shape, f32),
+            pltpu.SemaphoreType.DMA((7,)),
+        ],
         name="pack",
-    )
+        room=58,
+        far_in=range(7),
+    )
+    z_low = passed_along(z_last, "grp", 1)
+    z_high = passed_along(z_first, "grp", -1)
+    y_low = passed_along(y_last, "wide", 1)
+    y_high = passed_along(y_first, "wide", -1)
     recv = lax.all_to_all(send, ("wide", "grp"), split_axis=0, concat_axis=0, tiled=True)
     flat = 4 * tiles_x * rows
     sent_rows = packed_rows(rows_y, depth_z, n_wide)[-1]
     back_rows = packed_rows(rows_y, depth_z, n_wide)[2]
     with_edges = rows + depth_z + rows_y
-    forced, chunks = call(
-        first_body,
-        [((flat, lanes), f32), ((n_grp, sent_rows, lanes), f32)],
-        [velocity, scalar, y_low, y_high, z_low_cells, z_high_cells, recv, x_high, x_low],
+    forced, *chunks = call(
+        functools.partial(first_body, scalar.shape),
+        [((flat, lanes), f32)] + [((sent_rows, lanes), f32)] * n_grp,
+        [velocity, scalar, y_low, y_high, z_low, z_high, recv, x_high, x_low],
         [
+            pltpu.VMEM(velocity.shape, f32),
+            pltpu.VMEM(scalar.shape, f32),
+            pltpu.SemaphoreType.DMA((8,)),
+            pltpu.VMEM((flat, lanes), f32),
+            pltpu.VMEM((n_grp, sent_rows, lanes), f32),
             pltpu.VMEM((owners, lanes), f32),
             pltpu.VMEM((owners, lanes), f32),
             pltpu.VMEM((owners, lanes), jnp.int32),
@@ -657,11 +768,15 @@
             pltpu.VMEM((with_edges, length_x), f32),
             pltpu.SMEM((owners, lanes), jnp.int32),
             pltpu.SemaphoreType.DMA(()),
+            pltpu.SemaphoreType.DMA(()),
         ],
         name="first",
+        room=58,
         micros=40,
-    )
-    chunks = lax.all_to_all(chunks, "grp", split_axis=0, concat_axis=0, tiled=True)
+        far_in=(0, 1),
+        far_out=(0,),
+    )
+    chunks = exchanged(chunks)
     ends_size = full_z // n_wide
     coef, ends, small = call(
         functools.partial(forward_z_body, rows_y),
@@ -670,7 +785,10 @@
             ((3, full_z, lanes), f32),
             ((n_wide, ends_size + n_grp + 8, lanes), f32),
         ],
-        [chunks, z_high, z_low, full],
+        [*chunks, fz_high, fz_low, full],
+        [
+            pltpu.VMEM((n_grp, sent_rows, lanes), f32),
+        ],
         name="forward_z",
     )
     small = lax.all_to_all(small, "wide", split_axis=0, concat_axis=0, tiled=True)
@@ -685,23 +803,36 @@
         [owner, rank, small, place],
         name="unpack",
     )
-    (chunks,) = call(
+    chunks = call(
         functools.partial(backward_z_body, rows_y),
-        [((n_grp, back_rows, lanes), f32)],
-        [coef, ends, reach, full, zt_high, zt_low],
+        [((back_rows, lanes), f32)] * n_grp,
+        [coef, ends, reach, full, bz_high, bz_low],
         [
+            pltpu.VMEM((n_grp, back_rows, lanes), f32),
             pltpu.VMEM((rows_y // 2, full_z, lanes), f32),
             pltpu.VMEM((2, full_z // 2, lanes), f32),
         ],
         name="backward_z",
     )
-    chunks = lax.all_to_all(chunks, "grp", split_axis=0, concat_axis=0, tiled=True)
+    chunks = exchanged(chunks)
     velocity_out, scalar_out = call(
         last_body,
         [(velocity.shape, f32), (scalar.shape, f32)],
-        [chunks, forced, mine, xt_high, xt_low],
-        [pltpu.VMEM((with_edges, length_x), f32), pltpu.VMEM((with_edges, length_x), f32)],
+        [forced, mine, xt_high, xt_low, *chunks],
+        [
+            pltpu.VMEM(velocity.shape, f32),
+            pltpu.VMEM(scalar.shape, f32),
+            pltpu.VMEM((n_grp, back_rows, lanes), f32),
+            pltpu.VMEM((flat, lanes), f32),
+            pltpu.VMEM((with_edges, length_x), f32),
+            pltpu.VMEM((with_edges, length_x), f32),
+            pltpu.SemaphoreType.DMA(()),
+            pltpu.SemaphoreType.DMA((8,)),
+        ],
         name="last",
+        room=54,
+        far_in=(0,),
+        far_out=(0, 1),
     )
     return velocity_out, scalar_out, marker_force
 

time: 181 us -> 167 us (0.923)
  waiting for transfers between devices: 49.8 us -> 29.3 us
  local copies, waits for them, and re-layouts: 18.9 us -> 8.23 us
  starting transfers between devices: 23.1 us -> 32.9 us
  Pallas kernels: 61.1 us -> 68 us
    all_to_all x2 -> x0, waiting for transfers between devices: 43.3 us -> none  [per_device(): lax.all_to_all(chunks, 'grp', split_axis=0, concat_axis=0, tiled=True)]
    ppermute x0 -> x14, waiting for transfers between devices: none -> 23.1 us  [exchanged(): lax.ppermute(part, 'grp', [(i, i ^ d) for i in range(count)])]
    ppermute x0 -> x14, starting transfers between devices: none -> 21.3 us  [exchanged(): lax.ppermute(part, 'grp', [(i, i ^ d) for i in range(count)])]
    all_to_all x2 -> x0, starting transfers between devices: 11.4 us -> none  [per_device(): lax.all_to_all(chunks, 'grp', split_axis=0, concat_axis=0, tiled=True)]
    pallas_call x7, Pallas kernels: 61.1 us -> 68 us  [call(): pl.pallas_call(body, out_shape=shapes, in_specs=[hbm if i in far_in else...]
    unnamed x45, local copies, waits for them, and re-layouts: 11.4 us -> 5.53 us
    slice x3 -> x0, local copies, waits for them, and re-layouts: 5.7 us -> none  [the longest x1 3.12 us: edge(): lax.index_in_dim(velocity, index, dim, keepdims=False)]
  transfers between devices with their start and end apart: 7 -> 19, of which waited for: 3 -> 9; matrix products, arithmetic and copies ran while one was open for 2% -> 2% of each run, Pallas kernels for 1% -> 1%
where the time goes in v2:
time: 167 us
  Pallas kernels  68 us (41%)
  starting transfers between devices  32.9 us (20%)
  waiting for transfers between devices  29.3 us (18%)
  blocking collectives  27.3 us (16%)
  local copies, waits for them, and re-layouts  8.23 us (5%)
    pallas_call x7, Pallas kernels, call(): pl.pallas_call(body, out_shape=shapes, in_specs=[hbm if i in far_in else...  68 us
    ppermute x14, waiting for transfers between devices, exchanged(): lax.ppermute(part, 'grp', [(i, i ^ d) for i in range(count)])  23.1 us
    ppermute x14, starting transfers between devices, exchanged(): lax.ppermute(part, 'grp', [(i, i ^ d) for i in range(count)])  21.3 us
    all_to_all x1, blocking collectives, per_device(): lax.all_to_all(send, ('wide', 'grp'), split_axis=0, concat_axis=0, tiled=...  17.1 us
    all_to_all x1, blocking collectives, per_device(): lax.all_to_all(reach, 'wide', split_axis=0, concat_axis=0, tiled=True)  10.2 us
    ppermute x4, starting transfers between devices, passed_along(): lax.ppermute(value, axis, [(i, (i + steps) % count) for i in range(count)])  7.97 us
    all_to_all x1, waiting for transfers between devices, per_device(): lax.all_to_all(small, 'wide', split_axis=0, concat_axis=0, tiled=True)  6.21 us
    unnamed x45, local copies, waits for them, and re-layouts  5.53 us
  transfers between devices with their start and end apart: 19, of which 9 were waited for; matrix products, arithmetic and copies ran while one was open for 2% of the time, Pallas kernels for 1%

profile of v2, /device:TPU:1, one launch (start us, length us, event | category | flops | bytes accessed | tf_op | source)
XLA Modules:
  0.0 166.6 jit_solution(2239466161920575251)
XLA Ops:
  0.6 4.5 %pack.1 = (f32[128,256]{1,0:T(8,128)}, s32[1,1024]{1,0:T(1,128)}, f32[4,16,512]{2,1,0:T(8,128)}, f32[4,16,512]{2,1,0:T(8,128)}, f32[4,48,512]{2,1,0:T(8,128)}, /*index=5*/f32[4,48,512]{2,1,0:T(8,128)}) custom-call(s32[1,1024]{1,0:T(1,128)} %bitcast.12, s32[1,1024]{1,0:T(1,128)} %bitcast.16, s32[1,1024]{1,0:T(1,128)} %bitcast.17, f32[4,1024]{1,0:T(4,128)} %refs_3_.1, ...), custom_call_target="tpu_custom_call" | custom-call | bytes 7507968 | tf_op jit(solution)/shard_map/pack/pallas_call | solution.py:37
  5.1 3.0 %collective-permute-start.2 = (f32[4,48,512]{2,1,0:T(8,128)}, f32[4,48,512]{2,1,0:T(8,128)S(1)}, u32[]{:S(2)}, u32[]{:S(2)}) collective-permute-start(f32[4,48,512]{2,1,0:T(8,128)} %get-tuple-element.35), channel_id=1, source_target_pairs={{0,1},{1,2},{2,3},{3,4},{4,5},{5,6},{6,7},{7,0},{8,9},{9,10},{10,1... | collective-permute-start | bytes 1179656 | tf_op jit(solution)/shard_map/ppermute | solution.py:51
  8.2 0.0 collective-permute-start.3
  8.2 1.3 collective-permute-start
  9.5 3.6 %collective-permute-start.1 = (f32[4,16,512]{2,1,0:T(8,128)}, f32[4,16,512]{2,1,0:T(8,128)S(1)}, u32[]{:S(2)}, u32[]{:S(2)}) collective-permute-start(f32[4,16,512]{2,1,0:T(8,128)} %get-tuple-element.34), channel_id=1, source_target_pairs={{0,120},{8,0},{16,8},{24,16},{32,24},{40,32},{48,40},{56,48},{64,5... | collective-permute-start | bytes 393224 | tf_op jit(solution)/shard_map/ppermute | solution.py:51
  13.1 1.0 copy.20
  14.1 17.1 %all_to_all.21 = f32[128,1,256]{2,1,0:T(1,128)S(1)} all-to-all(f32[128,1,256]{2,1,0:T(1,128)S(1)} %copy.20), channel_id=1, replica_groups=mesh['wide'=16,'grp'=8] {'wide','grp'}, dimensions={0} | all-to-all | bytes 262144 | tf_op jit(solution)/shard_map/all_to_all | solution.py:749
  31.2 0.7 copy.23
  31.9 0.0 collective-permute-done.refs_2_
  31.9 0.0 collective-permute-done.1.refs_3_
  31.9 0.0 collective-permute-done.2.refs_4_
  31.9 0.0 copy-start.11
  31.9 0.0 collective-permute-done.3.refs_5_
  31.9 0.0 copy-start.12
  32.0 0.6 copy-done.20
  32.5 0.1 copy-done.21
  32.6 0.1 copy-done.11
  32.7 0.1 copy-done.12
  32.9 44.5 %first.1 = (f32[12288,128]{1,0:T(8,128)}, f32[440,128]{1,0:T(8,128)}, f32[440,128]{1,0:T(8,128)}, f32[440,128]{1,0:T(8,128)}, f32[440,128]{1,0:T(8,128)}, /*inde...) custom-call(f32[3,48,16,512]{3,2,1,0:T(8,128)} %refs_0_.1, ...), custom_call_target="tpu_custom_call" | custom-call | bytes 120000000 | tf_op jit(solution)/shard_map/first/pallas_call | solution.py:37
  77.4 1.3 collective-permute-start.4
  78.7 2.9 %collective-permute-start.5 = (f32[440,128]{1,0:T(8,128)}, f32[440,128]{1,0:T(8,128)S(1)}, u32[]{:S(2)}, u32[]{:S(2)}) collective-permute-start(f32[440,128]{1,0:T(8,128)} %get-tuple-element.41), channel_id=1, source_target_pairs={{0,5},{1,4},{2,7},{3,6},{4,1},{5,0},{6,3},{7,2},{8,13},{9,12},{10,... | collective-permute-start | bytes 675848 | tf_op jit(solution)/shard_map/ppermute | solution.py:377
  81.6 0.1 collective-permute-start.6
  81.7 0.8 collective-permute-start.7
  82.4 0.9 collective-permute-start.8
  83.4 1.8 %collective-permute-done.4.refs_0_ = f32[440,128]{1,0:T(8,128)S(1)} collective-permute-done((f32[440,128]{1,0:T(8,128)}, f32[440,128]{1,0:T(8,128)S(1)}, u32[]{:S(2)}, u32[]{:S(2)}) %collective-permute-start.4) | collective-permute-done | bytes 225312 | tf_op jit(solution)/shard_map/ppermute | solution.py:377
  85.2 3.7 %collective-permute-start.9 = (f32[440,128]{1,0:T(8,128)}, f32[440,128]{1,0:T(8,128)S(1)}, u32[]{:S(2)}, u32[]{:S(2)}) collective-permute-start(f32[440,128]{1,0:T(8,128)} %get-tuple-element.45), channel_id=1, source_target_pairs={{0,7},{1,6},{2,5},{3,4},{4,3},{5,2},{6,1},{7,0},{8,15},{9,14},{10,... | collective-permute-start | bytes 675848 | tf_op jit(solution)/shard_map/ppermute | solution.py:377
  88.8 3.9 %collective-permute-done.5.refs_1_ = f32[440,128]{1,0:T(8,128)S(1)} collective-permute-done((f32[440,128]{1,0:T(8,128)}, f32[440,128]{1,0:T(8,128)S(1)}, u32[]{:S(2)}, u32[]{:S(2)}) %collective-permute-start.5) | collective-permute-done | bytes 225312 | tf_op jit(solution)/shard_map/ppermute | solution.py:377
  92.8 0.0 collective-permute-start.10
  92.8 1.0 dynamic-slice_bitcast_fusion.refs_10_.table_ref
  93.7 0.4 collective-permute-done.6.refs_2_
  94.1 5.7 %collective-permute-done.7.refs_3_ = f32[440,128]{1,0:T(8,128)S(1)} collective-permute-done((f32[440,128]{1,0:T(8,128)}, f32[440,128]{1,0:T(8,128)S(1)}, u32[]{:S(2)}, u32[]{:S(2)}) %collective-permute-start.7) | collective-permute-done | bytes 225312 | tf_op jit(solution)/shard_map/ppermute | solution.py:377
  99.8 0.0 collective-permute-done.8.refs_4_
  99.8 1.3 collective-permute-done.9.refs_5_
  101.1 0.0 collective-permute-done.10.refs_6_
  101.1 0.0 copy-done.7
  101.1 0.9 copy-done
  102.0 3.9 %forward_z.1 = (f32[24,128,128]{2,1,0:T(8,128)S(1)}, f32[3,128,128]{2,1,0:T(8,128)S(1)}, f32[16,24,128]{2,1,0:T(8,128)}) custom-call(f32[440,128]{1,0:T(8,128)S(1)} %collective-permute-done.4.refs_0_, f32[440,128]{1,0:T(8,128)S(1)} %collective-permute-done.5.refs_1_, f32[440,128]{1,0:T(8,128)S(1)} %collective-permute-done.6.refs_2_, ...), custom_call_target="tpu_custom_call" | custom-call | bytes 4030464 | tf_op jit(solution)/shard_map/forward_z/pallas_call | solution.py:37
  105.9 0.7 copy-done.2
  106.6 3.7 %all-to-all-start.1 = ((f32[16,24,128]{2,1,0:T(8,128)}), f32[16,24,128]{2,1,0:T(8,128)S(1)}, u32[]{:S(2)}, u32[]{:S(2)}) async-start(f32[16,24,128]{2,1,0:T(8,128)} %get-tuple-element.48), calls=%async_computation.1 | async-start | bytes 393216 | tf_op jit(solution)/shard_map/all_to_all | solution.py:794
  110.3 0.7 dynamic-slice_bitcast_fusion.1.table_ref
  111.0 6.2 %all-to-all-done.1.back_ref.recv_ref = f32[16,24,128]{2,1,0:T(8,128)S(1)} async-done(((f32[16,24,128]{2,1,0:T(8,128)}), f32[16,24,128]{2,1,0:T(8,128)S(1)}, u32[]{:S(2)}, u32[]{:S(2)}) %all-to-all-start.1) | async-done | bytes 196640 | tf_op jit(solution)/shard_map/all_to_all | solution.py:794
  117.2 0.1 ring.1
  117.3 10.2 %all_to_all.22.small_ref = f32[16,8,128]{2,1,0:T(8,128)S(1)} all-to-all(f32[16,8,128]{2,1,0:T(8,128)S(1)} %ring.1), channel_id=1, replica_groups=mesh['wide'=16,'grp'=8] {'wide'}, dimensions={0} | all-to-all | bytes 131072 | tf_op jit(solution)/shard_map/all_to_all | solution.py:798
  127.4 0.9 copy-done.3
  128.4 3.5 %backward_z.1 = (f32[416,128]{1,0:T(8,128)S(1)}, f32[416,128]{1,0:T(8,128)S(1)}, f32[416,128]{1,0:T(8,128)S(1)}, f32[416,128]{1,0:T(8,128)S(1)}, f32[416,128]{1,...) custom-call(f32[24,128,128]{2,1,0:T(8,128)S(1)} %get-tuple-element.50.coef_ref, ...), custom_call_target="tpu_custom_call" | custom-call | bytes 3801088 | tf_op jit(solution)/shard_map/backward_z/pallas_call | solution.py:37
  131.9 1.4 collective-permute-start.11
  133.3 4.6 %collective-permute-start.12 = (f32[416,128]{1,0:T(8,128)S(1)}, f32[416,128]{1,0:T(8,128)S(1)}, u32[]{:S(2)}, u32[]{:S(2)}) collective-permute-start(f32[416,128]{1,0:T(8,128)S(1)} %get-tuple-element.53), channel_id=1, source_target_pairs={{0,5},{1,4},{2,7},{3,6},{4,1},{5,0},{6,3},{7,2},{8,13},{9,12},{10,... | collective-permute-start | bytes 638984 | tf_op jit(solution)/shard_map/ppermute | solution.py:377
  137.8 0.4 collective-permute-start.13
  138.3 0.0 collective-permute-start.14
  138.3 1.2 collective-permute-start.15
  139.5 0.0 collective-permute-done.11.refs_0_
  139.5 4.0 %collective-permute-start.16 = (f32[416,128]{1,0:T(8,128)S(1)}, f32[416,128]{1,0:T(8,128)S(1)}, u32[]{:S(2)}, u32[]{:S(2)}) collective-permute-start(f32[416,128]{1,0:T(8,128)S(1)} %get-tuple-element.57), channel_id=1, source_target_pairs={{0,7},{1,6},{2,5},{3,4},{4,3},{5,2},{6,1},{7,0},{8,15},{9,14},{10,... | collective-permute-start | bytes 638984 | tf_op jit(solution)/shard_map/ppermute | solution.py:377
  143.5 3.8 %collective-permute-done.12.refs_1_ = f32[416,128]{1,0:T(8,128)S(1)} collective-permute-done((f32[416,128]{1,0:T(8,128)S(1)}, f32[416,128]{1,0:T(8,128)S(1)}, u32[]{:S(2)}, u32[]{:S(2)}) %collective-permute-start.12) | collective-permute-done | bytes 213024 | tf_op jit(solution)/shard_map/ppermute | solution.py:377
  147.3 0.0 collective-permute-start.17
  147.4 1.0 unpack.1
  148.4 0.6 copy-done.4
  149.0 0.0 collective-permute-done.13.refs_2_
  149.0 4.9 %collective-permute-done.14.refs_3_ = f32[416,128]{1,0:T(8,128)S(1)} collective-permute-done((f32[416,128]{1,0:T(8,128)S(1)}, f32[416,128]{1,0:T(8,128)S(1)}, u32[]{:S(2)}, u32[]{:S(2)}) %collective-permute-start.14) | collective-permute-done | bytes 213024 | tf_op jit(solution)/shard_map/ppermute | solution.py:377
  154.0 0.0 collective-permute-done.15.refs_4_
  154.0 1.3 collective-permute-done.16.refs_5_
  155.3 0.0 collective-permute-done.17.refs_6_
  155.3 0.6 copy-done.18
  156.0 0.1 copy-done.19
  156.1 10.5 %last.1 = (f32[3,48,16,512]{3,2,1,0:T(8,128)}, f32[48,16,512]{2,1,0:T(8,128)}) custom-call(f32[12288,128]{1,0:T(8,128)} %get-tuple-element.38.far_ref, f32[128,128]{1,0:T(8,128)} %copy-done.4, bf16[512,512]{1,0:T(8,128)(2,1)} %constant.41.clone.high_ref, bf16[512,512]{1,0:T(8,128)(2,1)} %constant.42.clone.low_ref, f32[416,128]{1,0:T(8,128)} %copy-done.13, ...), custom_call_target="tpu_custom_call" | custom-call | bytes 15400960 | tf_op jit(solution)/shard_map/last/pallas_call | solution.py:37
  (32 shorter events, 0.1 us)
Async XLA Ops:
  5.1 26.8 %collective-permute-start.2 = (f32[4,48,512]{2,1,0:T(8,128)}, f32[4,48,512]{2,1,0:T(8,128)S(1)}, u32[]{:S(2)}, u32[]{:S(2)}) collective-permute-start(f32[4,48,512]{2,1,0:T(8,128)} %get-tuple-element.35), channel_id=1, source_target_pairs={{0,1},{1,2},{2,3},{3,4},{4,5},{5,6},{6,7},{7,0},{8,9},{9,10},{10,1... | collective-permute-start | bytes 1179656 | tf_op jit(solution)/shard_map/ppermute | solution.py:51
  8.2 23.8 %collective-permute-start.3 = (f32[4,48,512]{2,1,0:T(8,128)}, f32[4,48,512]{2,1,0:T(8,128)S(1)}, u32[]{:S(2)}, u32[]{:S(2)}) collective-permute-start(f32[4,48,512]{2,1,0:T(8,128)} %get-tuple-element.36), channel_id=1, source_target_pairs={{0,7},{1,0},{2,1},{3,2},{4,3},{5,4},{6,5},{7,6},{8,15},{9,8},{10,9... | collective-permute-start | bytes 1179656 | tf_op jit(solution)/shard_map/ppermute | solution.py:51
  8.2 23.7 %collective-permute-start = (f32[4,16,512]{2,1,0:T(8,128)}, f32[4,16,512]{2,1,0:T(8,128)S(1)}, u32[]{:S(2)}, u32[]{:S(2)}) collective-permute-start(f32[4,16,512]{2,1,0:T(8,128)} %get-tuple-element.33), channel_id=1, source_target_pairs={{0,8},{8,16},{16,24},{24,32},{32,40},{40,48},{48,56},{56,64},{64,7... | collective-permute-start | bytes 393224 | tf_op jit(solution)/shard_map/ppermute | solution.py:51
  9.5 22.4 %collective-permute-start.1 = (f32[4,16,512]{2,1,0:T(8,128)}, f32[4,16,512]{2,1,0:T(8,128)S(1)}, u32[]{:S(2)}, u32[]{:S(2)}) collective-permute-start(f32[4,16,512]{2,1,0:T(8,128)} %get-tuple-element.34), channel_id=1, source_target_pairs={{0,120},{8,0},{16,8},{24,16},{32,24},{40,32},{48,40},{56,48},{64,5... | collective-permute-start | bytes 393224 | tf_op jit(solution)/shard_map/ppermute | solution.py:51
  31.9 0.7 copy-start.20
  31.9 0.7 copy-start.21
  31.9 0.8 copy-start.11
  31.9 0.9 copy-start.12
  32.9 68.2 %copy-start.7 = (bf16[128,128]{1,0:T(8,128)(2,1)S(1)}, bf16[128,128]{1,0:T(8,128)(2,1)}, u32[]{:S(2)}) copy-start(bf16[128,128]{1,0:T(8,128)(2,1)} %constant.44.clone.refs_9_) | copy-start | bytes 98308
  32.9 68.2 %copy-start.8 = (bf16[128,128]{1,0:T(8,128)(2,1)S(1)}, bf16[128,128]{1,0:T(8,128)(2,1)}, u32[]{:S(2)}) copy-start(bf16[128,128]{1,0:T(8,128)(2,1)} %constant.43.clone.refs_8_) | copy-start | bytes 98308
  77.4 7.8 %collective-permute-start.4 = (f32[440,128]{1,0:T(8,128)}, f32[440,128]{1,0:T(8,128)S(1)}, u32[]{:S(2)}, u32[]{:S(2)}) collective-permute-start(f32[440,128]{1,0:T(8,128)} %get-tuple-element.40), channel_id=1, source_target_pairs={{0,4},{1,5},{2,6},{3,7},{4,0},{5,1},{6,2},{7,3},{8,12},{9,13},{10,... | collective-permute-start | bytes 675848 | tf_op jit(solution)/shard_map/ppermute | solution.py:377
  78.7 14.1 %collective-permute-start.5 = (f32[440,128]{1,0:T(8,128)}, f32[440,128]{1,0:T(8,128)S(1)}, u32[]{:S(2)}, u32[]{:S(2)}) collective-permute-start(f32[440,128]{1,0:T(8,128)} %get-tuple-element.41), channel_id=1, source_target_pairs={{0,5},{1,4},{2,7},{3,6},{4,1},{5,0},{6,3},{7,2},{8,13},{9,12},{10,... | collective-permute-start | bytes 675848 | tf_op jit(solution)/shard_map/ppermute | solution.py:377
  81.6 12.5 %collective-permute-start.6 = (f32[440,128]{1,0:T(8,128)}, f32[440,128]{1,0:T(8,128)S(1)}, u32[]{:S(2)}, u32[]{:S(2)}) collective-permute-start(f32[440,128]{1,0:T(8,128)} %get-tuple-element.42), channel_id=1, source_target_pairs={{0,2},{1,3},{2,0},{3,1},{4,6},{5,7},{6,4},{7,5},{8,10},{9,11},{10,... | collective-permute-start | bytes 675848 | tf_op jit(solution)/shard_map/ppermute | solution.py:377
  81.7 18.1 %collective-permute-start.7 = (f32[440,128]{1,0:T(8,128)}, f32[440,128]{1,0:T(8,128)S(1)}, u32[]{:S(2)}, u32[]{:S(2)}) collective-permute-start(f32[440,128]{1,0:T(8,128)} %get-tuple-element.43), channel_id=1, source_target_pairs={{0,3},{1,2},{2,1},{3,0},{4,7},{5,6},{6,5},{7,4},{8,11},{9,10},{10,... | collective-permute-start | bytes 675848 | tf_op jit(solution)/shard_map/ppermute | solution.py:377
  82.4 17.3 %collective-permute-start.8 = (f32[440,128]{1,0:T(8,128)}, f32[440,128]{1,0:T(8,128)S(1)}, u32[]{:S(2)}, u32[]{:S(2)}) collective-permute-start(f32[440,128]{1,0:T(8,128)} %get-tuple-element.44), channel_id=1, source_target_pairs={{0,6},{1,7},{2,4},{3,5},{4,2},{5,3},{6,0},{7,1},{8,14},{9,15},{10,... | collective-permute-start | bytes 675848 | tf_op jit(solution)/shard_map/ppermute | solution.py:377
  85.2 15.9 %collective-permute-start.9 = (f32[440,128]{1,0:T(8,128)}, f32[440,128]{1,0:T(8,128)S(1)}, u32[]{:S(2)}, u32[]{:S(2)}) collective-permute-start(f32[440,128]{1,0:T(8,128)} %get-tuple-element.45), channel_id=1, source_target_pairs={{0,7},{1,6},{2,5},{3,4},{4,3},{5,2},{6,1},{7,0},{8,15},{9,14},{10,... | collective-permute-start | bytes 675848 | tf_op jit(solution)/shard_map/ppermute | solution.py:377
  92.8 8.3 %collective-permute-start.10 = (f32[440,128]{1,0:T(8,128)}, f32[440,128]{1,0:T(8,128)S(1)}, u32[]{:S(2)}, u32[]{:S(2)}) collective-permute-start(f32[440,128]{1,0:T(8,128)} %get-tuple-element.46), channel_id=1, source_target_pairs={{0,1},{1,0},{2,3},{3,2},{4,5},{5,4},{6,7},{7,6},{8,9},{9,8},{10,11... | collective-permute-start | bytes 675848 | tf_op jit(solution)/shard_map/ppermute | solution.py:377
  92.8 34.7 %copy-start.5 = (bf16[128,128]{1,0:T(8,128)(2,1)S(1)}, bf16[128,128]{1,0:T(8,128)(2,1)}, u32[]{:S(2)}) copy-start(bf16[128,128]{1,0:T(8,128)(2,1)} %constant.46.clone.low_ref) | copy-start | bytes 98308
  92.8 34.7 %copy-start.6 = (bf16[128,128]{1,0:T(8,128)(2,1)S(1)}, bf16[128,128]{1,0:T(8,128)(2,1)}, u32[]{:S(2)}) copy-start(bf16[128,128]{1,0:T(8,128)(2,1)} %constant.45.clone.high_ref) | copy-start | bytes 98308
  101.1 0.9 copy-start
  105.9 0.7 copy-start.2
  106.6 40.8 %copy-start.9 = (s32[1024]{0:T(1024)S(1)}, s32[1024]{0:T(1024)}, u32[]{:S(2)}) copy-start(s32[1024]{0:T(1024)} %param.19) | copy-start | bytes 12292
  106.6 40.8 %copy-start.10 = (s32[1,1024]{1,0:T(1,128)S(1)}, s32[1,1024]{1,0:T(1,128)}, u32[]{:S(2)}) copy-start(s32[1,1024]{1,0:T(1,128)} %get-tuple-element.39.rank_ref) | copy-start | bytes 12292
  106.6 10.6 %all-to-all-start.1 = ((f32[16,24,128]{2,1,0:T(8,128)}), f32[16,24,128]{2,1,0:T(8,128)S(1)}, u32[]{:S(2)}, u32[]{:S(2)}) async-start(f32[16,24,128]{2,1,0:T(8,128)} %get-tuple-element.48), calls=%async_computation.1 | async-start | bytes 393216 | tf_op jit(solution)/shard_map/all_to_all | solution.py:794
  127.4 0.9 copy-start.3
  131.9 16.5 %copy-start.1 = (f32[416,128]{1,0:T(8,128)}, f32[416,128]{1,0:T(8,128)S(1)}, u32[]{:S(2)}) copy-start(f32[416,128]{1,0:T(8,128)S(1)} %get-tuple-element.59.refs_7_) | copy-start | bytes 638980
  131.9 7.6 %collective-permute-start.11 = (f32[416,128]{1,0:T(8,128)S(1)}, f32[416,128]{1,0:T(8,128)S(1)}, u32[]{:S(2)}, u32[]{:S(2)}) collective-permute-start(f32[416,128]{1,0:T(8,128)S(1)} %get-tuple-element.52), channel_id=1, source_target_pairs={{0,4},{1,5},{2,6},{3,7},{4,0},{5,1},{6,2},{7,3},{8,12},{9,13},{10,... | collective-permute-start | bytes 638984 | tf_op jit(solution)/shard_map/ppermute | solution.py:377
  133.3 14.1 %collective-permute-start.12 = (f32[416,128]{1,0:T(8,128)S(1)}, f32[416,128]{1,0:T(8,128)S(1)}, u32[]{:S(2)}, u32[]{:S(2)}) collective-permute-start(f32[416,128]{1,0:T(8,128)S(1)} %get-tuple-element.53), channel_id=1, source_target_pairs={{0,5},{1,4},{2,7},{3,6},{4,1},{5,0},{6,3},{7,2},{8,13},{9,12},{10,... | collective-permute-start | bytes 638984 | tf_op jit(solution)/shard_map/ppermute | solution.py:377
  137.8 11.2 %collective-permute-start.13 = (f32[416,128]{1,0:T(8,128)S(1)}, f32[416,128]{1,0:T(8,128)S(1)}, u32[]{:S(2)}, u32[]{:S(2)}) collective-permute-start(f32[416,128]{1,0:T(8,128)S(1)} %get-tuple-element.54), channel_id=1, source_target_pairs={{0,2},{1,3},{2,0},{3,1},{4,6},{5,7},{6,4},{7,5},{8,10},{9,11},{10,... | collective-permute-start | bytes 638984 | tf_op jit(solution)/shard_map/ppermute | solution.py:377
  138.3 15.7 %collective-permute-start.14 = (f32[416,128]{1,0:T(8,128)S(1)}, f32[416,128]{1,0:T(8,128)S(1)}, u32[]{:S(2)}, u32[]{:S(2)}) collective-permute-start(f32[416,128]{1,0:T(8,128)S(1)} %get-tuple-element.55), channel_id=1, source_target_pairs={{0,3},{1,2},{2,1},{3,0},{4,7},{5,6},{6,5},{7,4},{8,11},{9,10},{10,... | collective-permute-start | bytes 638984 | tf_op jit(solution)/shard_map/ppermute | solution.py:377
  138.3 15.7 %collective-permute-start.15 = (f32[416,128]{1,0:T(8,128)S(1)}, f32[416,128]{1,0:T(8,128)S(1)}, u32[]{:S(2)}, u32[]{:S(2)}) collective-permute-start(f32[416,128]{1,0:T(8,128)S(1)} %get-tuple-element.56), channel_id=1, source_target_pairs={{0,6},{1,7},{2,4},{3,5},{4,2},{5,3},{6,0},{7,1},{8,14},{9,15},{10,... | collective-permute-start | bytes 638984 | tf_op jit(solution)/shard_map/ppermute | solution.py:377
  139.5 15.8 %copy-start.13 = (f32[416,128]{1,0:T(8,128)}, f32[416,128]{1,0:T(8,128)S(1)}, u32[]{:S(2)}) copy-start(f32[416,128]{1,0:T(8,128)S(1)} %collective-permute-done.11.refs_0_) | copy-start | bytes 638980
  139.5 15.8 %collective-permute-start.16 = (f32[416,128]{1,0:T(8,128)S(1)}, f32[416,128]{1,0:T(8,128)S(1)}, u32[]{:S(2)}, u32[]{:S(2)}) collective-permute-start(f32[416,128]{1,0:T(8,128)S(1)} %get-tuple-element.57), channel_id=1, source_target_pairs={{0,7},{1,6},{2,5},{3,4},{4,3},{5,2},{6,1},{7,0},{8,15},{9,14},{10,... | collective-permute-start | bytes 638984 | tf_op jit(solution)/shard_map/ppermute | solution.py:377
  147.3 7.9 %copy-start.14 = (f32[416,128]{1,0:T(8,128)}, f32[416,128]{1,0:T(8,128)S(1)}, u32[]{:S(2)}) copy-start(f32[416,128]{1,0:T(8,128)S(1)} %collective-permute-done.12.refs_1_) | copy-start | bytes 638980
  147.3 7.9 %collective-permute-start.17 = (f32[416,128]{1,0:T(8,128)S(1)}, f32[416,128]{1,0:T(8,128)S(1)}, u32[]{:S(2)}, u32[]{:S(2)}) collective-permute-start(f32[416,128]{1,0:T(8,128)S(1)} %get-tuple-element.58), channel_id=1, source_target_pairs={{0,1},{1,0},{2,3},{3,2},{4,5},{5,4},{6,7},{7,6},{8,9},{9,8},{10,11... | collective-permute-start | bytes 638984 | tf_op jit(solution)/shard_map/ppermute | solution.py:377
  148.4 0.6 copy-start.4
  149.0 6.3 %copy-start.15 = (f32[416,128]{1,0:T(8,128)}, f32[416,128]{1,0:T(8,128)S(1)}, u32[]{:S(2)}) copy-start(f32[416,128]{1,0:T(8,128)S(1)} %collective-permute-done.13.refs_2_) | copy-start | bytes 638980
  154.0 1.3 copy-start.16
  154.0 1.3 copy-start.17
  155.3 0.7 copy-start.18
  155.3 0.8 copy-start.19

commit v3 on v2

--- a/solution.py
+++ b/solution.py
@@ -44,6 +44,15 @@
         cost_estimate=pl.CostEstimate(flops=0, bytes_accessed=moved, transcendentals=0),
         name=name,
     )(*args)
+
+
+def loop(low, high, body, init, by):
+    def several(turn, carry):
+        for i in range(by):
+            carry = body(low + turn * by + i, carry)
+        return carry
+
+    return lax.fori_loop(0, (high - low) // by, several, init)
 
 
 def passed_along(value, axis, steps):
@@ -131,7 +140,7 @@
             out[3, pl.ds(y, 1), :] = scal_ref[y, z : z + 1, :]
         return carry
 
-    lax.fori_loop(0, rows_y, edges, 0)
+    loop(0, rows_y, edges, 0, 4)
     for y, out in ((0, y_first), (rows_y - 1, y_last)):
         for f in range(3):
             out[f] = vel_ref[f, y]
@@ -205,7 +214,7 @@
     return out
 
 
-def marker_part(recv_ref, out_ref, force_ref, samp, table, index, sem, tiles_x, depth_z):
+def marker_part(recv_ref, star_ref, out_ref, force_ref, samp, table, index, sem, tiles_x, depth_z):
     sources = recv_ref.shape[0]
     wide_lane = iota((sources, lanes), 1)
     second = recv_ref[:, lanes : 2 * lanes]
@@ -231,45 +240,57 @@
     def at(place):
         return pl.ds(pl.multiple_of(place, 4), 4)
 
-    def gather(batch, carry):
-        found = jnp.zeros((4, lanes), f32)
-        for q in range(4):
-            for r in range(slots):
-                source = 4 * batch + q
-                value = out_ref[at(index[source, r]), :]
-                value = pltpu.roll(value, index[source, 32 + r], 1)
-                found = jnp.where(lane == 32 * q + r, value, found)
-        samp[pl.ds(pl.multiple_of(4 * batch, 4), 4), :] = found
-        return carry
-
-    lax.fori_loop(0, sources // 4, gather, 0)
     eta = jnp.where(wide_lane < 32, second, 0.0)
     eta = eta + pltpu.roll(eta, 32, 1)
     eta = eta + pltpu.roll(eta, 64, 1)
-    force = swap_groups(eta) * (swap_groups(recv_ref[:, 0:lanes]) - samp[...])
-    samp[...] = force
-    force_ref[...] = swap_groups(force)
-
-    def scatter(batch, carry):
-        mine = samp[pl.ds(pl.multiple_of(4 * batch, 4), 4), :]
-        for sub in range(4):
-            source = 4 * batch + sub
-            terms = []
-            for r in range(slots):
-                only = jnp.where(lane == 32 * sub + r, mine, 0.0)
-                terms.append(pltpu.roll(only, index[source, 64 + r], 1))
-            for q in range(0, slots, 4):
-                places = [index[source, q + j] for j in range(4)]
-                values = [out_ref[at(place), :] for place in places]
-                for j in range(4):
-                    for i in range(j):
-                        values[j] = jnp.where(places[i] == places[j], values[i], values[j])
-                    values[j] = values[j] + terms[q + j]
-                for j in range(4):
-                    out_ref[at(places[j]), :] = values[j]
-        return carry
-
-    lax.fori_loop(0, sources // 4, scatter, 0)
+    force_ref[...] = swap_groups(eta)
+    samp[...] = swap_groups(recv_ref[:, 0:lanes])
+
+    def rows_of(batch):
+        return pl.ds(pl.multiple_of(4 * batch, 4), 4)
+
+    def look(source, q, r, found):
+        value = star_ref[at(index[source, r]), :]
+        value = pltpu.roll(value, index[source, 32 + r], 1)
+        return jnp.where(lane == 32 * q + r, value, found)
+
+    def force_of(batch, found):
+        force = force_ref[rows_of(batch), :] * (samp[rows_of(batch), :] - found)
+        samp[rows_of(batch), :] = force
+        return force
+
+    def add(source, q, first, mine):
+        places = [index[source, first + j] for j in range(2)]
+        values = [out_ref[at(place), :] for place in places]
+        terms = []
+        for j in range(2):
+            only = jnp.where(lane == 32 * q + first + j, mine, 0.0)
+            terms.append(pltpu.roll(only, index[source, 64 + first + j], 1))
+        values[0] = values[0] + terms[0]
+        values[1] = jnp.where(places[0] == places[1], values[0], values[1]) + terms[1]
+        for j in range(2):
+            out_ref[at(places[j]), :] = values[j]
+
+    def both(batch, mine):
+        found = jnp.zeros((4, lanes), f32)
+        for q in range(4):
+            source = 4 * batch + q
+            for first in range(0, slots, 4):
+                for r in range(first, first + 4):
+                    found = look(source, q, r, found)
+                for r in (first, first + 2):
+                    add(source - 4, q, r, mine)
+        return force_of(batch, found)
+
+    found = jnp.zeros((4, lanes), f32)
+    for q in range(4):
+        for r in range(slots):
+            found = look(q, q, r, found)
+    mine = lax.fori_loop(1, sources // 4, both, force_of(0, found))
+    for q in range(4):
+        for r in range(0, slots, 2):
+            add(sources - 4 + q, q, r, mine)
+    force_ref[...] = swap_groups(samp[...])
 
 
 def at_row(y, x, f, tiles_x, depth_z):
@@ -277,7 +298,7 @@
 
 
 def stencil_part(
-    vel_far, scal_far, ylo_ref, yhi_ref, zlo_ref, zhi_ref, vel_ref, scal_ref, out_ref, sems
+    vel_far, scal_far, ylo_ref, yhi_ref, zlo_ref, zhi_ref, vel_ref, scal_ref, out_ref, same_ref, sems
 ):
     _, rows_y, depth_z, length_x = vel_ref.shape
     tiles_x = length_x // lanes
@@ -315,7 +336,9 @@
                 - (0.5 * time_step) * transport
             )
             for x in range(tiles_x):
-                out_ref[at_row(y, x, f, tiles_x, depth_z), :] = star[:, x * lanes : (x + 1) * lanes]
+                place = at_row(y, x, f, tiles_x, depth_z)
+                out_ref[place, :] = star[:, x * lanes : (x + 1) * lanes]
+                same_ref[place, :] = star[:, x * lanes : (x + 1) * lanes]
         return carry
 
     pieces = sems.shape[0] // 2
@@ -412,22 +435,24 @@
         sums[pl.ds(y, 1), :] = jnp.sum(folded, axis=0, keepdims=True)
         return carry
 
-    lax.fori_loop(0, rows_y, one_row, 0)
+    loop(0, rows_y, one_row, 0, 2)
     div[rows : rows + depth_z, :] = wide_row(forced_ref, 1, 0, tiles_x, depth_z)
 
 
 def first_body(shape, *refs):
     vel_far, scal_far, ylo, yhi, zlo, zhi, recv_ref, high_ref, low_ref, far_ref, *rest = refs
-    out_refs, rest = rest[:-13], rest[-13:]
-    vel_ref, scal_ref, sems, forced_ref, out_ref, *rest = rest
+    out_refs, rest = rest[:-14], rest[-14:]
+    vel_ref, scal_ref, sems, star_ref, forced_ref, out_ref, *rest = rest
     force, samp, table, div, modes, index, sem, far_sem = rest
     rows_y, depth_z, length_x = shape
     n_grp = out_ref.shape[0]
     n_wide = recv_ref.shape[0] // n_grp
     rows = rows_y * depth_z
     tiles_x = length_x // lanes
-    stencil_part(vel_far, scal_far, ylo, yhi, zlo, zhi, vel_ref, scal_ref, forced_ref, sems)
-    marker_part(recv_ref, forced_ref, force, samp, table, index, sem, tiles_x, depth_z)
+    stencil_part(
+        vel_far, scal_far, ylo, yhi, zlo, zhi, vel_ref, scal_ref, forced_ref, star_ref, sems
+    )
+    marker_part(recv_ref, star_ref, forced_ref, force, samp, table, index, sem, tiles_x, depth_z)
     keep = pltpu.make_async_copy(forced_ref, far_ref, far_sem)
     keep.start()
     divergence_part(forced_ref, div, samp, (rows_y, depth_z, length_x))
@@ -451,7 +476,7 @@
         send(front, back, depth_z, front)
         return carry
 
-    lax.fori_loop(0, rows_y // 2, shuffle, 0)
+    loop(0, rows_y // 2, shuffle, 0, 4)
     send(rows, rows + depth_z // 2, depth_z // 2, row)
     send(rows + depth_z, rows + depth_z + rows_y // 2, rows_y // 2, plane)
     total = jnp.broadcast_to(jnp.sum(samp[...].T, axis=0, keepdims=True), (end - sums_row, lanes))
@@ -499,12 +524,13 @@
     extra = jnp.concatenate([packed, other], axis=1).reshape(full_z, lanes)
     extra = jnp.where(first_half, times_z(extra, high_ref, low_ref), 0.0)
     ends_ref[2] = extra
-    up = lax.fori_loop(0, steps // 2, one_pair, extra)
-    down = lax.fori_loop(
+    up = loop(0, steps // 2, one_pair, extra, 3)
+    down = loop(
         0,
         steps,
         lambda i, total: coef_ref[steps - 1 - i] + root * total,
         jnp.zeros((full_z, lanes), f32),
+        2,
     )
     down = root * down
     ends_ref[0] = up
@@ -568,7 +594,7 @@
         ups[step] = total
         return total
 
-    lax.fori_loop(0, steps, rising, up_start)
+    loop(0, steps, rising, up_start, 2)
 
     def falling(i, total):
         pair = steps // 2 - 1 - i
@@ -587,7 +613,7 @@
                 out_ref[g, pl.ds(plane + step, 1), :] = value[before : before + 1, :]
         return total
 
-    down = lax.fori_loop(0, steps // 2, falling, down)
+    down = loop(0, steps // 2, falling, down, 3)
     extra = times_z(gain * (up_start + down), high_ref, low_ref)
     half = depth_z // 2
     for g in range(n_grp):
@@ -627,7 +653,7 @@
         take(front, back, depth_z, front)
         return carry
 
-    lax.fori_loop(0, rows_y // 2, shuffle, 0)
+    loop(0, rows_y // 2, shuffle, 0, 4)
     take(rows, rows + depth_z // 2, depth_z // 2, row)
     take(rows + depth_z, rows + depth_z + rows_y // 2, rows_y // 2, plane)
     chunk = modes.shape[0] // 4
@@ -658,7 +684,7 @@
     size = rows_y // pieces
     copies = []
     for piece in range(pieces):
-        lax.fori_loop(piece * size, (piece + 1) * size, one_row, 0)
+        loop(piece * size, (piece + 1) * size, one_row, 0, 2)
         part = pl.ds(piece * size, size)
         copies += [
             pltpu.make_async_copy(
@@ -760,6 +786,7 @@
             pltpu.VMEM(scalar.shape, f32),
             pltpu.SemaphoreType.DMA((8,)),
             pltpu.VMEM((flat, lanes), f32),
+            pltpu.VMEM((flat, lanes), f32),
             pltpu.VMEM((n_grp, sent_rows, lanes), f32),
             pltpu.VMEM((owners, lanes), f32),
             pltpu.VMEM((owners, lanes), f32),

time: 167 us -> 154 us (0.922)
  Pallas kernels: 68 us -> 55.3 us
    pallas_call x7, Pallas kernels: 68 us -> 55.3 us  [call(): pl.pallas_call(body, out_shape=shapes, in_specs=[hbm if i in far_in else...]
where the time goes in v3:
time: 154 us
  Pallas kernels  55.3 us (36%)
  starting transfers between devices  32.9 us (21%)
  waiting for transfers between devices  29.3 us (19%)
  blocking collectives  27.3 us (18%)
  local copies, waits for them, and re-layouts  8.23 us (5%)
    pallas_call x7, Pallas kernels, call(): pl.pallas_call(body, out_shape=shapes, in_specs=[hbm if i in far_in else...  55.3 us
    ppermute x14, waiting for transfers between devices, exchanged(): lax.ppermute(part, 'grp', [(i, i ^ d) for i in range(count)])  23.1 us
    ppermute x14, starting transfers between devices, exchanged(): lax.ppermute(part, 'grp', [(i, i ^ d) for i in range(count)])  21.3 us
    all_to_all x1, blocking collectives, per_device(): lax.all_to_all(send, ('wide', 'grp'), split_axis=0, concat_axis=0, tiled=...  17.1 us
    all_to_all x1, blocking collectives, per_device(): lax.all_to_all(reach, 'wide', split_axis=0, concat_axis=0, tiled=True)  10.2 us
    ppermute x4, starting transfers between devices, passed_along(): lax.ppermute(value, axis, [(i, (i + steps) % count) for i in range(count)])  7.97 us
    all_to_all x1, waiting for transfers between devices, per_device(): lax.all_to_all(small, 'wide', split_axis=0, concat_axis=0, tiled=True)  6.21 us
    unnamed x45, local copies, waits for them, and re-layouts  5.53 us
  transfers between devices with their start and end apart: 19, of which 9 were waited for; matrix products, arithmetic and copies ran while one was open for 2% of the time, Pallas kernels for 1%

profile of v3, /device:TPU:1, one launch (start us, length us, event | category | flops | bytes accessed | tf_op | source)
XLA Modules:
  0.0 153.9 jit_solution(7222730180895733609)
XLA Ops:
  0.6 4.3 %pack.1 = (f32[128,256]{1,0:T(8,128)}, s32[1,1024]{1,0:T(1,128)}, f32[4,16,512]{2,1,0:T(8,128)}, f32[4,16,512]{2,1,0:T(8,128)}, f32[4,48,512]{2,1,0:T(8,128)}, /*index=5*/f32[4,48,512]{2,1,0:T(8,128)}) custom-call(s32[1,1024]{1,0:T(1,128)} %bitcast.12, s32[1,1024]{1,0:T(1,128)} %bitcast.16, s32[1,1024]{1,0:T(1,128)} %bitcast.17, f32[4,1024]{1,0:T(4,128)} %refs_3_.1, ...), custom_call_target="tpu_custom_call" | custom-call | bytes 7507968 | tf_op jit(solution)/shard_map/pack/pallas_call | solution.py:37
  4.9 3.0 %collective-permute-start.2 = (f32[4,48,512]{2,1,0:T(8,128)}, f32[4,48,512]{2,1,0:T(8,128)S(1)}, u32[]{:S(2)}, u32[]{:S(2)}) collective-permute-start(f32[4,48,512]{2,1,0:T(8,128)} %get-tuple-element.35), channel_id=1, source_target_pairs={{0,1},{1,2},{2,3},{3,4},{4,5},{5,6},{6,7},{7,0},{8,9},{9,10},{10,1... | collective-permute-start | bytes 1179656 | tf_op jit(solution)/shard_map/ppermute | solution.py:60
  8.0 0.0 collective-permute-start.3
  8.0 1.3 collective-permute-start
  9.3 3.6 %collective-permute-start.1 = (f32[4,16,512]{2,1,0:T(8,128)}, f32[4,16,512]{2,1,0:T(8,128)S(1)}, u32[]{:S(2)}, u32[]{:S(2)}) collective-permute-start(f32[4,16,512]{2,1,0:T(8,128)} %get-tuple-element.34), channel_id=1, source_target_pairs={{0,120},{8,0},{16,8},{24,16},{32,24},{40,32},{48,40},{56,48},{64,5... | collective-permute-start | bytes 393224 | tf_op jit(solution)/shard_map/ppermute | solution.py:60
  12.9 1.0 copy.20
  13.9 17.1 %all_to_all.21 = f32[128,1,256]{2,1,0:T(1,128)S(1)} all-to-all(f32[128,1,256]{2,1,0:T(1,128)S(1)} %copy.20), channel_id=1, replica_groups=mesh['wide'=16,'grp'=8] {'wide','grp'}, dimensions={0} | all-to-all | bytes 262144 | tf_op jit(solution)/shard_map/all_to_all | solution.py:775
  31.0 0.7 copy.23
  31.7 0.0 collective-permute-done.refs_2_
  31.7 0.0 collective-permute-done.1.refs_3_
  31.7 0.0 collective-permute-done.2.refs_4_
  31.7 0.0 copy-start.11
  31.7 0.0 collective-permute-done.3.refs_5_
  31.7 0.0 copy-start.12
  31.7 0.6 copy-done.20
  32.3 0.1 copy-done.21
  32.4 0.1 copy-done.11
  32.5 0.1 copy-done.12
  32.7 37.1 %first.1 = (f32[12288,128]{1,0:T(8,128)}, f32[440,128]{1,0:T(8,128)}, f32[440,128]{1,0:T(8,128)}, f32[440,128]{1,0:T(8,128)}, f32[440,128]{1,0:T(8,128)}, /*inde...) custom-call(f32[3,48,16,512]{3,2,1,0:T(8,128)} %refs_0_.1, ...), custom_call_target="tpu_custom_call" | custom-call | bytes 120000000 | tf_op jit(solution)/shard_map/first/pallas_call | solution.py:37
  69.7 1.3 collective-permute-start.4
  71.0 2.9 %collective-permute-start.5 = (f32[440,128]{1,0:T(8,128)}, f32[440,128]{1,0:T(8,128)S(1)}, u32[]{:S(2)}, u32[]{:S(2)}) collective-permute-start(f32[440,128]{1,0:T(8,128)} %get-tuple-element.41), channel_id=1, source_target_pairs={{0,5},{1,4},{2,7},{3,6},{4,1},{5,0},{6,3},{7,2},{8,13},{9,12},{10,... | collective-permute-start | bytes 675848 | tf_op jit(solution)/shard_map/ppermute | solution.py:400
  74.0 0.1 collective-permute-start.6
  74.0 0.8 collective-permute-start.7
  74.8 0.9 collective-permute-start.8
  75.8 1.8 %collective-permute-done.4.refs_0_ = f32[440,128]{1,0:T(8,128)S(1)} collective-permute-done((f32[440,128]{1,0:T(8,128)}, f32[440,128]{1,0:T(8,128)S(1)}, u32[]{:S(2)}, u32[]{:S(2)}) %collective-permute-start.4) | collective-permute-done | bytes 225312 | tf_op jit(solution)/shard_map/ppermute | solution.py:400
  77.6 3.7 %collective-permute-start.9 = (f32[440,128]{1,0:T(8,128)}, f32[440,128]{1,0:T(8,128)S(1)}, u32[]{:S(2)}, u32[]{:S(2)}) collective-permute-start(f32[440,128]{1,0:T(8,128)} %get-tuple-element.45), channel_id=1, source_target_pairs={{0,7},{1,6},{2,5},{3,4},{4,3},{5,2},{6,1},{7,0},{8,15},{9,14},{10,... | collective-permute-start | bytes 675848 | tf_op jit(solution)/shard_map/ppermute | solution.py:400
  81.2 3.9 %collective-permute-done.5.refs_1_ = f32[440,128]{1,0:T(8,128)S(1)} collective-permute-done((f32[440,128]{1,0:T(8,128)}, f32[440,128]{1,0:T(8,128)S(1)}, u32[]{:S(2)}, u32[]{:S(2)}) %collective-permute-start.5) | collective-permute-done | bytes 225312 | tf_op jit(solution)/shard_map/ppermute | solution.py:400
  85.2 0.0 collective-permute-start.10
  85.2 1.0 dynamic-slice_bitcast_fusion.refs_10_.table_ref
  86.1 0.4 collective-permute-done.6.refs_2_
  86.5 5.7 %collective-permute-done.7.refs_3_ = f32[440,128]{1,0:T(8,128)S(1)} collective-permute-done((f32[440,128]{1,0:T(8,128)}, f32[440,128]{1,0:T(8,128)S(1)}, u32[]{:S(2)}, u32[]{:S(2)}) %collective-permute-start.7) | collective-permute-done | bytes 225312 | tf_op jit(solution)/shard_map/ppermute | solution.py:400
  92.1 0.0 collective-permute-done.8.refs_4_
  92.2 1.3 collective-permute-done.9.refs_5_
  93.5 0.0 collective-permute-done.10.refs_6_
  93.5 0.0 copy-done.7
  93.5 0.9 copy-done
  94.4 2.7 %forward_z.1 = (f32[24,128,128]{2,1,0:T(8,128)S(1)}, f32[3,128,128]{2,1,0:T(8,128)S(1)}, f32[16,24,128]{2,1,0:T(8,128)}) custom-call(f32[440,128]{1,0:T(8,128)S(1)} %collective-permute-done.4.refs_0_, f32[440,128]{1,0:T(8,128)S(1)} %collective-permute-done.5.refs_1_, f32[440,128]{1,0:T(8,128)S(1)} %collective-permute-done.6.refs_2_, ...), custom_call_target="tpu_custom_call" | custom-call | bytes 4030464 | tf_op jit(solution)/shard_map/forward_z/pallas_call | solution.py:37
  97.1 0.7 copy-done.2
  97.8 3.7 %all-to-all-start.1 = ((f32[16,24,128]{2,1,0:T(8,128)}), f32[16,24,128]{2,1,0:T(8,128)S(1)}, u32[]{:S(2)}, u32[]{:S(2)}) async-start(f32[16,24,128]{2,1,0:T(8,128)} %get-tuple-element.48), calls=%async_computation.1 | async-start | bytes 393216 | tf_op jit(solution)/shard_map/all_to_all | solution.py:821
  101.4 0.7 dynamic-slice_bitcast_fusion.1.table_ref
  102.1 6.2 %all-to-all-done.1.back_ref.recv_ref = f32[16,24,128]{2,1,0:T(8,128)S(1)} async-done(((f32[16,24,128]{2,1,0:T(8,128)}), f32[16,24,128]{2,1,0:T(8,128)S(1)}, u32[]{:S(2)}, u32[]{:S(2)}) %all-to-all-start.1) | async-done | bytes 196640 | tf_op jit(solution)/shard_map/all_to_all | solution.py:821
  108.3 0.1 ring.1
  108.4 10.2 %all_to_all.22.small_ref = f32[16,8,128]{2,1,0:T(8,128)S(1)} all-to-all(f32[16,8,128]{2,1,0:T(8,128)S(1)} %ring.1), channel_id=1, replica_groups=mesh['wide'=16,'grp'=8] {'wide'}, dimensions={0} | all-to-all | bytes 131072 | tf_op jit(solution)/shard_map/all_to_all | solution.py:825
  118.6 0.9 copy-done.3
  119.5 2.2 %backward_z.1 = (f32[416,128]{1,0:T(8,128)S(1)}, f32[416,128]{1,0:T(8,128)S(1)}, f32[416,128]{1,0:T(8,128)S(1)}, f32[416,128]{1,0:T(8,128)S(1)}, f32[416,128]{1,...) custom-call(f32[24,128,128]{2,1,0:T(8,128)S(1)} %get-tuple-element.50.coef_ref, ...), custom_call_target="tpu_custom_call" | custom-call | bytes 3801088 | tf_op jit(solution)/shard_map/backward_z/pallas_call | solution.py:37
  121.8 1.4 collective-permute-start.11
  123.1 4.6 %collective-permute-start.12 = (f32[416,128]{1,0:T(8,128)S(1)}, f32[416,128]{1,0:T(8,128)S(1)}, u32[]{:S(2)}, u32[]{:S(2)}) collective-permute-start(f32[416,128]{1,0:T(8,128)S(1)} %get-tuple-element.53), channel_id=1, source_target_pairs={{0,5},{1,4},{2,7},{3,6},{4,1},{5,0},{6,3},{7,2},{8,13},{9,12},{10,... | collective-permute-start | bytes 638984 | tf_op jit(solution)/shard_map/ppermute | solution.py:400
  127.7 0.4 collective-permute-start.13
  128.1 0.0 collective-permute-start.14
  128.1 1.2 collective-permute-start.15
  129.3 0.0 collective-permute-done.11.refs_0_
  129.3 4.0 %collective-permute-start.16 = (f32[416,128]{1,0:T(8,128)S(1)}, f32[416,128]{1,0:T(8,128)S(1)}, u32[]{:S(2)}, u32[]{:S(2)}) collective-permute-start(f32[416,128]{1,0:T(8,128)S(1)} %get-tuple-element.57), channel_id=1, source_target_pairs={{0,7},{1,6},{2,5},{3,4},{4,3},{5,2},{6,1},{7,0},{8,15},{9,14},{10,... | collective-permute-start | bytes 638984 | tf_op jit(solution)/shard_map/ppermute | solution.py:400
  133.4 3.8 %collective-permute-done.12.refs_1_ = f32[416,128]{1,0:T(8,128)S(1)} collective-permute-done((f32[416,128]{1,0:T(8,128)S(1)}, f32[416,128]{1,0:T(8,128)S(1)}, u32[]{:S(2)}, u32[]{:S(2)}) %collective-permute-start.12) | collective-permute-done | bytes 213024 | tf_op jit(solution)/shard_map/ppermute | solution.py:400
  137.2 0.0 collective-permute-start.17
  137.2 1.0 unpack.1
  138.3 0.6 copy-done.4
  138.9 0.0 collective-permute-done.13.refs_2_
  138.9 4.9 %collective-permute-done.14.refs_3_ = f32[416,128]{1,0:T(8,128)S(1)} collective-permute-done((f32[416,128]{1,0:T(8,128)S(1)}, f32[416,128]{1,0:T(8,128)S(1)}, u32[]{:S(2)}, u32[]{:S(2)}) %collective-permute-start.14) | collective-permute-done | bytes 213024 | tf_op jit(solution)/shard_map/ppermute | solution.py:400
  143.8 0.0 collective-permute-done.15.refs_4_
  143.8 1.3 collective-permute-done.16.refs_5_
  145.1 0.0 collective-permute-done.17.refs_6_
  145.2 0.6 copy-done.18
  145.8 0.1 copy-done.19
  145.9 7.9 %last.1 = (f32[3,48,16,512]{3,2,1,0:T(8,128)}, f32[48,16,512]{2,1,0:T(8,128)}) custom-call(f32[12288,128]{1,0:T(8,128)} %get-tuple-element.38.far_ref, f32[128,128]{1,0:T(8,128)} %copy-done.4, bf16[512,512]{1,0:T(8,128)(2,1)} %constant.41.clone.high_ref, bf16[512,512]{1,0:T(8,128)(2,1)} %constant.42.clone.low_ref, f32[416,128]{1,0:T(8,128)} %copy-done.13, ...), custom_call_target="tpu_custom_call" | custom-call | bytes 15400960 | tf_op jit(solution)/shard_map/last/pallas_call | solution.py:37
  (32 shorter events, 0.1 us)
Async XLA Ops:
  4.9 26.8 %collective-permute-start.2 = (f32[4,48,512]{2,1,0:T(8,128)}, f32[4,48,512]{2,1,0:T(8,128)S(1)}, u32[]{:S(2)}, u32[]{:S(2)}) collective-permute-start(f32[4,48,512]{2,1,0:T(8,128)} %get-tuple-element.35), channel_id=1, source_target_pairs={{0,1},{1,2},{2,3},{3,4},{4,5},{5,6},{6,7},{7,0},{8,9},{9,10},{10,1... | collective-permute-start | bytes 1179656 | tf_op jit(solution)/shard_map/ppermute | solution.py:60
  8.0 23.8 %collective-permute-start.3 = (f32[4,48,512]{2,1,0:T(8,128)}, f32[4,48,512]{2,1,0:T(8,128)S(1)}, u32[]{:S(2)}, u32[]{:S(2)}) collective-permute-start(f32[4,48,512]{2,1,0:T(8,128)} %get-tuple-element.36), channel_id=1, source_target_pairs={{0,7},{1,0},{2,1},{3,2},{4,3},{5,4},{6,5},{7,6},{8,15},{9,8},{10,9... | collective-permute-start | bytes 1179656 | tf_op jit(solution)/shard_map/ppermute | solution.py:60
  8.0 23.7 %collective-permute-start = (f32[4,16,512]{2,1,0:T(8,128)}, f32[4,16,512]{2,1,0:T(8,128)S(1)}, u32[]{:S(2)}, u32[]{:S(2)}) collective-permute-start(f32[4,16,512]{2,1,0:T(8,128)} %get-tuple-element.33), channel_id=1, source_target_pairs={{0,8},{8,16},{16,24},{24,32},{32,40},{40,48},{48,56},{56,64},{64,7... | collective-permute-start | bytes 393224 | tf_op jit(solution)/shard_map/ppermute | solution.py:60
  9.3 22.4 %collective-permute-start.1 = (f32[4,16,512]{2,1,0:T(8,128)}, f32[4,16,512]{2,1,0:T(8,128)S(1)}, u32[]{:S(2)}, u32[]{:S(2)}) collective-permute-start(f32[4,16,512]{2,1,0:T(8,128)} %get-tuple-element.34), channel_id=1, source_target_pairs={{0,120},{8,0},{16,8},{24,16},{32,24},{40,32},{48,40},{56,48},{64,5... | collective-permute-start | bytes 393224 | tf_op jit(solution)/shard_map/ppermute | solution.py:60
  31.7 0.7 copy-start.20
  31.7 0.7 copy-start.21
  31.7 0.8 copy-start.11
  31.7 0.9 copy-start.12
  32.6 60.8 %copy-start.7 = (bf16[128,128]{1,0:T(8,128)(2,1)S(1)}, bf16[128,128]{1,0:T(8,128)(2,1)}, u32[]{:S(2)}) copy-start(bf16[128,128]{1,0:T(8,128)(2,1)} %constant.44.clone.refs_9_) | copy-start | bytes 98308
  32.6 60.8 %copy-start.8 = (bf16[128,128]{1,0:T(8,128)(2,1)S(1)}, bf16[128,128]{1,0:T(8,128)(2,1)}, u32[]{:S(2)}) copy-start(bf16[128,128]{1,0:T(8,128)(2,1)} %constant.43.clone.refs_8_) | copy-start | bytes 98308
  69.7 7.8 %collective-permute-start.4 = (f32[440,128]{1,0:T(8,128)}, f32[440,128]{1,0:T(8,128)S(1)}, u32[]{:S(2)}, u32[]{:S(2)}) collective-permute-start(f32[440,128]{1,0:T(8,128)} %get-tuple-element.40), channel_id=1, source_target_pairs={{0,4},{1,5},{2,6},{3,7},{4,0},{5,1},{6,2},{7,3},{8,12},{9,13},{10,... | collective-permute-start | bytes 675848 | tf_op jit(solution)/shard_map/ppermute | solution.py:400
  71.0 14.1 %collective-permute-start.5 = (f32[440,128]{1,0:T(8,128)}, f32[440,128]{1,0:T(8,128)S(1)}, u32[]{:S(2)}, u32[]{:S(2)}) collective-permute-start(f32[440,128]{1,0:T(8,128)} %get-tuple-element.41), channel_id=1, source_target_pairs={{0,5},{1,4},{2,7},{3,6},{4,1},{5,0},{6,3},{7,2},{8,13},{9,12},{10,... | collective-permute-start | bytes 675848 | tf_op jit(solution)/shard_map/ppermute | solution.py:400
  74.0 12.5 %collective-permute-start.6 = (f32[440,128]{1,0:T(8,128)}, f32[440,128]{1,0:T(8,128)S(1)}, u32[]{:S(2)}, u32[]{:S(2)}) collective-permute-start(f32[440,128]{1,0:T(8,128)} %get-tuple-element.42), channel_id=1, source_target_pairs={{0,2},{1,3},{2,0},{3,1},{4,6},{5,7},{6,4},{7,5},{8,10},{9,11},{10,... | collective-permute-start | bytes 675848 | tf_op jit(solution)/shard_map/ppermute | solution.py:400
  74.0 18.1 %collective-permute-start.7 = (f32[440,128]{1,0:T(8,128)}, f32[440,128]{1,0:T(8,128)S(1)}, u32[]{:S(2)}, u32[]{:S(2)}) collective-permute-start(f32[440,128]{1,0:T(8,128)} %get-tuple-element.43), channel_id=1, source_target_pairs={{0,3},{1,2},{2,1},{3,0},{4,7},{5,6},{6,5},{7,4},{8,11},{9,10},{10,... | collective-permute-start | bytes 675848 | tf_op jit(solution)/shard_map/ppermute | solution.py:400
  74.8 17.3 %collective-permute-start.8 = (f32[440,128]{1,0:T(8,128)}, f32[440,128]{1,0:T(8,128)S(1)}, u32[]{:S(2)}, u32[]{:S(2)}) collective-permute-start(f32[440,128]{1,0:T(8,128)} %get-tuple-element.44), channel_id=1, source_target_pairs={{0,6},{1,7},{2,4},{3,5},{4,2},{5,3},{6,0},{7,1},{8,14},{9,15},{10,... | collective-permute-start | bytes 675848 | tf_op jit(solution)/shard_map/ppermute | solution.py:400
  77.6 15.9 %collective-permute-start.9 = (f32[440,128]{1,0:T(8,128)}, f32[440,128]{1,0:T(8,128)S(1)}, u32[]{:S(2)}, u32[]{:S(2)}) collective-permute-start(f32[440,128]{1,0:T(8,128)} %get-tuple-element.45), channel_id=1, source_target_pairs={{0,7},{1,6},{2,5},{3,4},{4,3},{5,2},{6,1},{7,0},{8,15},{9,14},{10,... | collective-permute-start | bytes 675848 | tf_op jit(solution)/shard_map/ppermute | solution.py:400
  85.2 8.3 %collective-permute-start.10 = (f32[440,128]{1,0:T(8,128)}, f32[440,128]{1,0:T(8,128)S(1)}, u32[]{:S(2)}, u32[]{:S(2)}) collective-permute-start(f32[440,128]{1,0:T(8,128)} %get-tuple-element.46), channel_id=1, source_target_pairs={{0,1},{1,0},{2,3},{3,2},{4,5},{5,4},{6,7},{7,6},{8,9},{9,8},{10,11... | collective-permute-start | bytes 675848 | tf_op jit(solution)/shard_map/ppermute | solution.py:400
  85.2 33.4 %copy-start.5 = (bf16[128,128]{1,0:T(8,128)(2,1)S(1)}, bf16[128,128]{1,0:T(8,128)(2,1)}, u32[]{:S(2)}) copy-start(bf16[128,128]{1,0:T(8,128)(2,1)} %constant.46.clone.low_ref) | copy-start | bytes 98308
  85.2 33.4 %copy-start.6 = (bf16[128,128]{1,0:T(8,128)(2,1)S(1)}, bf16[128,128]{1,0:T(8,128)(2,1)}, u32[]{:S(2)}) copy-start(bf16[128,128]{1,0:T(8,128)(2,1)} %constant.45.clone.high_ref) | copy-start | bytes 98308
  93.5 0.9 copy-start
  97.1 0.7 copy-start.2
  97.7 39.4 %copy-start.9 = (s32[1024]{0:T(1024)S(1)}, s32[1024]{0:T(1024)}, u32[]{:S(2)}) copy-start(s32[1024]{0:T(1024)} %param.19) | copy-start | bytes 12292
  97.8 39.5 %copy-start.10 = (s32[1,1024]{1,0:T(1,128)S(1)}, s32[1,1024]{1,0:T(1,128)}, u32[]{:S(2)}) copy-start(s32[1,1024]{1,0:T(1,128)} %get-tuple-element.39.rank_ref) | copy-start | bytes 12292
  97.8 10.6 %all-to-all-start.1 = ((f32[16,24,128]{2,1,0:T(8,128)}), f32[16,24,128]{2,1,0:T(8,128)S(1)}, u32[]{:S(2)}, u32[]{:S(2)}) async-start(f32[16,24,128]{2,1,0:T(8,128)} %get-tuple-element.48), calls=%async_computation.1 | async-start | bytes 393216 | tf_op jit(solution)/shard_map/all_to_all | solution.py:821
  118.6 0.9 copy-start.3
  121.8 16.5 %copy-start.1 = (f32[416,128]{1,0:T(8,128)}, f32[416,128]{1,0:T(8,128)S(1)}, u32[]{:S(2)}) copy-start(f32[416,128]{1,0:T(8,128)S(1)} %get-tuple-element.59.refs_7_) | copy-start | bytes 638980
  121.8 7.6 %collective-permute-start.11 = (f32[416,128]{1,0:T(8,128)S(1)}, f32[416,128]{1,0:T(8,128)S(1)}, u32[]{:S(2)}, u32[]{:S(2)}) collective-permute-start(f32[416,128]{1,0:T(8,128)S(1)} %get-tuple-element.52), channel_id=1, source_target_pairs={{0,4},{1,5},{2,6},{3,7},{4,0},{5,1},{6,2},{7,3},{8,12},{9,13},{10,... | collective-permute-start | bytes 638984 | tf_op jit(solution)/shard_map/ppermute | solution.py:400
  123.1 14.1 %collective-permute-start.12 = (f32[416,128]{1,0:T(8,128)S(1)}, f32[416,128]{1,0:T(8,128)S(1)}, u32[]{:S(2)}, u32[]{:S(2)}) collective-permute-start(f32[416,128]{1,0:T(8,128)S(1)} %get-tuple-element.53), channel_id=1, source_target_pairs={{0,5},{1,4},{2,7},{3,6},{4,1},{5,0},{6,3},{7,2},{8,13},{9,12},{10,... | collective-permute-start | bytes 638984 | tf_op jit(solution)/shard_map/ppermute | solution.py:400
  127.7 11.2 %collective-permute-start.13 = (f32[416,128]{1,0:T(8,128)S(1)}, f32[416,128]{1,0:T(8,128)S(1)}, u32[]{:S(2)}, u32[]{:S(2)}) collective-permute-start(f32[416,128]{1,0:T(8,128)S(1)} %get-tuple-element.54), channel_id=1, source_target_pairs={{0,2},{1,3},{2,0},{3,1},{4,6},{5,7},{6,4},{7,5},{8,10},{9,11},{10,... | collective-permute-start | bytes 638984 | tf_op jit(solution)/shard_map/ppermute | solution.py:400
  128.1 15.7 %collective-permute-start.14 = (f32[416,128]{1,0:T(8,128)S(1)}, f32[416,128]{1,0:T(8,128)S(1)}, u32[]{:S(2)}, u32[]{:S(2)}) collective-permute-start(f32[416,128]{1,0:T(8,128)S(1)} %get-tuple-element.55), channel_id=1, source_target_pairs={{0,3},{1,2},{2,1},{3,0},{4,7},{5,6},{6,5},{7,4},{8,11},{9,10},{10,... | collective-permute-start | bytes 638984 | tf_op jit(solution)/shard_map/ppermute | solution.py:400
  128.1 15.7 %collective-permute-start.15 = (f32[416,128]{1,0:T(8,128)S(1)}, f32[416,128]{1,0:T(8,128)S(1)}, u32[]{:S(2)}, u32[]{:S(2)}) collective-permute-start(f32[416,128]{1,0:T(8,128)S(1)} %get-tuple-element.56), channel_id=1, source_target_pairs={{0,6},{1,7},{2,4},{3,5},{4,2},{5,3},{6,0},{7,1},{8,14},{9,15},{10,... | collective-permute-start | bytes 638984 | tf_op jit(solution)/shard_map/ppermute | solution.py:400
  129.3 15.8 %copy-start.13 = (f32[416,128]{1,0:T(8,128)}, f32[416,128]{1,0:T(8,128)S(1)}, u32[]{:S(2)}) copy-start(f32[416,128]{1,0:T(8,128)S(1)} %collective-permute-done.11.refs_0_) | copy-start | bytes 638980
  129.3 15.8 %collective-permute-start.16 = (f32[416,128]{1,0:T(8,128)S(1)}, f32[416,128]{1,0:T(8,128)S(1)}, u32[]{:S(2)}, u32[]{:S(2)}) collective-permute-start(f32[416,128]{1,0:T(8,128)S(1)} %get-tuple-element.57), channel_id=1, source_target_pairs={{0,7},{1,6},{2,5},{3,4},{4,3},{5,2},{6,1},{7,0},{8,15},{9,14},{10,... | collective-permute-start | bytes 638984 | tf_op jit(solution)/shard_map/ppermute | solution.py:400
  137.2 7.9 %copy-start.14 = (f32[416,128]{1,0:T(8,128)}, f32[416,128]{1,0:T(8,128)S(1)}, u32[]{:S(2)}) copy-start(f32[416,128]{1,0:T(8,128)S(1)} %collective-permute-done.12.refs_1_) | copy-start | bytes 638980
  137.2 7.9 %collective-permute-start.17 = (f32[416,128]{1,0:T(8,128)S(1)}, f32[416,128]{1,0:T(8,128)S(1)}, u32[]{:S(2)}, u32[]{:S(2)}) collective-permute-start(f32[416,128]{1,0:T(8,128)S(1)} %get-tuple-element.58), channel_id=1, source_target_pairs={{0,1},{1,0},{2,3},{3,2},{4,5},{5,4},{6,7},{7,6},{8,9},{9,8},{10,11... | collective-permute-start | bytes 638984 | tf_op jit(solution)/shard_map/ppermute | solution.py:400
  138.3 0.6 copy-start.4
  138.9 6.3 %copy-start.15 = (f32[416,128]{1,0:T(8,128)}, f32[416,128]{1,0:T(8,128)S(1)}, u32[]{:S(2)}) copy-start(f32[416,128]{1,0:T(8,128)S(1)} %collective-permute-done.13.refs_2_) | copy-start | bytes 638980
  143.8 1.3 copy-start.16
  143.8 1.3 copy-start.17
  145.1 0.7 copy-start.18
  145.1 0.8 copy-start.19

commit v4 on v3

--- a/solution.py
+++ b/solution.py
@@ -140,7 +140,7 @@
             out[3, pl.ds(y, 1), :] = scal_ref[y, z : z + 1, :]
         return carry
 
-    loop(0, rows_y, edges, 0, 4)
+    loop(0, rows_y, edges, 0, 8)
     for y, out in ((0, y_first), (rows_y - 1, y_last)):
         for f in range(3):
             out[f] = vel_ref[f, y]
@@ -176,7 +176,7 @@
     slot = column - 5 * slots
     spare = (slot >= 0) & (slot < slots) & (slot.astype(f32) >= carry)
     total = jnp.concatenate([total, jnp.zeros((owners, 2 * lanes - 6 * slots), f32)], axis=1)
-    send_ref[...] = total + jnp.where(spare, (slot * lanes).astype(f32), 0.0)
+    send_ref[:, 0, :] = total + jnp.where(spare, (slot * lanes).astype(f32), 0.0)
 
 
 def unpack_body(
@@ -217,7 +217,7 @@
 def marker_part(recv_ref, star_ref, out_ref, force_ref, samp, table, index, sem, tiles_x, depth_z):
     sources = recv_ref.shape[0]
     wide_lane = iota((sources, lanes), 1)
-    second = recv_ref[:, lanes : 2 * lanes]
+    second = recv_ref[:, 0, lanes : 2 * lanes]
     cell = pltpu.roll(second.astype(jnp.int32), lanes - 32, 1)
     tile = lax.shift_right_logical(cell, 7)
     shift_x = tiles_x.bit_length() - 1
@@ -244,7 +244,7 @@
     eta = eta + pltpu.roll(eta, 32, 1)
     eta = eta + pltpu.roll(eta, 64, 1)
     force_ref[...] = swap_groups(eta)
-    samp[...] = swap_groups(recv_ref[:, 0:lanes])
+    samp[...] = swap_groups(recv_ref[:, 0, 0:lanes])
 
     def rows_of(batch):
         return pl.ds(pl.multiple_of(4 * batch, 4), 4)
@@ -363,7 +363,7 @@
     for piece in range(pieces):
         for copy in fetches[piece + 1] if piece + 1 < pieces else ():
             copy.wait()
-        lax.fori_loop(piece * size, (piece + 1) * size, one_row, 0)
+        loop(piece * size, (piece + 1) * size, one_row, 0, 2)
 
 
 def wide_row(ref, f, y, tiles_x, depth_z):
@@ -435,7 +435,7 @@
         sums[pl.ds(y, 1), :] = jnp.sum(folded, axis=0, keepdims=True)
         return carry
 
-    loop(0, rows_y, one_row, 0, 2)
+    loop(0, rows_y, one_row, 0, 4)
     div[rows : rows + depth_z, :] = wide_row(forced_ref, 1, 0, tiles_x, depth_z)
 
 
@@ -524,13 +524,13 @@
     extra = jnp.concatenate([packed, other], axis=1).reshape(full_z, lanes)
     extra = jnp.where(first_half, times_z(extra, high_ref, low_ref), 0.0)
     ends_ref[2] = extra
-    up = loop(0, steps // 2, one_pair, extra, 3)
+    up = loop(0, steps // 2, one_pair, extra, 4)
     down = loop(
         0,
         steps,
         lambda i, total: coef_ref[steps - 1 - i] + root * total,
         jnp.zeros((full_z, lanes), f32),
-        2,
+        4,
     )
     down = root * down
     ends_ref[0] = up
@@ -594,7 +594,7 @@
         ups[step] = total
         return total
 
-    loop(0, steps, rising, up_start, 2)
+    loop(0, steps, rising, up_start, 4)
 
     def falling(i, total):
         pair = steps // 2 - 1 - i
@@ -613,7 +613,7 @@
                 out_ref[g, pl.ds(plane + step, 1), :] = value[before : before + 1, :]
         return total
 
-    down = loop(0, steps // 2, falling, down, 3)
+    down = loop(0, steps // 2, falling, down, 4)
     extra = times_z(gain * (up_start + down), high_ref, low_ref)
     half = depth_z // 2
     for g in range(n_grp):
@@ -684,7 +684,7 @@
     size = rows_y // pieces
     copies = []
     for piece in range(pieces):
-        loop(piece * size, (piece + 1) * size, one_row, 0, 2)
+        loop(piece * size, (piece + 1) * size, one_row, 0, 4)
         part = pl.ds(piece * size, size)
         copies += [
             pltpu.make_async_copy(
@@ -742,7 +742,7 @@
     owner = marker_owner[None, :]
     send, rank, y_first, y_last, z_first, z_last = call(
         pack_body,
-        [((owners, 2 * lanes), f32), ((1, held), jnp.int32)]
+        [((owners, 1, 2 * lanes), f32), ((1, held), jnp.int32)]
         + [((4, depth_z, length_x), f32)] * 2
         + [((4, rows_y, length_x), f32)] * 2,
         [
@@ -798,7 +798,7 @@
             pltpu.SemaphoreType.DMA(()),
         ],
         name="first",
-        room=58,
+        room=50,
         micros=40,
         far_in=(0, 1),
         far_out=(0,),

time: 154 us -> 147 us (0.955)
  Pallas kernels: 55.3 us -> 49.8 us
  local copies, waits for them, and re-layouts: 8.23 us -> 6.33 us
    pallas_call x7, Pallas kernels: 55.3 us -> 49.8 us  [call(): pl.pallas_call(body, out_shape=shapes, in_specs=[hbm if i in far_in else...]
    unnamed x45 -> x42, local copies, waits for them, and re-layouts: 5.53 us -> 4.67 us
  transfers between devices with their start and end apart: 19 -> 19, of which waited for: 9 -> 9; matrix products, arithmetic and copies ran while one was open for 2% -> 1% of each run, Pallas kernels for 1% -> 1%
where the time goes in v4:
time: 147 us; the launch traced here: 146 us
  Pallas kernels  49.8 us (34%)
  starting transfers between devices  33.2 us (23%)
  waiting for transfers between devices  29 us (20%)
  blocking collectives  27.1 us (18%)
  local copies, waits for them, and re-layouts  6.33 us (4%)
    pallas_call x7, Pallas kernels, call(): pl.pallas_call(body, out_shape=shapes, in_specs=[hbm if i in far_in else...  49.8 us
    ppermute x14, waiting for transfers between devices, exchanged(): lax.ppermute(part, 'grp', [(i, i ^ d) for i in range(count)])  22.8 us
    ppermute x14, starting transfers between devices, exchanged(): lax.ppermute(part, 'grp', [(i, i ^ d) for i in range(count)])  21.5 us
    all_to_all x1, blocking collectives, per_device(): lax.all_to_all(send, ('wide', 'grp'), split_axis=0, concat_axis=0, tiled=...  17.1 us
    all_to_all x1, blocking collectives, per_device(): lax.all_to_all(reach, 'wide', split_axis=0, concat_axis=0, tiled=True)  10.1 us
    ppermute x4, starting transfers between devices, passed_along(): lax.ppermute(value, axis, [(i, (i + steps) % count) for i in range(count)])  7.97 us
    all_to_all x1, waiting for transfers between devices, per_device(): lax.all_to_all(small, 'wide', split_axis=0, concat_axis=0, tiled=True)  6.21 us
    unnamed x42, local copies, waits for them, and re-layouts  4.67 us
  transfers between devices with their start and end apart: 19, of which 9 were waited for; matrix products, arithmetic and copies ran while one was open for 1% of the time, Pallas kernels for 1%

profile of v4, /device:TPU:1, one launch (start us, length us, event | category | flops | bytes accessed | tf_op | source)
XLA Modules:
  0.0 146.4 jit_solution(7504332839555562966)
XLA Ops:
  0.6 0.0 copy-start
  0.6 0.0 copy-start.1
  0.7 4.3 %pack.1 = (f32[128,1,256]{2,1,0:T(1,128)}, s32[1,1024]{1,0:T(1,128)}, f32[4,16,512]{2,1,0:T(8,128)}, f32[4,16,512]{2,1,0:T(8,128)}, f32[4,48,512]{2,1,0:T(8,128)}, /*index=5*/f32[4,48,512]{2,1,0:T(8,128)}) custom-call(s32[1,1024]{1,0:T(1,128)} %bitcast.8, s32[1,1024]{1,0:T(1,128)} %bitcast.10, s32[1,1024]{1,0:T(1,128)} %bitcast.11, f32[4,1024]{1,0:T(4,128)} %refs_3_.1, ...), custom_call_target="tpu_custom_call" | custom-call | bytes 7507968 | tf_op jit(solution)/shard_map/pack/pallas_call | solution.py:37
  5.0 3.0 %collective-permute-start.2 = (f32[4,48,512]{2,1,0:T(8,128)}, f32[4,48,512]{2,1,0:T(8,128)S(1)}, u32[]{:S(2)}, u32[]{:S(2)}) collective-permute-start(f32[4,48,512]{2,1,0:T(8,128)} %get-tuple-element.35), channel_id=1, source_target_pairs={{0,1},{1,2},{2,3},{3,4},{4,5},{5,6},{6,7},{7,0},{8,9},{9,10},{10,1... | collective-permute-start | bytes 1179656 | tf_op jit(solution)/shard_map/ppermute | solution.py:60
  8.0 0.0 collective-permute-start.3
  8.0 1.3 collective-permute-start
  9.3 3.6 %collective-permute-start.1 = (f32[4,16,512]{2,1,0:T(8,128)}, f32[4,16,512]{2,1,0:T(8,128)S(1)}, u32[]{:S(2)}, u32[]{:S(2)}) collective-permute-start(f32[4,16,512]{2,1,0:T(8,128)} %get-tuple-element.34), channel_id=1, source_target_pairs={{0,120},{8,0},{16,8},{24,16},{32,24},{40,32},{48,40},{56,48},{64,5... | collective-permute-start | bytes 393224 | tf_op jit(solution)/shard_map/ppermute | solution.py:60
  13.0 17.1 %all_to_all.15.refs_6_ = f32[128,1,256]{2,1,0:T(1,128)S(1)} all-to-all(f32[128,1,256]{2,1,0:T(1,128)} %get-tuple-element.37), channel_id=1, replica_groups=mesh['wide'=16,'grp'=8] {'wide','grp'}, dimensions={0} | all-to-all | bytes 262144 | tf_op jit(solution)/shard_map/all_to_all | solution.py:775
  30.0 0.0 collective-permute-done.refs_2_
  30.0 0.0 collective-permute-done.1.refs_3_
  30.1 0.0 collective-permute-done.2.refs_4_
  30.1 0.0 collective-permute-done.3.refs_5_
  30.1 0.0 copy-done
  30.1 0.0 copy-done.1
  30.1 32.4 %first.1 = (f32[12288,128]{1,0:T(8,128)}, f32[440,128]{1,0:T(8,128)S(1)}, f32[440,128]{1,0:T(8,128)S(1)}, f32[440,128]{1,0:T(8,128)S(1)}, f32[440,128]{1,0:T(8,1...) custom-call(f32[3,48,16,512]{3,2,1,0:T(8,128)} %refs_0_.1, ...), custom_call_target="tpu_custom_call" | custom-call | bytes 120000000 | tf_op jit(solution)/shard_map/first/pallas_call | solution.py:37
  62.6 1.3 collective-permute-start.4
  63.9 2.8 %collective-permute-start.5 = (f32[440,128]{1,0:T(8,128)S(1)}, f32[440,128]{1,0:T(8,128)S(1)}, u32[]{:S(2)}, u32[]{:S(2)}) collective-permute-start(f32[440,128]{1,0:T(8,128)S(1)} %get-tuple-element.41), channel_id=1, source_target_pairs={{0,5},{1,4},{2,7},{3,6},{4,1},{5,0},{6,3},{7,2},{8,13},{9,12},{10,... | collective-permute-start | bytes 675848 | tf_op jit(solution)/shard_map/ppermute | solution.py:400
  66.7 0.0 collective-permute-start.6
  66.7 0.9 collective-permute-start.7
  67.6 1.0 collective-permute-start.8
  68.7 1.6 %collective-permute-done.4.refs_0_ = f32[440,128]{1,0:T(8,128)S(1)} collective-permute-done((f32[440,128]{1,0:T(8,128)S(1)}, f32[440,128]{1,0:T(8,128)S(1)}, u32[]{:S(2)}, u32[]{:S(2)}) %collective-permute-start.4) | collective-permute-done | bytes 225312 | tf_op jit(solution)/shard_map/ppermute | solution.py:400
  70.2 3.7 %collective-permute-start.9 = (f32[440,128]{1,0:T(8,128)S(1)}, f32[440,128]{1,0:T(8,128)S(1)}, u32[]{:S(2)}, u32[]{:S(2)}) collective-permute-start(f32[440,128]{1,0:T(8,128)S(1)} %get-tuple-element.45), channel_id=1, source_target_pairs={{0,7},{1,6},{2,5},{3,4},{4,3},{5,2},{6,1},{7,0},{8,15},{9,14},{10,... | collective-permute-start | bytes 675848 | tf_op jit(solution)/shard_map/ppermute | solution.py:400
  73.9 3.8 %collective-permute-done.5.refs_1_ = f32[440,128]{1,0:T(8,128)S(1)} collective-permute-done((f32[440,128]{1,0:T(8,128)S(1)}, f32[440,128]{1,0:T(8,128)S(1)}, u32[]{:S(2)}, u32[]{:S(2)}) %collective-permute-start.5) | collective-permute-done | bytes 225312 | tf_op jit(solution)/shard_map/ppermute | solution.py:400
  77.7 0.0 collective-permute-start.10
  77.7 1.0 dynamic-slice_bitcast_fusion.refs_10_.table_ref
  78.6 0.5 collective-permute-done.6.refs_2_
  79.2 5.7 %collective-permute-done.7.refs_3_ = f32[440,128]{1,0:T(8,128)S(1)} collective-permute-done((f32[440,128]{1,0:T(8,128)S(1)}, f32[440,128]{1,0:T(8,128)S(1)}, u32[]{:S(2)}, u32[]{:S(2)}) %collective-permute-start.7) | collective-permute-done | bytes 225312 | tf_op jit(solution)/shard_map/ppermute | solution.py:400
  84.8 0.0 collective-permute-done.8.refs_4_
  84.8 1.2 collective-permute-done.9.refs_5_
  86.1 0.0 collective-permute-done.10.refs_6_
  86.1 0.7 copy-done.2
  86.7 0.0 copy-done.10
  86.8 0.0 copy-done.11
  86.8 0.9 copy-done.3
  87.7 2.5 %forward_z.1 = (f32[24,128,128]{2,1,0:T(8,128)S(1)}, f32[3,128,128]{2,1,0:T(8,128)S(1)}, f32[16,24,128]{2,1,0:T(8,128)}) custom-call(f32[440,128]{1,0:T(8,128)S(1)} %collective-permute-done.4.refs_0_, f32[440,128]{1,0:T(8,128)S(1)} %collective-permute-done.5.refs_1_, f32[440,128]{1,0:T(8,128)S(1)} %collective-permute-done.6.refs_2_, ...), custom_call_target="tpu_custom_call" | custom-call | bytes 4030464 | tf_op jit(solution)/shard_map/forward_z/pallas_call | solution.py:37
  90.2 0.7 copy-done.5
  90.8 3.7 %all-to-all-start.1 = ((f32[16,24,128]{2,1,0:T(8,128)}), f32[16,24,128]{2,1,0:T(8,128)S(1)}, u32[]{:S(2)}, u32[]{:S(2)}) async-start(f32[16,24,128]{2,1,0:T(8,128)} %get-tuple-element.48), calls=%async_computation.1 | async-start | bytes 393216 | tf_op jit(solution)/shard_map/all_to_all | solution.py:821
  94.5 0.7 dynamic-slice_bitcast_fusion.1.table_ref
  95.2 6.2 %all-to-all-done.1.back_ref.recv_ref = f32[16,24,128]{2,1,0:T(8,128)S(1)} async-done(((f32[16,24,128]{2,1,0:T(8,128)}), f32[16,24,128]{2,1,0:T(8,128)S(1)}, u32[]{:S(2)}, u32[]{:S(2)}) %all-to-all-start.1) | async-done | bytes 196640 | tf_op jit(solution)/shard_map/all_to_all | solution.py:821
  101.4 0.1 ring.1
  101.5 10.1 %all_to_all.16.small_ref = f32[16,8,128]{2,1,0:T(8,128)S(1)} all-to-all(f32[16,8,128]{2,1,0:T(8,128)S(1)} %ring.1), channel_id=1, replica_groups=mesh['wide'=16,'grp'=8] {'wide'}, dimensions={0} | all-to-all | bytes 131072 | tf_op jit(solution)/shard_map/all_to_all | solution.py:825
  111.6 0.0 copy-done.8
  111.6 0.9 copy-done.6
  112.5 1.9 %backward_z.1 = (f32[416,128]{1,0:T(8,128)S(1)}, f32[416,128]{1,0:T(8,128)S(1)}, f32[416,128]{1,0:T(8,128)S(1)}, f32[416,128]{1,0:T(8,128)S(1)}, f32[416,128]{1,...) custom-call(f32[24,128,128]{2,1,0:T(8,128)S(1)} %get-tuple-element.50.coef_ref, ...), custom_call_target="tpu_custom_call" | custom-call | bytes 3801088 | tf_op jit(solution)/shard_map/backward_z/pallas_call | solution.py:37
  114.4 0.0 copy-start.4
  114.4 1.6 %collective-permute-start.11 = (f32[416,128]{1,0:T(8,128)S(1)}, f32[416,128]{1,0:T(8,128)S(1)}, u32[]{:S(2)}, u32[]{:S(2)}) collective-permute-start(f32[416,128]{1,0:T(8,128)S(1)} %get-tuple-element.52), channel_id=1, source_target_pairs={{0,4},{1,5},{2,6},{3,7},{4,0},{5,1},{6,2},{7,3},{8,12},{9,13},{10,... | collective-permute-start | bytes 638984 | tf_op jit(solution)/shard_map/ppermute | solution.py:400
  116.0 4.5 %collective-permute-start.12 = (f32[416,128]{1,0:T(8,128)S(1)}, f32[416,128]{1,0:T(8,128)S(1)}, u32[]{:S(2)}, u32[]{:S(2)}) collective-permute-start(f32[416,128]{1,0:T(8,128)S(1)} %get-tuple-element.53), channel_id=1, source_target_pairs={{0,5},{1,4},{2,7},{3,6},{4,1},{5,0},{6,3},{7,2},{8,13},{9,12},{10,... | collective-permute-start | bytes 638984 | tf_op jit(solution)/shard_map/ppermute | solution.py:400
  120.5 0.6 collective-permute-start.13
  121.0 0.0 collective-permute-start.14
  121.0 1.2 collective-permute-start.15
  122.2 0.0 collective-permute-done.11.refs_0_
  122.2 4.0 %collective-permute-start.16 = (f32[416,128]{1,0:T(8,128)S(1)}, f32[416,128]{1,0:T(8,128)S(1)}, u32[]{:S(2)}, u32[]{:S(2)}) collective-permute-start(f32[416,128]{1,0:T(8,128)S(1)} %get-tuple-element.57), channel_id=1, source_target_pairs={{0,7},{1,6},{2,5},{3,4},{4,3},{5,2},{6,1},{7,0},{8,15},{9,14},{10,... | collective-permute-start | bytes 638984 | tf_op jit(solution)/shard_map/ppermute | solution.py:400
  126.2 3.7 %collective-permute-done.12.refs_1_ = f32[416,128]{1,0:T(8,128)S(1)} collective-permute-done((f32[416,128]{1,0:T(8,128)S(1)}, f32[416,128]{1,0:T(8,128)S(1)}, u32[]{:S(2)}, u32[]{:S(2)}) %collective-permute-start.12) | collective-permute-done | bytes 213024 | tf_op jit(solution)/shard_map/ppermute | solution.py:400
  129.9 0.0 collective-permute-start.17
  129.9 1.0 unpack.1
  131.0 0.6 copy-done.7
  131.6 0.0 collective-permute-done.13.refs_2_
  131.6 5.1 %collective-permute-done.14.refs_3_ = f32[416,128]{1,0:T(8,128)S(1)} collective-permute-done((f32[416,128]{1,0:T(8,128)S(1)}, f32[416,128]{1,0:T(8,128)S(1)}, u32[]{:S(2)}, u32[]{:S(2)}) %collective-permute-start.14) | collective-permute-done | bytes 213024 | tf_op jit(solution)/shard_map/ppermute | solution.py:400
  136.7 0.0 collective-permute-done.15.refs_4_
  136.7 1.2 collective-permute-done.16.refs_5_
  137.9 0.0 collective-permute-done.17.refs_6_
  137.9 0.6 copy-done.19
  138.6 0.1 copy-done.20
  138.7 7.5 %last.1 = (f32[3,48,16,512]{3,2,1,0:T(8,128)}, f32[48,16,512]{2,1,0:T(8,128)}) custom-call(f32[12288,128]{1,0:T(8,128)} %get-tuple-element.38.far_ref, f32[128,128]{1,0:T(8,128)} %copy-done.7, bf16[512,512]{1,0:T(8,128)(2,1)} %constant.41.clone.high_ref, bf16[512,512]{1,0:T(8,128)(2,1)} %constant.42.clone.low_ref, f32[416,128]{1,0:T(8,128)} %copy-done.14, ...), custom_call_target="tpu_custom_call" | custom-call | bytes 15400960 | tf_op jit(solution)/shard_map/last/pallas_call | solution.py:37
  (28 shorter events, 0.1 us)
Async XLA Ops:
  0.6 29.4 %copy-start = (bf16[512,512]{1,0:T(8,128)(2,1)S(1)}, bf16[512,512]{1,0:T(8,128)(2,1)}, u32[]{:S(2)}) copy-start(bf16[512,512]{1,0:T(8,128)(2,1)} %constant.40.clone.refs_8_) | copy-start | bytes 1572868
  0.6 29.4 %copy-start.1 = (bf16[512,512]{1,0:T(8,128)(2,1)S(1)}, bf16[512,512]{1,0:T(8,128)(2,1)}, u32[]{:S(2)}) copy-start(bf16[512,512]{1,0:T(8,128)(2,1)} %constant.39.clone.refs_7_) | copy-start | bytes 1572868
  5.0 25.1 %collective-permute-start.2 = (f32[4,48,512]{2,1,0:T(8,128)}, f32[4,48,512]{2,1,0:T(8,128)S(1)}, u32[]{:S(2)}, u32[]{:S(2)}) collective-permute-start(f32[4,48,512]{2,1,0:T(8,128)} %get-tuple-element.35), channel_id=1, source_target_pairs={{0,1},{1,2},{2,3},{3,4},{4,5},{5,6},{6,7},{7,0},{8,9},{9,10},{10,1... | collective-permute-start | bytes 1179656 | tf_op jit(solution)/shard_map/ppermute | solution.py:60
  8.0 22.0 %collective-permute-start.3 = (f32[4,48,512]{2,1,0:T(8,128)}, f32[4,48,512]{2,1,0:T(8,128)S(1)}, u32[]{:S(2)}, u32[]{:S(2)}) collective-permute-start(f32[4,48,512]{2,1,0:T(8,128)} %get-tuple-element.36), channel_id=1, source_target_pairs={{0,7},{1,0},{2,1},{3,2},{4,3},{5,4},{6,5},{7,6},{8,15},{9,8},{10,9... | collective-permute-start | bytes 1179656 | tf_op jit(solution)/shard_map/ppermute | solution.py:60
  8.0 22.0 %collective-permute-start = (f32[4,16,512]{2,1,0:T(8,128)}, f32[4,16,512]{2,1,0:T(8,128)S(1)}, u32[]{:S(2)}, u32[]{:S(2)}) collective-permute-start(f32[4,16,512]{2,1,0:T(8,128)} %get-tuple-element.33), channel_id=1, source_target_pairs={{0,8},{8,16},{16,24},{24,32},{32,40},{40,48},{48,56},{56,64},{64,7... | collective-permute-start | bytes 393224 | tf_op jit(solution)/shard_map/ppermute | solution.py:60
  9.3 20.7 %collective-permute-start.1 = (f32[4,16,512]{2,1,0:T(8,128)}, f32[4,16,512]{2,1,0:T(8,128)S(1)}, u32[]{:S(2)}, u32[]{:S(2)}) collective-permute-start(f32[4,16,512]{2,1,0:T(8,128)} %get-tuple-element.34), channel_id=1, source_target_pairs={{0,120},{8,0},{16,8},{24,16},{32,24},{40,32},{48,40},{56,48},{64,5... | collective-permute-start | bytes 393224 | tf_op jit(solution)/shard_map/ppermute | solution.py:60
  30.0 56.7 %copy-start.10 = (bf16[128,128]{1,0:T(8,128)(2,1)S(1)}, bf16[128,128]{1,0:T(8,128)(2,1)}, u32[]{:S(2)}) copy-start(bf16[128,128]{1,0:T(8,128)(2,1)} %constant.44.clone.refs_9_) | copy-start | bytes 98308
  30.0 56.7 %copy-start.11 = (bf16[128,128]{1,0:T(8,128)(2,1)S(1)}, bf16[128,128]{1,0:T(8,128)(2,1)}, u32[]{:S(2)}) copy-start(bf16[128,128]{1,0:T(8,128)(2,1)} %constant.43.clone.refs_8_) | copy-start | bytes 98308
  62.6 7.7 %collective-permute-start.4 = (f32[440,128]{1,0:T(8,128)S(1)}, f32[440,128]{1,0:T(8,128)S(1)}, u32[]{:S(2)}, u32[]{:S(2)}) collective-permute-start(f32[440,128]{1,0:T(8,128)S(1)} %get-tuple-element.40), channel_id=1, source_target_pairs={{0,4},{1,5},{2,6},{3,7},{4,0},{5,1},{6,2},{7,3},{8,12},{9,13},{10,... | collective-permute-start | bytes 675848 | tf_op jit(solution)/shard_map/ppermute | solution.py:400
  63.9 13.8 %collective-permute-start.5 = (f32[440,128]{1,0:T(8,128)S(1)}, f32[440,128]{1,0:T(8,128)S(1)}, u32[]{:S(2)}, u32[]{:S(2)}) collective-permute-start(f32[440,128]{1,0:T(8,128)S(1)} %get-tuple-element.41), channel_id=1, source_target_pairs={{0,5},{1,4},{2,7},{3,6},{4,1},{5,0},{6,3},{7,2},{8,13},{9,12},{10,... | collective-permute-start | bytes 675848 | tf_op jit(solution)/shard_map/ppermute | solution.py:400
  66.7 12.5 %collective-permute-start.6 = (f32[440,128]{1,0:T(8,128)S(1)}, f32[440,128]{1,0:T(8,128)S(1)}, u32[]{:S(2)}, u32[]{:S(2)}) collective-permute-start(f32[440,128]{1,0:T(8,128)S(1)} %get-tuple-element.42), channel_id=1, source_target_pairs={{0,2},{1,3},{2,0},{3,1},{4,6},{5,7},{6,4},{7,5},{8,10},{9,11},{10,... | collective-permute-start | bytes 675848 | tf_op jit(solution)/shard_map/ppermute | solution.py:400
  66.7 18.1 %collective-permute-start.7 = (f32[440,128]{1,0:T(8,128)S(1)}, f32[440,128]{1,0:T(8,128)S(1)}, u32[]{:S(2)}, u32[]{:S(2)}) collective-permute-start(f32[440,128]{1,0:T(8,128)S(1)} %get-tuple-element.43), channel_id=1, source_target_pairs={{0,3},{1,2},{2,1},{3,0},{4,7},{5,6},{6,5},{7,4},{8,11},{9,10},{10,... | collective-permute-start | bytes 675848 | tf_op jit(solution)/shard_map/ppermute | solution.py:400
  67.6 17.2 %collective-permute-start.8 = (f32[440,128]{1,0:T(8,128)S(1)}, f32[440,128]{1,0:T(8,128)S(1)}, u32[]{:S(2)}, u32[]{:S(2)}) collective-permute-start(f32[440,128]{1,0:T(8,128)S(1)} %get-tuple-element.44), channel_id=1, source_target_pairs={{0,6},{1,7},{2,4},{3,5},{4,2},{5,3},{6,0},{7,1},{8,14},{9,15},{10,... | collective-permute-start | bytes 675848 | tf_op jit(solution)/shard_map/ppermute | solution.py:400
  70.2 15.8 %collective-permute-start.9 = (f32[440,128]{1,0:T(8,128)S(1)}, f32[440,128]{1,0:T(8,128)S(1)}, u32[]{:S(2)}, u32[]{:S(2)}) collective-permute-start(f32[440,128]{1,0:T(8,128)S(1)} %get-tuple-element.45), channel_id=1, source_target_pairs={{0,7},{1,6},{2,5},{3,4},{4,3},{5,2},{6,1},{7,0},{8,15},{9,14},{10,... | collective-permute-start | bytes 675848 | tf_op jit(solution)/shard_map/ppermute | solution.py:400
  77.7 8.4 %collective-permute-start.10 = (f32[440,128]{1,0:T(8,128)S(1)}, f32[440,128]{1,0:T(8,128)S(1)}, u32[]{:S(2)}, u32[]{:S(2)}) collective-permute-start(f32[440,128]{1,0:T(8,128)S(1)} %get-tuple-element.46), channel_id=1, source_target_pairs={{0,1},{1,0},{2,3},{3,2},{4,5},{5,4},{6,7},{7,6},{8,9},{9,8},{10,11... | collective-permute-start | bytes 675848 | tf_op jit(solution)/shard_map/ppermute | solution.py:400
  77.7 33.9 %copy-start.8 = (bf16[128,128]{1,0:T(8,128)(2,1)S(1)}, bf16[128,128]{1,0:T(8,128)(2,1)}, u32[]{:S(2)}) copy-start(bf16[128,128]{1,0:T(8,128)(2,1)} %constant.46.clone.low_ref) | copy-start | bytes 98308
  77.7 33.9 %copy-start.9 = (bf16[128,128]{1,0:T(8,128)(2,1)S(1)}, bf16[128,128]{1,0:T(8,128)(2,1)}, u32[]{:S(2)}) copy-start(bf16[128,128]{1,0:T(8,128)(2,1)} %constant.45.clone.high_ref) | copy-start | bytes 98308
  86.1 0.7 copy-start.2
  86.8 0.9 copy-start.3
  90.2 0.7 copy-start.5
  90.8 39.1 %copy-start.12 = (s32[1024]{0:T(1024)S(1)}, s32[1024]{0:T(1024)}, u32[]{:S(2)}) copy-start(s32[1024]{0:T(1024)} %param.19) | copy-start | bytes 12292
  90.8 39.1 %copy-start.13 = (s32[1,1024]{1,0:T(1,128)S(1)}, s32[1,1024]{1,0:T(1,128)}, u32[]{:S(2)}) copy-start(s32[1,1024]{1,0:T(1,128)} %get-tuple-element.39.rank_ref) | copy-start | bytes 12292
  90.8 10.6 %all-to-all-start.1 = ((f32[16,24,128]{2,1,0:T(8,128)}), f32[16,24,128]{2,1,0:T(8,128)S(1)}, u32[]{:S(2)}, u32[]{:S(2)}) async-start(f32[16,24,128]{2,1,0:T(8,128)} %get-tuple-element.48), calls=%async_computation.1 | async-start | bytes 393216 | tf_op jit(solution)/shard_map/all_to_all | solution.py:821
  111.6 0.9 copy-start.6
  114.4 16.6 %copy-start.4 = (f32[416,128]{1,0:T(8,128)}, f32[416,128]{1,0:T(8,128)S(1)}, u32[]{:S(2)}) copy-start(f32[416,128]{1,0:T(8,128)S(1)} %get-tuple-element.59.refs_7_) | copy-start | bytes 638980
  114.4 7.8 %collective-permute-start.11 = (f32[416,128]{1,0:T(8,128)S(1)}, f32[416,128]{1,0:T(8,128)S(1)}, u32[]{:S(2)}, u32[]{:S(2)}) collective-permute-start(f32[416,128]{1,0:T(8,128)S(1)} %get-tuple-element.52), channel_id=1, source_target_pairs={{0,4},{1,5},{2,6},{3,7},{4,0},{5,1},{6,2},{7,3},{8,12},{9,13},{10,... | collective-permute-start | bytes 638984 | tf_op jit(solution)/shard_map/ppermute | solution.py:400
  116.0 13.9 %collective-permute-start.12 = (f32[416,128]{1,0:T(8,128)S(1)}, f32[416,128]{1,0:T(8,128)S(1)}, u32[]{:S(2)}, u32[]{:S(2)}) collective-permute-start(f32[416,128]{1,0:T(8,128)S(1)} %get-tuple-element.53), channel_id=1, source_target_pairs={{0,5},{1,4},{2,7},{3,6},{4,1},{5,0},{6,3},{7,2},{8,13},{9,12},{10,... | collective-permute-start | bytes 638984 | tf_op jit(solution)/shard_map/ppermute | solution.py:400
  120.5 11.1 %collective-permute-start.13 = (f32[416,128]{1,0:T(8,128)S(1)}, f32[416,128]{1,0:T(8,128)S(1)}, u32[]{:S(2)}, u32[]{:S(2)}) collective-permute-start(f32[416,128]{1,0:T(8,128)S(1)} %get-tuple-element.54), channel_id=1, source_target_pairs={{0,2},{1,3},{2,0},{3,1},{4,6},{5,7},{6,4},{7,5},{8,10},{9,11},{10,... | collective-permute-start | bytes 638984 | tf_op jit(solution)/shard_map/ppermute | solution.py:400
  121.0 15.6 %collective-permute-start.14 = (f32[416,128]{1,0:T(8,128)S(1)}, f32[416,128]{1,0:T(8,128)S(1)}, u32[]{:S(2)}, u32[]{:S(2)}) collective-permute-start(f32[416,128]{1,0:T(8,128)S(1)} %get-tuple-element.55), channel_id=1, source_target_pairs={{0,3},{1,2},{2,1},{3,0},{4,7},{5,6},{6,5},{7,4},{8,11},{9,10},{10,... | collective-permute-start | bytes 638984 | tf_op jit(solution)/shard_map/ppermute | solution.py:400
  121.0 15.6 %collective-permute-start.15 = (f32[416,128]{1,0:T(8,128)S(1)}, f32[416,128]{1,0:T(8,128)S(1)}, u32[]{:S(2)}, u32[]{:S(2)}) collective-permute-start(f32[416,128]{1,0:T(8,128)S(1)} %get-tuple-element.56), channel_id=1, source_target_pairs={{0,6},{1,7},{2,4},{3,5},{4,2},{5,3},{6,0},{7,1},{8,14},{9,15},{10,... | collective-permute-start | bytes 638984 | tf_op jit(solution)/shard_map/ppermute | solution.py:400
  122.2 15.7 %copy-start.14 = (f32[416,128]{1,0:T(8,128)}, f32[416,128]{1,0:T(8,128)S(1)}, u32[]{:S(2)}) copy-start(f32[416,128]{1,0:T(8,128)S(1)} %collective-permute-done.11.refs_0_) | copy-start | bytes 638980
  122.2 15.7 %collective-permute-start.16 = (f32[416,128]{1,0:T(8,128)S(1)}, f32[416,128]{1,0:T(8,128)S(1)}, u32[]{:S(2)}, u32[]{:S(2)}) collective-permute-start(f32[416,128]{1,0:T(8,128)S(1)} %get-tuple-element.57), channel_id=1, source_target_pairs={{0,7},{1,6},{2,5},{3,4},{4,3},{5,2},{6,1},{7,0},{8,15},{9,14},{10,... | collective-permute-start | bytes 638984 | tf_op jit(solution)/shard_map/ppermute | solution.py:400
  129.9 8.0 %copy-start.15 = (f32[416,128]{1,0:T(8,128)}, f32[416,128]{1,0:T(8,128)S(1)}, u32[]{:S(2)}) copy-start(f32[416,128]{1,0:T(8,128)S(1)} %collective-permute-done.12.refs_1_) | copy-start | bytes 638980
  129.9 8.0 %collective-permute-start.17 = (f32[416,128]{1,0:T(8,128)S(1)}, f32[416,128]{1,0:T(8,128)S(1)}, u32[]{:S(2)}, u32[]{:S(2)}) collective-permute-start(f32[416,128]{1,0:T(8,128)S(1)} %get-tuple-element.58), channel_id=1, source_target_pairs={{0,1},{1,0},{2,3},{3,2},{4,5},{5,4},{6,7},{7,6},{8,9},{9,8},{10,11... | collective-permute-start | bytes 638984 | tf_op jit(solution)/shard_map/ppermute | solution.py:400
  131.0 0.6 copy-start.7
  131.6 6.3 %copy-start.16 = (f32[416,128]{1,0:T(8,128)}, f32[416,128]{1,0:T(8,128)S(1)}, u32[]{:S(2)}) copy-start(f32[416,128]{1,0:T(8,128)S(1)} %collective-permute-done.13.refs_2_) | copy-start | bytes 638980
  136.7 1.3 copy-start.17
  136.7 1.3 copy-start.18
  137.9 0.7 copy-start.19
  137.9 0.8 copy-start.20

commit v5 on v4

--- a/solution.py
+++ b/solution.py
@@ -120,31 +120,23 @@
 
 
 def pack_body(*refs):
-    far, near, sems = refs[:7], refs[13:20], refs[20]
+    far, near, sems = refs[:7], refs[13:18], refs[18]
     send_ref, rank_ref, y_first, y_last, z_first, z_last = refs[7:13]
-    owner_ref, tile_ref, offset_ref, target_ref, eta_ref, vel_ref, scal_ref = near
-    copies = [pltpu.make_async_copy(a, b, sems.at[i]) for i, (a, b) in enumerate(zip(far, near))]
-    for copy in copies:
+    vel_far, scal_far = far[5:]
+    rows_y, depth_z, _ = scal_far.shape
+    pairs = list(zip(far[:5], near))
+    for y, out in ((0, y_first), (rows_y - 1, y_last)):
+        pairs += [(vel_far.at[:, y], out.at[0:3]), (scal_far.at[y], out.at[3])]
+    for z, out in ((0, z_first), (depth_z - 1, z_last)):
+        pairs += [(vel_far.at[:, :, z, :], out.at[0:3]), (scal_far.at[:, z, :], out.at[3])]
+    copies = [pltpu.make_async_copy(a, b, sems.at[i]) for i, (a, b) in enumerate(pairs)]
+    for copy in copies[5:] + copies[:5]:
         copy.start()
     for copy in copies[:5]:
         copy.wait()
-    pack_markers(owner_ref, tile_ref, offset_ref, target_ref, eta_ref, send_ref, rank_ref)
+    pack_markers(*near, send_ref, rank_ref)
     for copy in copies[5:]:
         copy.wait()
-    rows_y, depth_z, _ = scal_ref.shape
-
-    def edges(y, carry):
-        for z, out in ((0, z_first), (depth_z - 1, z_last)):
-            for f in range(3):
-                out[f, pl.ds(y, 1), :] = vel_ref[f, y, z : z + 1, :]
-            out[3, pl.ds(y, 1), :] = scal_ref[y, z : z + 1, :]
-        return carry
-
-    loop(0, rows_y, edges, 0, 8)
-    for y, out in ((0, y_first), (rows_y - 1, y_last)):
-        for f in range(3):
-            out[f] = vel_ref[f, y]
-        out[3] = scal_ref[y]
 
 
 def pack_markers(owner_ref, tile_ref, offset_ref, target_ref, eta_ref, send_ref, rank_ref):
@@ -363,7 +355,7 @@
     for piece in range(pieces):
         for copy in fetches[piece + 1] if piece + 1 < pieces else ():
             copy.wait()
-        loop(piece * size, (piece + 1) * size, one_row, 0, 2)
+        loop(piece * size, (piece + 1) * size, one_row, 0, 3)
 
 
 def wide_row(ref, f, y, tiles_x, depth_z):
@@ -435,7 +427,7 @@
         sums[pl.ds(y, 1), :] = jnp.sum(folded, axis=0, keepdims=True)
         return carry
 
-    loop(0, rows_y, one_row, 0, 4)
+    loop(0, rows_y, one_row, 0, 6)
     div[rows : rows + depth_z, :] = wide_row(forced_ref, 1, 0, tiles_x, depth_z)
 
 
@@ -476,7 +468,7 @@
         send(front, back, depth_z, front)
         return carry
 
-    loop(0, rows_y // 2, shuffle, 0, 4)
+    loop(0, rows_y // 2, shuffle, 0, 8)
     send(rows, rows + depth_z // 2, depth_z // 2, row)
     send(rows + depth_z, rows + depth_z + rows_y // 2, rows_y // 2, plane)
     total = jnp.broadcast_to(jnp.sum(samp[...].T, axis=0, keepdims=True), (end - sums_row, lanes))
@@ -524,7 +516,7 @@
     extra = jnp.concatenate([packed, other], axis=1).reshape(full_z, lanes)
     extra = jnp.where(first_half, times_z(extra, high_ref, low_ref), 0.0)
     ends_ref[2] = extra
-    up = loop(0, steps // 2, one_pair, extra, 4)
+    up = loop(0, steps // 2, one_pair, extra, 6)
     down = loop(
         0,
         steps,
@@ -613,7 +605,7 @@
                 out_ref[g, pl.ds(plane + step, 1), :] = value[before : before + 1, :]
         return total
 
-    down = loop(0, steps // 2, falling, down, 4)
+    down = loop(0, steps // 2, falling, down, 6)
     extra = times_z(gain * (up_start + down), high_ref, low_ref)
     half = depth_z // 2
     for g in range(n_grp):
@@ -653,7 +645,7 @@
         take(front, back, depth_z, front)
         return carry
 
-    loop(0, rows_y // 2, shuffle, 0, 4)
+    loop(0, rows_y // 2, shuffle, 0, 8)
     take(rows, rows + depth_z // 2, depth_z // 2, row)
     take(rows + depth_z, rows + depth_z + rows_y // 2, rows_y // 2, plane)
     chunk = modes.shape[0] // 4
@@ -684,7 +676,7 @@
     size = rows_y // pieces
     copies = []
     for piece in range(pieces):
-        loop(piece * size, (piece + 1) * size, one_row, 0, 4)
+        loop(piece * size, (piece + 1) * size, one_row, 0, 6)
         part = pl.ds(piece * size, size)
         copies += [
             pltpu.make_async_copy(
@@ -760,9 +752,7 @@
             pltpu.VMEM((1, held), jnp.int32),
             pltpu.VMEM((4, held), f32),
             pltpu.VMEM((1, held), f32),
-            pltpu.VMEM(velocity.shape, f32),
-            pltpu.VMEM(scalar.shape, f32),
-            pltpu.SemaphoreType.DMA((7,)),
+            pltpu.SemaphoreType.DMA((13,)),
         ],
         name="pack",
         room=58,

time: 147 us -> 144 us (0.980)
  Pallas kernels: 49.8 us -> 47.4 us
    pallas_call x7, Pallas kernels: 49.8 us -> 47.4 us  [call(): pl.pallas_call(body, out_shape=shapes, in_specs=[hbm if i in far_in else...]
where the time goes in v5:
time: 144 us
  Pallas kernels  47.4 us (33%)
  starting transfers between devices  33.2 us (23%)
  waiting for transfers between devices  28.9 us (20%)
  blocking collectives  27.1 us (19%)
  local copies, waits for them, and re-layouts  6.33 us (4%)
    pallas_call x7, Pallas kernels, call(): pl.pallas_call(body, out_shape=shapes, in_specs=[hbm if i in far_in else...  47.4 us
    ppermute x14, waiting for transfers between devices, exchanged(): lax.ppermute(part, 'grp', [(i, i ^ d) for i in range(count)])  22.7 us
    ppermute x14, starting transfers between devices, exchanged(): lax.ppermute(part, 'grp', [(i, i ^ d) for i in range(count)])  21.6 us
    all_to_all x1, blocking collectives, per_device(): lax.all_to_all(send, ('wide', 'grp'), split_axis=0, concat_axis=0, tiled=...  17.1 us
    all_to_all x1, blocking collectives, per_device(): lax.all_to_all(reach, 'wide', split_axis=0, concat_axis=0, tiled=True)  10.1 us
    ppermute x4, starting transfers between devices, passed_along(): lax.ppermute(value, axis, [(i, (i + steps) % count) for i in range(count)])  7.97 us
    all_to_all x1, waiting for transfers between devices, per_device(): lax.all_to_all(small, 'wide', split_axis=0, concat_axis=0, tiled=True)  6.21 us
    unnamed x42, local copies, waits for them, and re-layouts  4.67 us
  transfers between devices with their start and end apart: 19, of which 9 were waited for; matrix products, arithmetic and copies ran while one was open for 1% of the time, Pallas kernels for 1%

profile of v5, /device:TPU:1, one launch (start us, length us, event | category | flops | bytes accessed | tf_op | source)
XLA Modules:
  0.0 144.0 jit_solution(8366285858784511642)
XLA Ops:
  0.6 0.0 copy-start
  0.6 0.0 copy-start.1
  0.7 3.1 %pack.1 = (f32[128,1,256]{2,1,0:T(1,128)}, s32[1,1024]{1,0:T(1,128)}, f32[4,16,512]{2,1,0:T(8,128)}, f32[4,16,512]{2,1,0:T(8,128)}, f32[4,48,512]{2,1,0:T(8,128)}, /*index=5*/f32[4,48,512]{2,1,0:T(8,128)}) custom-call(s32[1,1024]{1,0:T(1,128)} %bitcast.8, s32[1,1024]{1,0:T(1,128)} %bitcast.10, s32[1,1024]{1,0:T(1,128)} %bitcast.11, f32[4,1024]{1,0:T(4,128)} %refs_3_.1, ...), custom_call_target="tpu_custom_call" | custom-call | bytes 7507968 | tf_op jit(solution)/shard_map/pack/pallas_call | solution.py:37
  3.8 3.0 %collective-permute-start.2 = (f32[4,48,512]{2,1,0:T(8,128)}, f32[4,48,512]{2,1,0:T(8,128)S(1)}, u32[]{:S(2)}, u32[]{:S(2)}) collective-permute-start(f32[4,48,512]{2,1,0:T(8,128)} %get-tuple-element.35), channel_id=1, source_target_pairs={{0,1},{1,2},{2,3},{3,4},{4,5},{5,6},{6,7},{7,0},{8,9},{9,10},{10,1... | collective-permute-start | bytes 1179656 | tf_op jit(solution)/shard_map/ppermute | solution.py:60
  6.8 0.0 collective-permute-start.3
  6.8 1.3 collective-permute-start
  8.1 3.6 %collective-permute-start.1 = (f32[4,16,512]{2,1,0:T(8,128)}, f32[4,16,512]{2,1,0:T(8,128)S(1)}, u32[]{:S(2)}, u32[]{:S(2)}) collective-permute-start(f32[4,16,512]{2,1,0:T(8,128)} %get-tuple-element.34), channel_id=1, source_target_pairs={{0,120},{8,0},{16,8},{24,16},{32,24},{40,32},{48,40},{56,48},{64,5... | collective-permute-start | bytes 393224 | tf_op jit(solution)/shard_map/ppermute | solution.py:60
  11.8 17.1 %all_to_all.15.refs_6_ = f32[128,1,256]{2,1,0:T(1,128)S(1)} all-to-all(f32[128,1,256]{2,1,0:T(1,128)} %get-tuple-element.37), channel_id=1, replica_groups=mesh['wide'=16,'grp'=8] {'wide','grp'}, dimensions={0} | all-to-all | bytes 262144 | tf_op jit(solution)/shard_map/all_to_all | solution.py:765
  28.8 0.0 collective-permute-done.refs_2_
  28.8 0.0 collective-permute-done.1.refs_3_
  28.8 0.0 collective-permute-done.2.refs_4_
  28.8 0.0 collective-permute-done.3.refs_5_
  28.9 0.0 copy-done
  28.9 0.0 copy-done.1
  28.9 31.7 %first.1 = (f32[12288,128]{1,0:T(8,128)}, f32[440,128]{1,0:T(8,128)S(1)}, f32[440,128]{1,0:T(8,128)S(1)}, f32[440,128]{1,0:T(8,128)S(1)}, f32[440,128]{1,0:T(8,1...) custom-call(f32[3,48,16,512]{3,2,1,0:T(8,128)} %refs_0_.1, ...), custom_call_target="tpu_custom_call" | custom-call | bytes 120000000 | tf_op jit(solution)/shard_map/first/pallas_call | solution.py:37
  60.6 1.3 collective-permute-start.4
  61.9 2.8 %collective-permute-start.5 = (f32[440,128]{1,0:T(8,128)S(1)}, f32[440,128]{1,0:T(8,128)S(1)}, u32[]{:S(2)}, u32[]{:S(2)}) collective-permute-start(f32[440,128]{1,0:T(8,128)S(1)} %get-tuple-element.41), channel_id=1, source_target_pairs={{0,5},{1,4},{2,7},{3,6},{4,1},{5,0},{6,3},{7,2},{8,13},{9,12},{10,... | collective-permute-start | bytes 675848 | tf_op jit(solution)/shard_map/ppermute | solution.py:392
  64.7 0.0 collective-permute-start.6
  64.8 0.9 collective-permute-start.7
  65.7 1.1 collective-permute-start.8
  66.7 1.6 %collective-permute-done.4.refs_0_ = f32[440,128]{1,0:T(8,128)S(1)} collective-permute-done((f32[440,128]{1,0:T(8,128)S(1)}, f32[440,128]{1,0:T(8,128)S(1)}, u32[]{:S(2)}, u32[]{:S(2)}) %collective-permute-start.4) | collective-permute-done | bytes 225312 | tf_op jit(solution)/shard_map/ppermute | solution.py:392
  68.3 3.7 %collective-permute-start.9 = (f32[440,128]{1,0:T(8,128)S(1)}, f32[440,128]{1,0:T(8,128)S(1)}, u32[]{:S(2)}, u32[]{:S(2)}) collective-permute-start(f32[440,128]{1,0:T(8,128)S(1)} %get-tuple-element.45), channel_id=1, source_target_pairs={{0,7},{1,6},{2,5},{3,4},{4,3},{5,2},{6,1},{7,0},{8,15},{9,14},{10,... | collective-permute-start | bytes 675848 | tf_op jit(solution)/shard_map/ppermute | solution.py:392
  71.9 3.8 %collective-permute-done.5.refs_1_ = f32[440,128]{1,0:T(8,128)S(1)} collective-permute-done((f32[440,128]{1,0:T(8,128)S(1)}, f32[440,128]{1,0:T(8,128)S(1)}, u32[]{:S(2)}, u32[]{:S(2)}) %collective-permute-start.5) | collective-permute-done | bytes 225312 | tf_op jit(solution)/shard_map/ppermute | solution.py:392
  75.7 0.0 collective-permute-start.10
  75.7 1.0 dynamic-slice_bitcast_fusion.refs_10_.table_ref
  76.7 0.5 collective-permute-done.6.refs_2_
  77.2 5.7 %collective-permute-done.7.refs_3_ = f32[440,128]{1,0:T(8,128)S(1)} collective-permute-done((f32[440,128]{1,0:T(8,128)S(1)}, f32[440,128]{1,0:T(8,128)S(1)}, u32[]{:S(2)}, u32[]{:S(2)}) %collective-permute-start.7) | collective-permute-done | bytes 225312 | tf_op jit(solution)/shard_map/ppermute | solution.py:392
  82.9 0.0 collective-permute-done.8.refs_4_
  82.9 1.2 collective-permute-done.9.refs_5_
  84.1 0.0 collective-permute-done.10.refs_6_
  84.1 0.7 copy-done.2
  84.8 0.0 copy-done.10
  84.8 0.0 copy-done.11
  84.8 0.9 copy-done.3
  85.7 2.3 %forward_z.1 = (f32[24,128,128]{2,1,0:T(8,128)S(1)}, f32[3,128,128]{2,1,0:T(8,128)S(1)}, f32[16,24,128]{2,1,0:T(8,128)}) custom-call(f32[440,128]{1,0:T(8,128)S(1)} %collective-permute-done.4.refs_0_, f32[440,128]{1,0:T(8,128)S(1)} %collective-permute-done.5.refs_1_, f32[440,128]{1,0:T(8,128)S(1)} %collective-permute-done.6.refs_2_, ...), custom_call_target="tpu_custom_call" | custom-call | bytes 4030464 | tf_op jit(solution)/shard_map/forward_z/pallas_call | solution.py:37
  88.0 0.7 copy-done.5
  88.7 3.7 %all-to-all-start.1 = ((f32[16,24,128]{2,1,0:T(8,128)}), f32[16,24,128]{2,1,0:T(8,128)S(1)}, u32[]{:S(2)}, u32[]{:S(2)}) async-start(f32[16,24,128]{2,1,0:T(8,128)} %get-tuple-element.48), calls=%async_computation.1 | async-start | bytes 393216 | tf_op jit(solution)/shard_map/all_to_all | solution.py:811
  92.4 0.7 dynamic-slice_bitcast_fusion.1.table_ref
  93.1 6.2 %all-to-all-done.1.back_ref.recv_ref = f32[16,24,128]{2,1,0:T(8,128)S(1)} async-done(((f32[16,24,128]{2,1,0:T(8,128)}), f32[16,24,128]{2,1,0:T(8,128)S(1)}, u32[]{:S(2)}, u32[]{:S(2)}) %all-to-all-start.1) | async-done | bytes 196640 | tf_op jit(solution)/shard_map/all_to_all | solution.py:811
  99.3 0.1 ring.1
  99.4 10.1 %all_to_all.16.small_ref = f32[16,8,128]{2,1,0:T(8,128)S(1)} all-to-all(f32[16,8,128]{2,1,0:T(8,128)S(1)} %ring.1), channel_id=1, replica_groups=mesh['wide'=16,'grp'=8] {'wide'}, dimensions={0} | all-to-all | bytes 131072 | tf_op jit(solution)/shard_map/all_to_all | solution.py:815
  109.4 0.0 copy-done.8
  109.4 0.0 copy-done.9
  109.4 0.9 copy-done.6
  110.3 1.7 %backward_z.1 = (f32[416,128]{1,0:T(8,128)S(1)}, f32[416,128]{1,0:T(8,128)S(1)}, f32[416,128]{1,0:T(8,128)S(1)}, f32[416,128]{1,0:T(8,128)S(1)}, f32[416,128]{1,...) custom-call(f32[24,128,128]{2,1,0:T(8,128)S(1)} %get-tuple-element.50.coef_ref, ...), custom_call_target="tpu_custom_call" | custom-call | bytes 3801088 | tf_op jit(solution)/shard_map/backward_z/pallas_call | solution.py:37
  112.1 1.6 %collective-permute-start.11 = (f32[416,128]{1,0:T(8,128)S(1)}, f32[416,128]{1,0:T(8,128)S(1)}, u32[]{:S(2)}, u32[]{:S(2)}) collective-permute-start(f32[416,128]{1,0:T(8,128)S(1)} %get-tuple-element.52), channel_id=1, source_target_pairs={{0,4},{1,5},{2,6},{3,7},{4,0},{5,1},{6,2},{7,3},{8,12},{9,13},{10,... | collective-permute-start | bytes 638984 | tf_op jit(solution)/shard_map/ppermute | solution.py:392
  113.6 4.5 %collective-permute-start.12 = (f32[416,128]{1,0:T(8,128)S(1)}, f32[416,128]{1,0:T(8,128)S(1)}, u32[]{:S(2)}, u32[]{:S(2)}) collective-permute-start(f32[416,128]{1,0:T(8,128)S(1)} %get-tuple-element.53), channel_id=1, source_target_pairs={{0,5},{1,4},{2,7},{3,6},{4,1},{5,0},{6,3},{7,2},{8,13},{9,12},{10,... | collective-permute-start | bytes 638984 | tf_op jit(solution)/shard_map/ppermute | solution.py:392
  118.1 0.6 collective-permute-start.13
  118.7 0.0 collective-permute-start.14
  118.7 1.2 collective-permute-start.15
  119.9 0.0 collective-permute-done.11.refs_0_
  119.9 4.0 %collective-permute-start.16 = (f32[416,128]{1,0:T(8,128)S(1)}, f32[416,128]{1,0:T(8,128)S(1)}, u32[]{:S(2)}, u32[]{:S(2)}) collective-permute-start(f32[416,128]{1,0:T(8,128)S(1)} %get-tuple-element.57), channel_id=1, source_target_pairs={{0,7},{1,6},{2,5},{3,4},{4,3},{5,2},{6,1},{7,0},{8,15},{9,14},{10,... | collective-permute-start | bytes 638984 | tf_op jit(solution)/shard_map/ppermute | solution.py:392
  123.9 3.7 %collective-permute-done.12.refs_1_ = f32[416,128]{1,0:T(8,128)S(1)} collective-permute-done((f32[416,128]{1,0:T(8,128)S(1)}, f32[416,128]{1,0:T(8,128)S(1)}, u32[]{:S(2)}, u32[]{:S(2)}) %collective-permute-start.12) | collective-permute-done | bytes 213024 | tf_op jit(solution)/shard_map/ppermute | solution.py:392
  127.5 0.0 collective-permute-start.17
  127.6 1.0 unpack.1
  128.6 0.6 copy-done.7
  129.2 0.0 collective-permute-done.13.refs_2_
  129.2 5.1 %collective-permute-done.14.refs_3_ = f32[416,128]{1,0:T(8,128)S(1)} collective-permute-done((f32[416,128]{1,0:T(8,128)S(1)}, f32[416,128]{1,0:T(8,128)S(1)}, u32[]{:S(2)}, u32[]{:S(2)}) %collective-permute-start.14) | collective-permute-done | bytes 213024 | tf_op jit(solution)/shard_map/ppermute | solution.py:392
  134.3 0.0 collective-permute-done.15.refs_4_
  134.3 1.2 collective-permute-done.16.refs_5_
  135.5 0.0 collective-permute-done.17.refs_6_
  135.6 0.6 copy-done.19
  136.2 0.1 copy-done.20
  136.3 7.5 %last.1 = (f32[3,48,16,512]{3,2,1,0:T(8,128)}, f32[48,16,512]{2,1,0:T(8,128)}) custom-call(f32[12288,128]{1,0:T(8,128)} %get-tuple-element.38.far_ref, f32[128,128]{1,0:T(8,128)} %copy-done.7, bf16[512,512]{1,0:T(8,128)(2,1)} %constant.41.clone.high_ref, bf16[512,512]{1,0:T(8,128)(2,1)} %constant.42.clone.low_ref, f32[416,128]{1,0:T(8,128)} %copy-done.14, ...), custom_call_target="tpu_custom_call" | custom-call | bytes 15400960 | tf_op jit(solution)/shard_map/last/pallas_call | solution.py:37
  (28 shorter events, 0.1 us)
Async XLA Ops:
  0.6 28.2 %copy-start = (bf16[512,512]{1,0:T(8,128)(2,1)S(1)}, bf16[512,512]{1,0:T(8,128)(2,1)}, u32[]{:S(2)}) copy-start(bf16[512,512]{1,0:T(8,128)(2,1)} %constant.40.clone.refs_8_) | copy-start | bytes 1572868
  0.6 28.2 %copy-start.1 = (bf16[512,512]{1,0:T(8,128)(2,1)S(1)}, bf16[512,512]{1,0:T(8,128)(2,1)}, u32[]{:S(2)}) copy-start(bf16[512,512]{1,0:T(8,128)(2,1)} %constant.39.clone.refs_7_) | copy-start | bytes 1572868
  3.8 25.1 %collective-permute-start.2 = (f32[4,48,512]{2,1,0:T(8,128)}, f32[4,48,512]{2,1,0:T(8,128)S(1)}, u32[]{:S(2)}, u32[]{:S(2)}) collective-permute-start(f32[4,48,512]{2,1,0:T(8,128)} %get-tuple-element.35), channel_id=1, source_target_pairs={{0,1},{1,2},{2,3},{3,4},{4,5},{5,6},{6,7},{7,0},{8,9},{9,10},{10,1... | collective-permute-start | bytes 1179656 | tf_op jit(solution)/shard_map/ppermute | solution.py:60
  6.8 22.0 %collective-permute-start.3 = (f32[4,48,512]{2,1,0:T(8,128)}, f32[4,48,512]{2,1,0:T(8,128)S(1)}, u32[]{:S(2)}, u32[]{:S(2)}) collective-permute-start(f32[4,48,512]{2,1,0:T(8,128)} %get-tuple-element.36), channel_id=1, source_target_pairs={{0,7},{1,0},{2,1},{3,2},{4,3},{5,4},{6,5},{7,6},{8,15},{9,8},{10,9... | collective-permute-start | bytes 1179656 | tf_op jit(solution)/shard_map/ppermute | solution.py:60
  6.8 22.0 %collective-permute-start = (f32[4,16,512]{2,1,0:T(8,128)}, f32[4,16,512]{2,1,0:T(8,128)S(1)}, u32[]{:S(2)}, u32[]{:S(2)}) collective-permute-start(f32[4,16,512]{2,1,0:T(8,128)} %get-tuple-element.33), channel_id=1, source_target_pairs={{0,8},{8,16},{16,24},{24,32},{32,40},{40,48},{48,56},{56,64},{64,7... | collective-permute-start | bytes 393224 | tf_op jit(solution)/shard_map/ppermute | solution.py:60
  8.1 20.7 %collective-permute-start.1 = (f32[4,16,512]{2,1,0:T(8,128)}, f32[4,16,512]{2,1,0:T(8,128)S(1)}, u32[]{:S(2)}, u32[]{:S(2)}) collective-permute-start(f32[4,16,512]{2,1,0:T(8,128)} %get-tuple-element.34), channel_id=1, source_target_pairs={{0,120},{8,0},{16,8},{24,16},{32,24},{40,32},{48,40},{56,48},{64,5... | collective-permute-start | bytes 393224 | tf_op jit(solution)/shard_map/ppermute | solution.py:60
  28.8 56.0 %copy-start.10 = (bf16[128,128]{1,0:T(8,128)(2,1)S(1)}, bf16[128,128]{1,0:T(8,128)(2,1)}, u32[]{:S(2)}) copy-start(bf16[128,128]{1,0:T(8,128)(2,1)} %constant.44.clone.refs_9_) | copy-start | bytes 98308
  28.8 56.0 %copy-start.11 = (bf16[128,128]{1,0:T(8,128)(2,1)S(1)}, bf16[128,128]{1,0:T(8,128)(2,1)}, u32[]{:S(2)}) copy-start(bf16[128,128]{1,0:T(8,128)(2,1)} %constant.43.clone.refs_8_) | copy-start | bytes 98308
  60.6 7.7 %collective-permute-start.4 = (f32[440,128]{1,0:T(8,128)S(1)}, f32[440,128]{1,0:T(8,128)S(1)}, u32[]{:S(2)}, u32[]{:S(2)}) collective-permute-start(f32[440,128]{1,0:T(8,128)S(1)} %get-tuple-element.40), channel_id=1, source_target_pairs={{0,4},{1,5},{2,6},{3,7},{4,0},{5,1},{6,2},{7,3},{8,12},{9,13},{10,... | collective-permute-start | bytes 675848 | tf_op jit(solution)/shard_map/ppermute | solution.py:392
  61.9 13.8 %collective-permute-start.5 = (f32[440,128]{1,0:T(8,128)S(1)}, f32[440,128]{1,0:T(8,128)S(1)}, u32[]{:S(2)}, u32[]{:S(2)}) collective-permute-start(f32[440,128]{1,0:T(8,128)S(1)} %get-tuple-element.41), channel_id=1, source_target_pairs={{0,5},{1,4},{2,7},{3,6},{4,1},{5,0},{6,3},{7,2},{8,13},{9,12},{10,... | collective-permute-start | bytes 675848 | tf_op jit(solution)/shard_map/ppermute | solution.py:392
  64.7 12.5 %collective-permute-start.6 = (f32[440,128]{1,0:T(8,128)S(1)}, f32[440,128]{1,0:T(8,128)S(1)}, u32[]{:S(2)}, u32[]{:S(2)}) collective-permute-start(f32[440,128]{1,0:T(8,128)S(1)} %get-tuple-element.42), channel_id=1, source_target_pairs={{0,2},{1,3},{2,0},{3,1},{4,6},{5,7},{6,4},{7,5},{8,10},{9,11},{10,... | collective-permute-start | bytes 675848 | tf_op jit(solution)/shard_map/ppermute | solution.py:392
  64.8 18.1 %collective-permute-start.7 = (f32[440,128]{1,0:T(8,128)S(1)}, f32[440,128]{1,0:T(8,128)S(1)}, u32[]{:S(2)}, u32[]{:S(2)}) collective-permute-start(f32[440,128]{1,0:T(8,128)S(1)} %get-tuple-element.43), channel_id=1, source_target_pairs={{0,3},{1,2},{2,1},{3,0},{4,7},{5,6},{6,5},{7,4},{8,11},{9,10},{10,... | collective-permute-start | bytes 675848 | tf_op jit(solution)/shard_map/ppermute | solution.py:392
  65.7 17.2 %collective-permute-start.8 = (f32[440,128]{1,0:T(8,128)S(1)}, f32[440,128]{1,0:T(8,128)S(1)}, u32[]{:S(2)}, u32[]{:S(2)}) collective-permute-start(f32[440,128]{1,0:T(8,128)S(1)} %get-tuple-element.44), channel_id=1, source_target_pairs={{0,6},{1,7},{2,4},{3,5},{4,2},{5,3},{6,0},{7,1},{8,14},{9,15},{10,... | collective-permute-start | bytes 675848 | tf_op jit(solution)/shard_map/ppermute | solution.py:392
  68.3 15.8 %collective-permute-start.9 = (f32[440,128]{1,0:T(8,128)S(1)}, f32[440,128]{1,0:T(8,128)S(1)}, u32[]{:S(2)}, u32[]{:S(2)}) collective-permute-start(f32[440,128]{1,0:T(8,128)S(1)} %get-tuple-element.45), channel_id=1, source_target_pairs={{0,7},{1,6},{2,5},{3,4},{4,3},{5,2},{6,1},{7,0},{8,15},{9,14},{10,... | collective-permute-start | bytes 675848 | tf_op jit(solution)/shard_map/ppermute | solution.py:392
  75.7 8.4 %collective-permute-start.10 = (f32[440,128]{1,0:T(8,128)S(1)}, f32[440,128]{1,0:T(8,128)S(1)}, u32[]{:S(2)}, u32[]{:S(2)}) collective-permute-start(f32[440,128]{1,0:T(8,128)S(1)} %get-tuple-element.46), channel_id=1, source_target_pairs={{0,1},{1,0},{2,3},{3,2},{4,5},{5,4},{6,7},{7,6},{8,9},{9,8},{10,11... | collective-permute-start | bytes 675848 | tf_op jit(solution)/shard_map/ppermute | solution.py:392
  75.7 33.7 %copy-start.8 = (bf16[128,128]{1,0:T(8,128)(2,1)S(1)}, bf16[128,128]{1,0:T(8,128)(2,1)}, u32[]{:S(2)}) copy-start(bf16[128,128]{1,0:T(8,128)(2,1)} %constant.46.clone.low_ref) | copy-start | bytes 98308
  75.7 33.7 %copy-start.9 = (bf16[128,128]{1,0:T(8,128)(2,1)S(1)}, bf16[128,128]{1,0:T(8,128)(2,1)}, u32[]{:S(2)}) copy-start(bf16[128,128]{1,0:T(8,128)(2,1)} %constant.45.clone.high_ref) | copy-start | bytes 98308
  84.1 0.7 copy-start.2
  84.8 0.9 copy-start.3
  88.0 0.7 copy-start.5
  88.7 38.9 %copy-start.12 = (s32[1024]{0:T(1024)S(1)}, s32[1024]{0:T(1024)}, u32[]{:S(2)}) copy-start(s32[1024]{0:T(1024)} %param.19) | copy-start | bytes 12292
  88.7 38.9 %copy-start.13 = (s32[1,1024]{1,0:T(1,128)S(1)}, s32[1,1024]{1,0:T(1,128)}, u32[]{:S(2)}) copy-start(s32[1,1024]{1,0:T(1,128)} %get-tuple-element.39.rank_ref) | copy-start | bytes 12292
  88.7 10.6 %all-to-all-start.1 = ((f32[16,24,128]{2,1,0:T(8,128)}), f32[16,24,128]{2,1,0:T(8,128)S(1)}, u32[]{:S(2)}, u32[]{:S(2)}) async-start(f32[16,24,128]{2,1,0:T(8,128)} %get-tuple-element.48), calls=%async_computation.1 | async-start | bytes 393216 | tf_op jit(solution)/shard_map/all_to_all | solution.py:811
  109.4 0.9 copy-start.6
  112.1 16.6 %copy-start.4 = (f32[416,128]{1,0:T(8,128)}, f32[416,128]{1,0:T(8,128)S(1)}, u32[]{:S(2)}) copy-start(f32[416,128]{1,0:T(8,128)S(1)} %get-tuple-element.59.refs_7_) | copy-start | bytes 638980
  112.1 7.8 %collective-permute-start.11 = (f32[416,128]{1,0:T(8,128)S(1)}, f32[416,128]{1,0:T(8,128)S(1)}, u32[]{:S(2)}, u32[]{:S(2)}) collective-permute-start(f32[416,128]{1,0:T(8,128)S(1)} %get-tuple-element.52), channel_id=1, source_target_pairs={{0,4},{1,5},{2,6},{3,7},{4,0},{5,1},{6,2},{7,3},{8,12},{9,13},{10,... | collective-permute-start | bytes 638984 | tf_op jit(solution)/shard_map/ppermute | solution.py:392
  113.6 13.9 %collective-permute-start.12 = (f32[416,128]{1,0:T(8,128)S(1)}, f32[416,128]{1,0:T(8,128)S(1)}, u32[]{:S(2)}, u32[]{:S(2)}) collective-permute-start(f32[416,128]{1,0:T(8,128)S(1)} %get-tuple-element.53), channel_id=1, source_target_pairs={{0,5},{1,4},{2,7},{3,6},{4,1},{5,0},{6,3},{7,2},{8,13},{9,12},{10,... | collective-permute-start | bytes 638984 | tf_op jit(solution)/shard_map/ppermute | solution.py:392
  118.1 11.1 %collective-permute-start.13 = (f32[416,128]{1,0:T(8,128)S(1)}, f32[416,128]{1,0:T(8,128)S(1)}, u32[]{:S(2)}, u32[]{:S(2)}) collective-permute-start(f32[416,128]{1,0:T(8,128)S(1)} %get-tuple-element.54), channel_id=1, source_target_pairs={{0,2},{1,3},{2,0},{3,1},{4,6},{5,7},{6,4},{7,5},{8,10},{9,11},{10,... | collective-permute-start | bytes 638984 | tf_op jit(solution)/shard_map/ppermute | solution.py:392
  118.7 15.6 %collective-permute-start.14 = (f32[416,128]{1,0:T(8,128)S(1)}, f32[416,128]{1,0:T(8,128)S(1)}, u32[]{:S(2)}, u32[]{:S(2)}) collective-permute-start(f32[416,128]{1,0:T(8,128)S(1)} %get-tuple-element.55), channel_id=1, source_target_pairs={{0,3},{1,2},{2,1},{3,0},{4,7},{5,6},{6,5},{7,4},{8,11},{9,10},{10,... | collective-permute-start | bytes 638984 | tf_op jit(solution)/shard_map/ppermute | solution.py:392
  118.7 15.6 %collective-permute-start.15 = (f32[416,128]{1,0:T(8,128)S(1)}, f32[416,128]{1,0:T(8,128)S(1)}, u32[]{:S(2)}, u32[]{:S(2)}) collective-permute-start(f32[416,128]{1,0:T(8,128)S(1)} %get-tuple-element.56), channel_id=1, source_target_pairs={{0,6},{1,7},{2,4},{3,5},{4,2},{5,3},{6,0},{7,1},{8,14},{9,15},{10,... | collective-permute-start | bytes 638984 | tf_op jit(solution)/shard_map/ppermute | solution.py:392
  119.9 15.7 %copy-start.14 = (f32[416,128]{1,0:T(8,128)}, f32[416,128]{1,0:T(8,128)S(1)}, u32[]{:S(2)}) copy-start(f32[416,128]{1,0:T(8,128)S(1)} %collective-permute-done.11.refs_0_) | copy-start | bytes 638980
  119.9 15.7 %collective-permute-start.16 = (f32[416,128]{1,0:T(8,128)S(1)}, f32[416,128]{1,0:T(8,128)S(1)}, u32[]{:S(2)}, u32[]{:S(2)}) collective-permute-start(f32[416,128]{1,0:T(8,128)S(1)} %get-tuple-element.57), channel_id=1, source_target_pairs={{0,7},{1,6},{2,5},{3,4},{4,3},{5,2},{6,1},{7,0},{8,15},{9,14},{10,... | collective-permute-start | bytes 638984 | tf_op jit(solution)/shard_map/ppermute | solution.py:392
  127.5 8.0 %copy-start.15 = (f32[416,128]{1,0:T(8,128)}, f32[416,128]{1,0:T(8,128)S(1)}, u32[]{:S(2)}) copy-start(f32[416,128]{1,0:T(8,128)S(1)} %collective-permute-done.12.refs_1_) | copy-start | bytes 638980
  127.5 8.0 %collective-permute-start.17 = (f32[416,128]{1,0:T(8,128)S(1)}, f32[416,128]{1,0:T(8,128)S(1)}, u32[]{:S(2)}, u32[]{:S(2)}) collective-permute-start(f32[416,128]{1,0:T(8,128)S(1)} %get-tuple-element.58), channel_id=1, source_target_pairs={{0,1},{1,0},{2,3},{3,2},{4,5},{5,4},{6,7},{7,6},{8,9},{9,8},{10,11... | collective-permute-start | bytes 638984 | tf_op jit(solution)/shard_map/ppermute | solution.py:392
  128.6 0.6 copy-start.7
  129.2 6.3 %copy-start.16 = (f32[416,128]{1,0:T(8,128)}, f32[416,128]{1,0:T(8,128)S(1)}, u32[]{:S(2)}) copy-start(f32[416,128]{1,0:T(8,128)S(1)} %collective-permute-done.13.refs_2_) | copy-start | bytes 638980
  134.3 1.2 copy-start.17
  134.3 1.2 copy-start.18
  135.5 0.7 copy-start.19
  135.5 0.8 copy-start.20

commit v6 on v5

--- a/solution.py
+++ b/solution.py
@@ -130,7 +130,7 @@
     for z, out in ((0, z_first), (depth_z - 1, z_last)):
         pairs += [(vel_far.at[:, :, z, :], out.at[0:3]), (scal_far.at[:, z, :], out.at[3])]
     copies = [pltpu.make_async_copy(a, b, sems.at[i]) for i, (a, b) in enumerate(pairs)]
-    for copy in copies[5:] + copies[:5]:
+    for copy in copies:
         copy.start()
     for copy in copies[:5]:
         copy.wait()
@@ -847,7 +847,7 @@
             pltpu.SemaphoreType.DMA((8,)),
         ],
         name="last",
-        room=54,
+        room=51,
         far_in=(0,),
         far_out=(0, 1),
     )

time: 144 us -> 142 us (0.986)
  Pallas kernels: 47.4 us -> 44.6 us
    pallas_call x7, Pallas kernels: 47.4 us -> 44.6 us  [call(): pl.pallas_call(body, out_shape=shapes, in_specs=[hbm if i in far_in else...]
    unnamed x42 -> x30, local copies, waits for them, and re-layouts: 4.67 us -> 3.94 us
  transfers between devices with their start and end apart: 19 -> 19, of which waited for: 9 -> 10; matrix products, arithmetic and copies ran while one was open for 1% -> 1% of each run, Pallas kernels for 1% -> 1%
where the time goes in v6:
time: 142 us; the launch traced here: 141 us
  Pallas kernels  44.6 us (31%)
  starting transfers between devices  33.1 us (23%)
  waiting for transfers between devices  29.6 us (21%)
  blocking collectives  27.2 us (19%)
  local copies, waits for them, and re-layouts  5.6 us (4%)
    pallas_call x7, Pallas kernels, call(): pl.pallas_call(body, out_shape=shapes, in_specs=[hbm if i in far_in else...  44.6 us
    ppermute x14, waiting for transfers between devices, exchanged(): lax.ppermute(part, 'grp', [(i, i ^ d) for i in range(count)])  23.4 us
    ppermute x14, starting transfers between devices, exchanged(): lax.ppermute(part, 'grp', [(i, i ^ d) for i in range(count)])  21.5 us
    all_to_all x1, blocking collectives, per_device(): lax.all_to_all(send, ('wide', 'grp'), split_axis=0, concat_axis=0, tiled=...  17.1 us
    all_to_all x1, blocking collectives, per_device(): lax.all_to_all(reach, 'wide', split_axis=0, concat_axis=0, tiled=True)  10.1 us
    ppermute x4, starting transfers between devices, passed_along(): lax.ppermute(value, axis, [(i, (i + steps) % count) for i in range(count)])  7.97 us
    all_to_all x1, waiting for transfers between devices, per_device(): lax.all_to_all(small, 'wide', split_axis=0, concat_axis=0, tiled=True)  6.2 us
    unnamed x30, local copies, waits for them, and re-layouts  3.94 us
  transfers between devices with their start and end apart: 19, of which 10 were waited for; matrix products, arithmetic and copies ran while one was open for 1% of the time, Pallas kernels for 1%

profile of v6, /device:TPU:1, one launch (start us, length us, event | category | flops | bytes accessed | tf_op | source)
XLA Modules:
  0.0 141.1 jit_solution(4144945511733608751)
XLA Ops:
  0.6 0.0 copy-start.2
  0.6 0.0 copy-start.3
  0.7 2.7 %pack.1 = (f32[128,1,256]{2,1,0:T(1,128)}, s32[1,1024]{1,0:T(1,128)}, f32[4,16,512]{2,1,0:T(8,128)}, f32[4,16,512]{2,1,0:T(8,128)}, f32[4,48,512]{2,1,0:T(8,128)}, /*index=5*/f32[4,48,512]{2,1,0:T(8,128)}) custom-call(s32[1,1024]{1,0:T(1,128)} %bitcast.8, s32[1,1024]{1,0:T(1,128)} %bitcast.10, s32[1,1024]{1,0:T(1,128)} %bitcast.11, f32[4,1024]{1,0:T(4,128)} %refs_3_.1, ...), custom_call_target="tpu_custom_call" | custom-call | bytes 7507968 | tf_op jit(solution)/shard_map/pack/pallas_call | solution.py:37
  3.4 3.0 %collective-permute-start.2 = (f32[4,48,512]{2,1,0:T(8,128)}, f32[4,48,512]{2,1,0:T(8,128)S(1)}, u32[]{:S(2)}, u32[]{:S(2)}) collective-permute-start(f32[4,48,512]{2,1,0:T(8,128)} %get-tuple-element.35), channel_id=1, source_target_pairs={{0,1},{1,2},{2,3},{3,4},{4,5},{5,6},{6,7},{7,0},{8,9},{9,10},{10,1... | collective-permute-start | bytes 1179656 | tf_op jit(solution)/shard_map/ppermute | solution.py:60
  6.4 0.0 collective-permute-start.3
  6.4 1.3 collective-permute-start
  7.7 3.6 %collective-permute-start.1 = (f32[4,16,512]{2,1,0:T(8,128)}, f32[4,16,512]{2,1,0:T(8,128)S(1)}, u32[]{:S(2)}, u32[]{:S(2)}) collective-permute-start(f32[4,16,512]{2,1,0:T(8,128)} %get-tuple-element.34), channel_id=1, source_target_pairs={{0,120},{8,0},{16,8},{24,16},{32,24},{40,32},{48,40},{56,48},{64,5... | collective-permute-start | bytes 393224 | tf_op jit(solution)/shard_map/ppermute | solution.py:60
  11.4 17.1 %all_to_all.15.refs_6_ = f32[128,1,256]{2,1,0:T(1,128)S(1)} all-to-all(f32[128,1,256]{2,1,0:T(1,128)} %get-tuple-element.37), channel_id=1, replica_groups=mesh['wide'=16,'grp'=8] {'wide','grp'}, dimensions={0} | all-to-all | bytes 262144 | tf_op jit(solution)/shard_map/all_to_all | solution.py:765
  28.4 0.0 collective-permute-done.refs_2_
  28.4 0.0 collective-permute-done.1.refs_3_
  28.4 0.0 collective-permute-done.2.refs_4_
  28.5 0.0 collective-permute-done.3.refs_5_
  28.5 0.0 copy-done.2
  28.5 0.0 copy-done.3
  28.5 31.7 %first.1 = (f32[12288,128]{1,0:T(8,128)}, f32[440,128]{1,0:T(8,128)S(1)}, f32[440,128]{1,0:T(8,128)S(1)}, f32[440,128]{1,0:T(8,128)S(1)}, f32[440,128]{1,0:T(8,1...) custom-call(f32[3,48,16,512]{3,2,1,0:T(8,128)} %refs_0_.1, ...), custom_call_target="tpu_custom_call" | custom-call | bytes 120000000 | tf_op jit(solution)/shard_map/first/pallas_call | solution.py:37
  60.2 1.3 collective-permute-start.4
  61.5 2.8 %collective-permute-start.5 = (f32[440,128]{1,0:T(8,128)S(1)}, f32[440,128]{1,0:T(8,128)S(1)}, u32[]{:S(2)}, u32[]{:S(2)}) collective-permute-start(f32[440,128]{1,0:T(8,128)S(1)} %get-tuple-element.41), channel_id=1, source_target_pairs={{0,5},{1,4},{2,7},{3,6},{4,1},{5,0},{6,3},{7,2},{8,13},{9,12},{10,... | collective-permute-start | bytes 675848 | tf_op jit(solution)/shard_map/ppermute | solution.py:392
  64.3 0.0 collective-permute-start.6
  64.4 0.9 collective-permute-start.7
  65.3 1.0 collective-permute-start.8
  66.3 1.6 %collective-permute-done.4.refs_0_ = f32[440,128]{1,0:T(8,128)S(1)} collective-permute-done((f32[440,128]{1,0:T(8,128)S(1)}, f32[440,128]{1,0:T(8,128)S(1)}, u32[]{:S(2)}, u32[]{:S(2)}) %collective-permute-start.4) | collective-permute-done | bytes 225312 | tf_op jit(solution)/shard_map/ppermute | solution.py:392
  67.9 3.7 %collective-permute-start.9 = (f32[440,128]{1,0:T(8,128)S(1)}, f32[440,128]{1,0:T(8,128)S(1)}, u32[]{:S(2)}, u32[]{:S(2)}) collective-permute-start(f32[440,128]{1,0:T(8,128)S(1)} %get-tuple-element.45), channel_id=1, source_target_pairs={{0,7},{1,6},{2,5},{3,4},{4,3},{5,2},{6,1},{7,0},{8,15},{9,14},{10,... | collective-permute-start | bytes 675848 | tf_op jit(solution)/shard_map/ppermute | solution.py:392
  71.5 3.8 %collective-permute-done.5.refs_1_ = f32[440,128]{1,0:T(8,128)S(1)} collective-permute-done((f32[440,128]{1,0:T(8,128)S(1)}, f32[440,128]{1,0:T(8,128)S(1)}, u32[]{:S(2)}, u32[]{:S(2)}) %collective-permute-start.5) | collective-permute-done | bytes 225312 | tf_op jit(solution)/shard_map/ppermute | solution.py:392
  75.3 0.0 collective-permute-start.10
  75.3 1.0 dynamic-slice_bitcast_fusion.refs_10_.table_ref
  76.3 0.5 collective-permute-done.6.refs_2_
  76.8 5.7 %collective-permute-done.7.refs_3_ = f32[440,128]{1,0:T(8,128)S(1)} collective-permute-done((f32[440,128]{1,0:T(8,128)S(1)}, f32[440,128]{1,0:T(8,128)S(1)}, u32[]{:S(2)}, u32[]{:S(2)}) %collective-permute-start.7) | collective-permute-done | bytes 225312 | tf_op jit(solution)/shard_map/ppermute | solution.py:392
  82.5 0.0 collective-permute-done.8.refs_4_
  82.5 1.2 collective-permute-done.9.refs_5_
  83.7 0.0 collective-permute-done.10.refs_6_
  83.7 0.7 copy-done.4
  84.4 0.0 copy-done.11
  84.4 0.0 copy-done.12
  84.4 0.9 copy-done.5
  85.3 1.6 %forward_z.1 = (f32[24,128,128]{2,1,0:T(8,128)S(1)}, f32[3,128,128]{2,1,0:T(8,128)S(1)}, f32[16,24,128]{2,1,0:T(8,128)S(1)}) custom-call(f32[440,128]{1,0:T(8,128)S(1)} %collective-permute-done.4.refs_0_, f32[440,128]{1,0:T(8,128)S(1)} %collective-permute-done.5.refs_1_, f32[440,128]{1,0:T(8,128)S(1)} %collective-permute-done.6.refs_2_, ...), custom_call_target="tpu_custom_call" | custom-call | bytes 4030464 | tf_op jit(solution)/shard_map/forward_z/pallas_call | solution.py:37
  87.0 0.0 copy-start.6
  87.0 0.7 copy-done.6
  87.6 0.7 copy-done.8
  88.3 3.7 %all-to-all-start.1 = ((f32[16,24,128]{2,1,0:T(8,128)}), f32[16,24,128]{2,1,0:T(8,128)S(1)}, u32[]{:S(2)}, u32[]{:S(2)}) async-start(f32[16,24,128]{2,1,0:T(8,128)} %copy-done.8), calls=%async_computation.1 | async-start | bytes 393216 | tf_op jit(solution)/shard_map/all_to_all | solution.py:811
  92.0 0.7 dynamic-slice_bitcast_fusion.1.table_ref
  92.7 6.2 %all-to-all-done.1.back_ref.recv_ref = f32[16,24,128]{2,1,0:T(8,128)S(1)} async-done(((f32[16,24,128]{2,1,0:T(8,128)}), f32[16,24,128]{2,1,0:T(8,128)S(1)}, u32[]{:S(2)}, u32[]{:S(2)}) %all-to-all-start.1) | async-done | bytes 196640 | tf_op jit(solution)/shard_map/all_to_all | solution.py:811
  98.9 0.1 ring.1
  99.0 10.1 %all_to_all.16.small_ref = f32[16,8,128]{2,1,0:T(8,128)S(1)} all-to-all(f32[16,8,128]{2,1,0:T(8,128)S(1)} %ring.1), channel_id=1, replica_groups=mesh['wide'=16,'grp'=8] {'wide'}, dimensions={0} | all-to-all | bytes 131072 | tf_op jit(solution)/shard_map/all_to_all | solution.py:815
  109.1 0.0 copy-done.9
  109.1 0.9 copy-done.7
  110.0 1.7 %backward_z.1 = (f32[416,128]{1,0:T(8,128)S(1)}, f32[416,128]{1,0:T(8,128)S(1)}, f32[416,128]{1,0:T(8,128)S(1)}, f32[416,128]{1,0:T(8,128)S(1)}, f32[416,128]{1,...) custom-call(f32[24,128,128]{2,1,0:T(8,128)S(1)} %get-tuple-element.50.coef_ref, ...), custom_call_target="tpu_custom_call" | custom-call | bytes 3801088 | tf_op jit(solution)/shard_map/backward_z/pallas_call | solution.py:37
  111.7 1.5 %collective-permute-start.11 = (f32[416,128]{1,0:T(8,128)S(1)}, f32[416,128]{1,0:T(8,128)S(1)}, u32[]{:S(2)}, u32[]{:S(2)}) collective-permute-start(f32[416,128]{1,0:T(8,128)S(1)} %get-tuple-element.52), channel_id=1, source_target_pairs={{0,4},{1,5},{2,6},{3,7},{4,0},{5,1},{6,2},{7,3},{8,12},{9,13},{10,... | collective-permute-start | bytes 638984 | tf_op jit(solution)/shard_map/ppermute | solution.py:392
  113.3 4.5 %collective-permute-start.12 = (f32[416,128]{1,0:T(8,128)S(1)}, f32[416,128]{1,0:T(8,128)S(1)}, u32[]{:S(2)}, u32[]{:S(2)}) collective-permute-start(f32[416,128]{1,0:T(8,128)S(1)} %get-tuple-element.53), channel_id=1, source_target_pairs={{0,5},{1,4},{2,7},{3,6},{4,1},{5,0},{6,3},{7,2},{8,13},{9,12},{10,... | collective-permute-start | bytes 638984 | tf_op jit(solution)/shard_map/ppermute | solution.py:392
  117.8 0.6 collective-permute-start.13
  118.3 0.0 collective-permute-start.14
  118.3 1.2 collective-permute-start.15
  119.5 0.0 collective-permute-done.11.refs_0_
  119.5 4.0 %collective-permute-start.16 = (f32[416,128]{1,0:T(8,128)S(1)}, f32[416,128]{1,0:T(8,128)S(1)}, u32[]{:S(2)}, u32[]{:S(2)}) collective-permute-start(f32[416,128]{1,0:T(8,128)S(1)} %get-tuple-element.57), channel_id=1, source_target_pairs={{0,7},{1,6},{2,5},{3,4},{4,3},{5,2},{6,1},{7,0},{8,15},{9,14},{10,... | collective-permute-start | bytes 638984 | tf_op jit(solution)/shard_map/ppermute | solution.py:392
  123.5 3.7 %collective-permute-done.12.refs_1_ = f32[416,128]{1,0:T(8,128)S(1)} collective-permute-done((f32[416,128]{1,0:T(8,128)S(1)}, f32[416,128]{1,0:T(8,128)S(1)}, u32[]{:S(2)}, u32[]{:S(2)}) %collective-permute-start.12) | collective-permute-done | bytes 213024 | tf_op jit(solution)/shard_map/ppermute | solution.py:392
  127.2 0.0 collective-permute-start.17
  127.2 0.0 copy-done.13
  127.2 1.0 unpack.1
  128.2 0.6 collective-permute-done.13.refs_2_
  128.8 5.2 %collective-permute-done.14.refs_3_ = f32[416,128]{1,0:T(8,128)S(1)} collective-permute-done((f32[416,128]{1,0:T(8,128)S(1)}, f32[416,128]{1,0:T(8,128)S(1)}, u32[]{:S(2)}, u32[]{:S(2)}) %collective-permute-start.14) | collective-permute-done | bytes 213024 | tf_op jit(solution)/shard_map/ppermute | solution.py:392
  134.0 0.0 collective-permute-done.15.refs_4_
  134.0 1.2 collective-permute-done.16.refs_5_
  135.2 0.0 collective-permute-done.17.refs_6_
  135.2 0.0 copy-done.1
  135.2 5.8 %last.1 = (f32[3,48,16,512]{3,2,1,0:T(8,128)}, f32[48,16,512]{2,1,0:T(8,128)}) custom-call(f32[12288,128]{1,0:T(8,128)} %get-tuple-element.38.far_ref, f32[128,128]{1,0:T(8,128)S(1)} %get-tuple-element.49.mean_ref, bf16[512,512]{1,0:T(8,128)(2,1)S(1)} %copy-done.1, bf16[512,512]{1,0:T(8,128)(2,1)S(1)} %copy-done, ...), custom_call_target="tpu_custom_call" | custom-call | bytes 15400960 | tf_op jit(solution)/shard_map/last/pallas_call | solution.py:37
  (16 shorter events, 0.0 us)
Async XLA Ops:
  0.6 27.8 %copy-start.2 = (bf16[512,512]{1,0:T(8,128)(2,1)S(1)}, bf16[512,512]{1,0:T(8,128)(2,1)}, u32[]{:S(2)}) copy-start(bf16[512,512]{1,0:T(8,128)(2,1)} %constant.40.clone.refs_8_) | copy-start | bytes 1572868
  0.6 27.8 %copy-start.3 = (bf16[512,512]{1,0:T(8,128)(2,1)S(1)}, bf16[512,512]{1,0:T(8,128)(2,1)}, u32[]{:S(2)}) copy-start(bf16[512,512]{1,0:T(8,128)(2,1)} %constant.39.clone.refs_7_) | copy-start | bytes 1572868
  3.4 25.1 %collective-permute-start.2 = (f32[4,48,512]{2,1,0:T(8,128)}, f32[4,48,512]{2,1,0:T(8,128)S(1)}, u32[]{:S(2)}, u32[]{:S(2)}) collective-permute-start(f32[4,48,512]{2,1,0:T(8,128)} %get-tuple-element.35), channel_id=1, source_target_pairs={{0,1},{1,2},{2,3},{3,4},{4,5},{5,6},{6,7},{7,0},{8,9},{9,10},{10,1... | collective-permute-start | bytes 1179656 | tf_op jit(solution)/shard_map/ppermute | solution.py:60
  6.4 22.0 %collective-permute-start.3 = (f32[4,48,512]{2,1,0:T(8,128)}, f32[4,48,512]{2,1,0:T(8,128)S(1)}, u32[]{:S(2)}, u32[]{:S(2)}) collective-permute-start(f32[4,48,512]{2,1,0:T(8,128)} %get-tuple-element.36), channel_id=1, source_target_pairs={{0,7},{1,0},{2,1},{3,2},{4,3},{5,4},{6,5},{7,6},{8,15},{9,8},{10,9... | collective-permute-start | bytes 1179656 | tf_op jit(solution)/shard_map/ppermute | solution.py:60
  6.4 22.0 %collective-permute-start = (f32[4,16,512]{2,1,0:T(8,128)}, f32[4,16,512]{2,1,0:T(8,128)S(1)}, u32[]{:S(2)}, u32[]{:S(2)}) collective-permute-start(f32[4,16,512]{2,1,0:T(8,128)} %get-tuple-element.33), channel_id=1, source_target_pairs={{0,8},{8,16},{16,24},{24,32},{32,40},{40,48},{48,56},{56,64},{64,7... | collective-permute-start | bytes 393224 | tf_op jit(solution)/shard_map/ppermute | solution.py:60
  7.7 20.7 %collective-permute-start.1 = (f32[4,16,512]{2,1,0:T(8,128)}, f32[4,16,512]{2,1,0:T(8,128)S(1)}, u32[]{:S(2)}, u32[]{:S(2)}) collective-permute-start(f32[4,16,512]{2,1,0:T(8,128)} %get-tuple-element.34), channel_id=1, source_target_pairs={{0,120},{8,0},{16,8},{24,16},{32,24},{40,32},{48,40},{56,48},{64,5... | collective-permute-start | bytes 393224 | tf_op jit(solution)/shard_map/ppermute | solution.py:60
  28.4 56.0 %copy-start.11 = (bf16[128,128]{1,0:T(8,128)(2,1)S(1)}, bf16[128,128]{1,0:T(8,128)(2,1)}, u32[]{:S(2)}) copy-start(bf16[128,128]{1,0:T(8,128)(2,1)} %constant.44.clone.refs_9_) | copy-start | bytes 98308
  28.4 56.0 %copy-start.12 = (bf16[128,128]{1,0:T(8,128)(2,1)S(1)}, bf16[128,128]{1,0:T(8,128)(2,1)}, u32[]{:S(2)}) copy-start(bf16[128,128]{1,0:T(8,128)(2,1)} %constant.43.clone.refs_8_) | copy-start | bytes 98308
  60.2 7.7 %collective-permute-start.4 = (f32[440,128]{1,0:T(8,128)S(1)}, f32[440,128]{1,0:T(8,128)S(1)}, u32[]{:S(2)}, u32[]{:S(2)}) collective-permute-start(f32[440,128]{1,0:T(8,128)S(1)} %get-tuple-element.40), channel_id=1, source_target_pairs={{0,4},{1,5},{2,6},{3,7},{4,0},{5,1},{6,2},{7,3},{8,12},{9,13},{10,... | collective-permute-start | bytes 675848 | tf_op jit(solution)/shard_map/ppermute | solution.py:392
  61.5 13.8 %collective-permute-start.5 = (f32[440,128]{1,0:T(8,128)S(1)}, f32[440,128]{1,0:T(8,128)S(1)}, u32[]{:S(2)}, u32[]{:S(2)}) collective-permute-start(f32[440,128]{1,0:T(8,128)S(1)} %get-tuple-element.41), channel_id=1, source_target_pairs={{0,5},{1,4},{2,7},{3,6},{4,1},{5,0},{6,3},{7,2},{8,13},{9,12},{10,... | collective-permute-start | bytes 675848 | tf_op jit(solution)/shard_map/ppermute | solution.py:392
  64.3 12.5 %collective-permute-start.6 = (f32[440,128]{1,0:T(8,128)S(1)}, f32[440,128]{1,0:T(8,128)S(1)}, u32[]{:S(2)}, u32[]{:S(2)}) collective-permute-start(f32[440,128]{1,0:T(8,128)S(1)} %get-tuple-element.42), channel_id=1, source_target_pairs={{0,2},{1,3},{2,0},{3,1},{4,6},{5,7},{6,4},{7,5},{8,10},{9,11},{10,... | collective-permute-start | bytes 675848 | tf_op jit(solution)/shard_map/ppermute | solution.py:392
  64.4 18.1 %collective-permute-start.7 = (f32[440,128]{1,0:T(8,128)S(1)}, f32[440,128]{1,0:T(8,128)S(1)}, u32[]{:S(2)}, u32[]{:S(2)}) collective-permute-start(f32[440,128]{1,0:T(8,128)S(1)} %get-tuple-element.43), channel_id=1, source_target_pairs={{0,3},{1,2},{2,1},{3,0},{4,7},{5,6},{6,5},{7,4},{8,11},{9,10},{10,... | collective-permute-start | bytes 675848 | tf_op jit(solution)/shard_map/ppermute | solution.py:392
  65.3 17.2 %collective-permute-start.8 = (f32[440,128]{1,0:T(8,128)S(1)}, f32[440,128]{1,0:T(8,128)S(1)}, u32[]{:S(2)}, u32[]{:S(2)}) collective-permute-start(f32[440,128]{1,0:T(8,128)S(1)} %get-tuple-element.44), channel_id=1, source_target_pairs={{0,6},{1,7},{2,4},{3,5},{4,2},{5,3},{6,0},{7,1},{8,14},{9,15},{10,... | collective-permute-start | bytes 675848 | tf_op jit(solution)/shard_map/ppermute | solution.py:392
  67.9 15.8 %collective-permute-start.9 = (f32[440,128]{1,0:T(8,128)S(1)}, f32[440,128]{1,0:T(8,128)S(1)}, u32[]{:S(2)}, u32[]{:S(2)}) collective-permute-start(f32[440,128]{1,0:T(8,128)S(1)} %get-tuple-element.45), channel_id=1, source_target_pairs={{0,7},{1,6},{2,5},{3,4},{4,3},{5,2},{6,1},{7,0},{8,15},{9,14},{10,... | collective-permute-start | bytes 675848 | tf_op jit(solution)/shard_map/ppermute | solution.py:392
  75.3 8.4 %collective-permute-start.10 = (f32[440,128]{1,0:T(8,128)S(1)}, f32[440,128]{1,0:T(8,128)S(1)}, u32[]{:S(2)}, u32[]{:S(2)}) collective-permute-start(f32[440,128]{1,0:T(8,128)S(1)} %get-tuple-element.46), channel_id=1, source_target_pairs={{0,1},{1,0},{2,3},{3,2},{4,5},{5,4},{6,7},{7,6},{8,9},{9,8},{10,11... | collective-permute-start | bytes 675848 | tf_op jit(solution)/shard_map/ppermute | solution.py:392
  75.3 33.7 %copy-start.9 = (bf16[128,128]{1,0:T(8,128)(2,1)S(1)}, bf16[128,128]{1,0:T(8,128)(2,1)}, u32[]{:S(2)}) copy-start(bf16[128,128]{1,0:T(8,128)(2,1)} %constant.46.clone.low_ref) | copy-start | bytes 98308
  75.3 33.7 %copy-start.10 = (bf16[128,128]{1,0:T(8,128)(2,1)S(1)}, bf16[128,128]{1,0:T(8,128)(2,1)}, u32[]{:S(2)}) copy-start(bf16[128,128]{1,0:T(8,128)(2,1)} %constant.45.clone.high_ref) | copy-start | bytes 98308
  83.7 0.7 copy-start.4
  84.4 0.9 copy-start.5
  85.3 41.8 %copy-start.13 = (s32[1024]{0:T(1024)S(1)}, s32[1024]{0:T(1024)}, u32[]{:S(2)}) copy-start(s32[1024]{0:T(1024)} %param.19) | copy-start | bytes 12292
  85.3 41.8 %copy-start.14 = (s32[1,1024]{1,0:T(1,128)S(1)}, s32[1,1024]{1,0:T(1,128)}, u32[]{:S(2)}) copy-start(s32[1,1024]{1,0:T(1,128)} %get-tuple-element.39.rank_ref) | copy-start | bytes 12292
  87.0 0.7 copy-start.6
  87.6 0.7 copy-start.8
  88.3 46.9 %copy-start = (bf16[512,512]{1,0:T(8,128)(2,1)S(1)}, bf16[512,512]{1,0:T(8,128)(2,1)}, u32[]{:S(2)}) copy-start(bf16[512,512]{1,0:T(8,128)(2,1)} %constant.42.clone.low_ref) | copy-start | bytes 1572868
  88.3 46.9 %copy-start.1 = (bf16[512,512]{1,0:T(8,128)(2,1)S(1)}, bf16[512,512]{1,0:T(8,128)(2,1)}, u32[]{:S(2)}) copy-start(bf16[512,512]{1,0:T(8,128)(2,1)} %constant.41.clone.high_ref) | copy-start | bytes 1572868
  88.3 10.6 %all-to-all-start.1 = ((f32[16,24,128]{2,1,0:T(8,128)}), f32[16,24,128]{2,1,0:T(8,128)S(1)}, u32[]{:S(2)}, u32[]{:S(2)}) async-start(f32[16,24,128]{2,1,0:T(8,128)} %copy-done.8), calls=%async_computation.1 | async-start | bytes 393216 | tf_op jit(solution)/shard_map/all_to_all | solution.py:811
  109.1 0.9 copy-start.7
  111.7 7.8 %collective-permute-start.11 = (f32[416,128]{1,0:T(8,128)S(1)}, f32[416,128]{1,0:T(8,128)S(1)}, u32[]{:S(2)}, u32[]{:S(2)}) collective-permute-start(f32[416,128]{1,0:T(8,128)S(1)} %get-tuple-element.52), channel_id=1, source_target_pairs={{0,4},{1,5},{2,6},{3,7},{4,0},{5,1},{6,2},{7,3},{8,12},{9,13},{10,... | collective-permute-start | bytes 638984 | tf_op jit(solution)/shard_map/ppermute | solution.py:392
  113.3 13.9 %collective-permute-start.12 = (f32[416,128]{1,0:T(8,128)S(1)}, f32[416,128]{1,0:T(8,128)S(1)}, u32[]{:S(2)}, u32[]{:S(2)}) collective-permute-start(f32[416,128]{1,0:T(8,128)S(1)} %get-tuple-element.53), channel_id=1, source_target_pairs={{0,5},{1,4},{2,7},{3,6},{4,1},{5,0},{6,3},{7,2},{8,13},{9,12},{10,... | collective-permute-start | bytes 638984 | tf_op jit(solution)/shard_map/ppermute | solution.py:392
  117.8 11.0 %collective-permute-start.13 = (f32[416,128]{1,0:T(8,128)S(1)}, f32[416,128]{1,0:T(8,128)S(1)}, u32[]{:S(2)}, u32[]{:S(2)}) collective-permute-start(f32[416,128]{1,0:T(8,128)S(1)} %get-tuple-element.54), channel_id=1, source_target_pairs={{0,2},{1,3},{2,0},{3,1},{4,6},{5,7},{6,4},{7,5},{8,10},{9,11},{10,... | collective-permute-start | bytes 638984 | tf_op jit(solution)/shard_map/ppermute | solution.py:392
  118.3 15.6 %collective-permute-start.14 = (f32[416,128]{1,0:T(8,128)S(1)}, f32[416,128]{1,0:T(8,128)S(1)}, u32[]{:S(2)}, u32[]{:S(2)}) collective-permute-start(f32[416,128]{1,0:T(8,128)S(1)} %get-tuple-element.55), channel_id=1, source_target_pairs={{0,3},{1,2},{2,1},{3,0},{4,7},{5,6},{6,5},{7,4},{8,11},{9,10},{10,... | collective-permute-start | bytes 638984 | tf_op jit(solution)/shard_map/ppermute | solution.py:392
  118.3 15.6 %collective-permute-start.15 = (f32[416,128]{1,0:T(8,128)S(1)}, f32[416,128]{1,0:T(8,128)S(1)}, u32[]{:S(2)}, u32[]{:S(2)}) collective-permute-start(f32[416,128]{1,0:T(8,128)S(1)} %get-tuple-element.56), channel_id=1, source_target_pairs={{0,6},{1,7},{2,4},{3,5},{4,2},{5,3},{6,0},{7,1},{8,14},{9,15},{10,... | collective-permute-start | bytes 638984 | tf_op jit(solution)/shard_map/ppermute | solution.py:392
  119.5 15.7 %collective-permute-start.16 = (f32[416,128]{1,0:T(8,128)S(1)}, f32[416,128]{1,0:T(8,128)S(1)}, u32[]{:S(2)}, u32[]{:S(2)}) collective-permute-start(f32[416,128]{1,0:T(8,128)S(1)} %get-tuple-element.57), channel_id=1, source_target_pairs={{0,7},{1,6},{2,5},{3,4},{4,3},{5,2},{6,1},{7,0},{8,15},{9,14},{10,... | collective-permute-start | bytes 638984 | tf_op jit(solution)/shard_map/ppermute | solution.py:392
  127.2 8.0 %collective-permute-start.17 = (f32[416,128]{1,0:T(8,128)S(1)}, f32[416,128]{1,0:T(8,128)S(1)}, u32[]{:S(2)}, u32[]{:S(2)}) collective-permute-start(f32[416,128]{1,0:T(8,128)S(1)} %get-tuple-element.58), channel_id=1, source_target_pairs={{0,1},{1,0},{2,3},{3,2},{4,5},{5,4},{6,7},{7,6},{8,9},{9,8},{10,11... | collective-permute-start | bytes 638984 | tf_op jit(solution)/shard_map/ppermute | solution.py:392
